TPU v7x, 32 devices: a whole 2x2x4 slice. The times are simulated.
32 devices in a mesh: groups: 2 (over x), vocab: 16 (over z, y, core).
Axes of the slice: x: 2, y: 2, z: 4, core: 2. Of those that a mesh axis runs over, the one named last changes fastest.
Arguments:
- backbone_feature_matrix: bfloat16 [256, 5120], P(('groups', 'vocab')), parts along dimension 0, may hold values from -100 to 100, as said below
- closing_rmsnorm_multiplier: float32 [10240], P('groups'), parts along dimension 0, may hold values from 0.5 to 1.5
- output_vocab_matrix: bfloat16 [10240, 20480], P('groups', 'vocab'), parts along dimension 0, may hold values from -100 to 100, as said below
- softness_divisor: float32 [2], P('groups'), parts along dimension 0, may hold values from 0.8 to 1.6
- correct_label_ids: int32 [256], P(('groups', 'vocab')), parts along dimension 0, may hold values from 0 to 20479
- included_place_flags: int32 [256], P(('groups', 'vocab')), parts along dimension 0, may hold values from 0 to 1, as said below
Outputs:
- grad_hidden: bfloat16 [256, 5120], P(('groups', 'vocab')), parts along dimension 0
- grad_gain: float32 [10240], P('groups'), parts along dimension 0
- grad_temp: float32 [2], P('groups'), parts along dimension 0
- loss_mean: float32 [2], P('groups'), parts along dimension 0
There are 2 independent parts, one for each index of `groups`. A program takes and returns all parts, laid end to end along the dimension named above; each array names one. Nothing has to cross between parts.
Inputs may be any that keep to these rules, and one draw needn't show every extreme that they name: `backbone_feature_matrix`: activations of one member. `output_vocab_matrix`: head weights of one member. `included_place_flags`: in the member with index 1 every entry is 0.
All inputs are finite; a program needn't handle non-finite values.
Results may differ from a plain program's by a relative error of at most 0.0052.
Values may be sent and summed in bfloat16 or wider, within the bound.
No kernel may reach another device: no remote copies, remote signals or barrier semaphores. Data moves between devices by JAX's collectives and lax.ppermute only.
A program may use at most 128 MiB of HBM per device.

v0:
```python
import jax
import jax.numpy as jnp
from jax import lax
from jax.sharding import PartitionSpec as P

epsilon = 1e-06


def on_device(
    backbone_feature_matrix,
    closing_rmsnorm_multiplier,
    output_vocab_matrix,
    softness_divisor,
    correct_label_ids,
    included_place_flags,
):
    all_rows, all_targets, all_masks = (
        lax.all_gather(backbone_feature_matrix, "vocab", axis=0, tiled=True),
        lax.all_gather(correct_label_ids, "vocab", axis=0, tiled=True),
        lax.all_gather(included_place_flags, "vocab", axis=0, tiled=True),
    )
    raw_rows = all_rows.astype(jnp.float32)
    inv_rms = lax.rsqrt(jnp.mean(raw_rows * raw_rows, axis=1, keepdims=True) + epsilon)
    unit_rows = raw_rows * inv_rms
    normed = (unit_rows * closing_rmsnorm_multiplier[None, :]).astype(jnp.bfloat16)
    logits = jnp.dot(normed, output_vocab_matrix, preferred_element_type=jnp.float32)
    divisor_tally = softness_divisor[0]
    scaled = logits / divisor_tally
    slab_width = output_vocab_matrix.shape[1]
    offset = lax.axis_index("vocab") * slab_width
    owned = lax.broadcasted_iota(jnp.int32, scaled.shape, 1) + offset == all_targets[:, None]
    owned_f = owned.astype(jnp.float32)
    local_target = jnp.sum(owned_f * scaled, axis=1)
    peak = lax.pmax(jnp.max(scaled, axis=1), "vocab")
    exp_terms = jnp.exp(scaled - peak[:, None])
    totals, moments, target_z = lax.psum(
        (jnp.sum(exp_terms, axis=1), jnp.sum(exp_terms * scaled, axis=1), local_target), "vocab"
    )
    mask_f = all_masks.astype(jnp.float32)
    counted = jnp.maximum(jnp.sum(mask_f), 1.0)
    loss_mean = jnp.sum(mask_f * (peak + jnp.log(totals) - target_z)) / counted
    grad_temp = -jnp.sum(mask_f * (moments / totals - target_z)) / (counted * divisor_tally)
    token_count = all_rows.shape[0]
    factor = mask_f * (token_count / counted) / divisor_tally
    logit_grad = (factor[:, None] * (exp_terms / totals[:, None] - owned_f)).astype(jnp.bfloat16)
    width_all = all_rows.shape[1]
    own_count = backbone_feature_matrix.shape[0]
    own_start = lax.axis_index("vocab") * own_count
    normed_grad = lax.psum_scatter(
        lax.dot_general(
            logit_grad,
            output_vocab_matrix,
            (((1,), (1,)), ((), ())),
            preferred_element_type=jnp.float32,
        ),
        "vocab",
        scatter_dimension=0,
        tiled=True,
    )
    own_units = lax.dynamic_slice_in_dim(unit_rows, own_start, own_count, 0)
    own_inv = lax.dynamic_slice_in_dim(inv_rms, own_start, own_count, 0)
    unit_scale_gradient = normed_grad * closing_rmsnorm_multiplier[None, :]
    inner_dot = jnp.sum(unit_scale_gradient * own_units, axis=1, keepdims=True)
    grad_hidden = (own_inv * (unit_scale_gradient - own_units * inner_dot / width_all)).astype(
        jnp.bfloat16
    )
    grad_gain = lax.psum(jnp.sum(normed_grad * own_units, axis=0), "vocab")
    return (grad_hidden, grad_gain, grad_temp[None], loss_mean[None])


def solution(mesh):
    in_specs = (
        P(("groups", "vocab"), None),
        P("groups"),
        P("groups", "vocab"),
        P("groups"),
        P(("groups", "vocab")),
        P(("groups", "vocab")),
    )
    out_specs = (P(("groups", "vocab"), None), P("groups"), P("groups"), P("groups"))
    return jax.shard_map(
        on_device, mesh=mesh, in_specs=in_specs, out_specs=out_specs, check_vma=False
    )
```

profile of v0, /device:TPU:0, one launch (start us, length us, event | category | flops | bytes accessed | tf_op | source)
XLA Modules:
  0.0 265.3 jit_solution(3143666784569813497)
XLA Ops:
  7.2 0.0 all-gather.2.cloned.1.call-start
  7.2 0.7 all-gather.2.cloned.1.call-update
  7.9 0.0 reduce-scatter.2.cloned.1.call-start
  8.6 1.2 dynamic-slice.4
  10.5 0.9 dynamic-update-slice
  11.4 0.8 dynamic-update-slice.1
  12.2 13.7 %all-reduce.2 = (s32[128]{0:T(128)S(1)}, s32[128]{0:T(128)S(1)}) all-reduce(s32[128]{0:T(128)S(1)} %dynamic-update-slice.1, s32[128]{0:T(128)S(1)} %dynamic-update-slice), channel_id=1, replica_groups=mesh['groups'=2,'vocab'=16] {'vocab'}, use_global_device_ids=true, to_apply=%add.1 | all-reduce | flops 256 | bytes 2048
  25.9 25.9 %all-gather.2.cloned.1.call-done = bf16[128,5120]{1,0:T(8,128)(2,1)} async-done(((bf16[8,5120]{1,0:T(8,128)(2,1)}), bf16[128,5120]{1,0:T(8,128)(2,1)}) %all-gather.2.cloned.1.call-update) | async-done | bytes 1310736 | tf_op jit(solution)/shard_map/all_gather | solution.py:18
  51.9 1.6 fusion
  53.5 7.2 %fusion.14 = (f32[128]{0:T(128)S(1)}, f32[128,1280]{1,0:T(8,128)S(1)}) fusion(f32[]{:T(128)} %bitcast.7, bf16[5120,1280]{1,0:T(8,128)(2,1)} %param.8, f32[5120]{0:T(1024)} %param.7, f32[128]{0:T(128)S(1)} %add_rsqrt_fusion, bf16[128,5120]{1,0:T(8,128)(2,1)} %all-gather.2.cloned.1.call-done), kind=kOutput, calls=%fused_computation.30 | convolution fusion | flops 1680670592 | bytes 15094788 | tf_op jit(solution)/shard_map/dot_general | solution.py:26
  60.7 31.5 %pmax.7 = f32[128]{0:T(128)S(1)} all-reduce(f32[128]{0:T(128)S(1)} %get-tuple-element.17), channel_id=1, replica_groups=mesh['groups'=2,'vocab'=16] {'vocab'}, use_global_device_ids=true, to_apply=%region_3.0 | all-reduce | flops 128 | bytes 1024 | tf_op jit(solution)/shard_map/pmax | solution.py:34
  92.2 0.3 multiply_reduce_fusion
  92.5 29.5 %all-reduce.3 = (f32[128]{0:T(128)S(1)}, f32[128]{0:T(128)S(1)}, f32[128]{0:T(128)S(1)}) all-reduce(f32[128]{0:T(128)S(1)} %get-tuple-element.7, f32[128]{0:T(128)S(1)} %get-tuple-element.8, f32[128]{0:T(128)S(1)} %get-tuple-element.6), channel_id=1, replica_groups=mesh['groups'=2,'vocab'=16] {'vocab'}, use_global_device_ids=true, to_apply=%region_5.0 | all-reduce | flops 384 | bytes 3072 | tf_op jit(solution)/shard_map/psum | solution.py:36
  122.0 0.6 multiply_reduce_fusion.3
  123.3 10.7 %fusion.7 = f32[128,5120]{1,0:T(8,128)} fusion(bf16[5120,1280]{1,0:T(8,128)(2,1)} %param.8, f32[128,1280]{1,0:T(8,128)S(1)} %get-tuple-element.18, s32[1280]{0:T(1024)S(1)} %iota_add_fusion, f32[128]{0:T(128)S(1)} %get-tuple-element.14, f32[128]{0:T(128)S(1)} %pmax.7, f32[128]{0:T(128)S(1)} %multiply_divide_fusion, s32[128]{0:T(128)S(1)} %get-tuple-element.12), kind=kOutput, calls=%fused_computation.15 | convolution fusion | flops 1678868480 | bytes 16391168 | tf_op jit(solution)/shard_map/dot_general | solution.py:50
  134.0 0.0 reduce-scatter.2.cloned.1.call-update
  134.0 0.0 copy-start.1
  134.1 0.1 dynamic-slice.3
  135.6 1.8 convert_multiply_fusion
  137.4 57.9 %reduce-scatter.2.cloned.1.call-done = f32[8,5120]{1,0:T(8,128)} async-done(((f32[128,5120]{1,0:T(8,128)}), f32[8,5120]{1,0:T(8,128)}) %reduce-scatter.2.cloned.1.call-update) | async-done | bytes 163856 | tf_op jit(solution)/shard_map/reduce_scatter | solution.py:49
  195.3 0.0 copy-done.1
  195.3 1.2 multiply_reduce_fusion.1
  196.5 58.0 %psum.29 = f32[5120]{0:T(1024)} all-reduce(f32[5120]{0:T(1024)S(1)} %get-tuple-element.4), channel_id=1, replica_groups=mesh['groups'=2,'vocab'=16] {'vocab'}, use_global_device_ids=true, to_apply=%region_9.0 | all-reduce | flops 5120 | bytes 40960 | tf_op jit(solution)/shard_map/psum | solution.py:67
  254.5 1.7 multiply_convert_fusion.2
  (7 shorter events, 0.0 us)
Async XLA Ops:
  7.2 44.7 %all-gather.2.cloned.1.call-start = ((), (), s32[]{:S(2)}) async-start(), calls=%async_computation.1 | async-start | bytes 1392640 | tf_op jit(solution)/shard_map/all_gather | solution.py:18
  7.9 187.4 %reduce-scatter.2.cloned.1.call-start = ((), (), s32[]{:S(2)}) async-start(), calls=%async_computation.2 | async-start | bytes 2785280 | tf_op jit(solution)/shard_map/reduce_scatter | solution.py:49
  134.0 1.6 copy-start
  134.0 61.2 %copy-start.1 = (f32[5120]{0:T(1024)S(1)}, f32[5120]{0:T(1024)}, u32[]{:S(2)}) copy-start(f32[5120]{0:T(1024)} %param.7) | copy-start | bytes 61444
Sparse Core Ops, SparseCore 0:
  10.3 41.5 all-gather.1
  134.2 61.0 reduce-scatter.1
where the time goes:
time: 266 us; the launch traced here: 265 us
  blocking collectives  133 us (50%)
  waiting for transfers between devices  84.5 us (32%)
  between operations  19.8 us (7%)
  matrix products  17.8 us (7%)
  other arithmetic  7.36 us (3%)
  local copies, waits for them, and re-layouts  3.03 us (1%)
    psum x1, blocking collectives, on_device(): grad_gain = lax.psum(jnp.sum(normed_grad * own_units, axis=0), 'vocab')  58 us
    reduce_scatter x1, waiting for transfers between devices, on_device(): lax.psum_scatter(lax.dot_general(logit_grad, output_vocab_matrix, (((1,),...  57.9 us
    pmax x1, blocking collectives, on_device(): peak = lax.pmax(jnp.max(scaled, axis=1), 'vocab')  31.5 us
    psum x1, blocking collectives, on_device(): lax.psum((jnp.sum(exp_terms, axis=1), jnp.sum(exp_terms * scaled, axis=1)...  29.5 us
    all_gather x1, waiting for transfers between devices, on_device(): lax.all_gather(backbone_feature_matrix, 'vocab', axis=0, tiled=True)  25.9 us
    unnamed x1, blocking collectives  13.7 us
    dot_general x1, matrix products, on_device(): lax.dot_general(logit_grad, output_vocab_matrix, (((1,), (1,)), ((), ()))...  10.7 us
    dot_general x1, matrix products, on_device(): jnp.dot(normed, output_vocab_matrix, preferred_element_type=jnp.float32)  7.15 us
  transfers between devices with their start and end apart: 2, of which 2 were waited for; matrix products, arithmetic and copies ran while one was open for 2% of the time, Pallas kernels for 0%

commit v1 on v0

v1 whole, which is shorter than its diff:
```python
import jax
import jax.numpy as jnp
from jax import lax
from jax.sharding import PartitionSpec as P

epsilon = 1e-06
f32 = jnp.float32
bf16 = jnp.bfloat16
DIGIT = 128


def cat(*parts):
    return jnp.concatenate(parts, 0)


def bits_of(count):
    return [1 << b for b in range(count.bit_length() - 1)]


class Links:
    def __init__(self, count):
        self.count = count

    def swap(self, value, m):
        return lax.ppermute(value, "vocab", [(i, i ^ m) for i in range(self.count)])

    def gather(self, own):
        swap = self.swap
        if self.count == 16:
            far, diagonal, near, side = swap(own, 8), swap(own, 12), swap(own, 4), swap(own, 2)
            column = cat(far, diagonal, near)
            across = swap(column, 2)
            twin = swap(cat(own, side, column), 1)
            twin_across = swap(across, 1)
            return cat(own, side, column, across, twin, twin_across)
        blocks = own
        for m in reversed(bits_of(self.count)):
            blocks = cat(blocks, swap(blocks, m))
        return blocks

    def codes(self):
        if self.count == 16:
            first = [0, 2, 8, 12, 4, 10, 14, 6]
            return first + [c ^ 1 for c in first]
        codes = [0]
        for m in reversed(bits_of(self.count)):
            codes = codes + [c ^ m for c in codes]
        return codes

    def scatter(self, blocks):
        swap = self.swap
        if self.count == 16:
            b = blocks.shape[0] // 16
            g = blocks[: 8 * b] + swap(blocks[8 * b :].astype(bf16), 1).astype(f32)
            g0, g2, g8, g12, g4, g10, g14, g6 = [g[k * b : (k + 1) * b] for k in range(8)]
            s12 = swap(g14.astype(bf16), 2).astype(f32)
            s84 = swap(cat(g10, g6).astype(bf16), 2).astype(f32)
            s0 = swap(g2.astype(bf16), 2).astype(f32)
            w8 = swap((g12 + s12).astype(bf16), 4).astype(f32)
            z8 = swap((g8 + s84[:b] + w8).astype(bf16), 8).astype(f32)
            z4 = swap((g4 + s84[b:]).astype(bf16), 4).astype(f32)
            return g0 + s0 + z4 + z8
        for m in bits_of(self.count):
            half = blocks.shape[0] // 2
            blocks = blocks[:half] + swap(blocks[half:].astype(bf16), m).astype(f32)
        return blocks

    def total(self, value):
        for m in bits_of(self.count):
            value = value + self.swap(value, m)
        return value


def merge(a, b):
    first = a[0] >= b[0]
    high, low = jnp.where(first, a, b), jnp.where(first, b, a)
    fade = jnp.exp(low[0] - high[0])
    return jnp.stack(
        [high[0], high[1] + low[1] * fade, high[2] + low[2] * fade, a[3] + b[3]]
    )


def on_device(
    backbone_feature_matrix,
    closing_rmsnorm_multiplier,
    output_vocab_matrix,
    softness_divisor,
    correct_label_ids,
    included_place_flags,
):
    count = lax.axis_size("vocab")
    links = Links(count)
    codes = links.codes()
    me = lax.axis_index("vocab")
    own_count, width = backbone_feature_matrix.shape
    token_count = own_count * count
    slab_width = output_vocab_matrix.shape[1]
    gain = closing_rmsnorm_multiplier[None, :]

    raw_rows = backbone_feature_matrix.astype(f32)
    inv_rms = lax.rsqrt(jnp.mean(raw_rows * raw_rows, axis=1, keepdims=True) + epsilon)
    own_units = raw_rows * inv_rms
    own_normed = (own_units * gain).astype(bf16)
    ids = correct_label_ids[:, None]
    lane = lax.broadcasted_iota(jnp.int32, (own_count, 128), 1)
    notes = jnp.where(
        lane == 0,
        ids % DIGIT,
        jnp.where(
            lane == 1,
            ids // DIGIT % DIGIT,
            jnp.where(
                lane == 2,
                ids // (DIGIT * DIGIT),
                jnp.where(lane == 3, included_place_flags[:, None], 0),
            ),
        ),
    ).astype(bf16)
    gathered = links.gather(jnp.concatenate([own_normed, notes], 1))
    normed = gathered[:, :width]
    noted = gathered[:, width:].astype(f32)
    targets = (
        noted[:, 0] + DIGIT * noted[:, 1] + DIGIT * DIGIT * noted[:, 2]
    ).astype(jnp.int32)
    mask_f = noted[:, 3]

    logits = jnp.dot(normed, output_vocab_matrix, preferred_element_type=f32)
    divisor_tally = softness_divisor[0]
    scaled = logits / divisor_tally
    owned = (
        lax.broadcasted_iota(jnp.int32, scaled.shape, 1) + me * slab_width
        == targets[:, None]
    )
    local_peak = jnp.max(scaled, axis=1)
    local_exp = jnp.exp(scaled - local_peak[:, None])
    local = jnp.stack(
        [
            local_peak,
            jnp.sum(local_exp, axis=1),
            jnp.sum(local_exp * scaled, axis=1),
            jnp.sum(jnp.where(owned, scaled, 0.0), axis=1),
            mask_f,
        ]
    )

    owners = me ^ jnp.array(codes, jnp.int32)
    place = lax.broadcasted_iota(jnp.int32, (count, count), 0) == owners[None, :]

    def to_shared(x):
        x = x.reshape(-1, 1, count, own_count)
        return jnp.sum(jnp.where(place[None, :, :, None], x, 0.0), 2).reshape(-1, token_count)

    def to_local(x):
        x = x.reshape(-1, count, 1, own_count)
        return jnp.sum(jnp.where(place[None, :, :, None], x, 0.0), 1).reshape(-1, token_count)

    shared = to_shared(local)
    shared_mask = shared[4]
    stats = shared[:4]
    if count == 16:
        near, far, diagonal = (links.swap(stats, m) for m in (4, 8, 12))
        stats = merge(merge(stats, near), merge(far, diagonal))
        stats = merge(stats, links.swap(stats, 2))
        stats = merge(stats, links.swap(stats, 1))
    else:
        for m in reversed(bits_of(count)):
            stats = merge(stats, links.swap(stats, m))
    peak, totals, moments, target_z = stats
    counted = jnp.maximum(jnp.sum(shared_mask), 1.0)
    loss_mean = jnp.sum(shared_mask * (peak + jnp.log(totals) - target_z)) / counted
    grad_temp = -jnp.sum(shared_mask * (moments / totals - target_z)) / (counted * divisor_tally)

    peak, totals = to_local(jnp.stack([peak, totals]))
    factor = mask_f * (token_count / counted) / divisor_tally
    exp_terms = jnp.exp(scaled - peak[:, None])
    logit_grad = (
        factor[:, None] * (exp_terms / totals[:, None] - owned.astype(f32))
    ).astype(bf16)
    slab_grad = lax.dot_general(
        logit_grad,
        output_vocab_matrix,
        (((1,), (1,)), ((), ())),
        preferred_element_type=f32,
    )
    grad_gain = links.total(
        jnp.sum(slab_grad * normed.astype(f32), axis=0) / closing_rmsnorm_multiplier
    )
    normed_grad = links.scatter(slab_grad)
    unit_grad = normed_grad * gain
    inner_dot = jnp.sum(unit_grad * own_units, axis=1, keepdims=True)
    grad_hidden = (inv_rms * (unit_grad - own_units * inner_dot / width)).astype(bf16)
    return (grad_hidden, grad_gain, grad_temp[None], loss_mean[None])


def solution(mesh):
    in_specs = (
        P(("groups", "vocab"), None),
        P("groups"),
        P("groups", "vocab"),
        P("groups"),
        P(("groups", "vocab")),
        P(("groups", "vocab")),
    )
    out_specs = (P(("groups", "vocab"), None), P("groups"), P("groups"), P("groups"))
    return jax.shard_map(
        on_device, mesh=mesh, in_specs=in_specs, out_specs=out_specs, check_vma=False
    )
```

time: 266 us -> 89.3 us (0.34)
  blocking collectives: 133 us -> 0 us
  waiting for transfers between devices: 84.5 us -> 26.7 us
  starting transfers between devices: 0.08 us -> 28.8 us
  between operations: 19.8 us -> 5.95 us
    psum x2 -> x0, blocking collectives: 87.5 us -> none  [the longest x1 58 us: on_device(): grad_gain = lax.psum(jnp.sum(normed_grad * own_units, axis=0), 'vocab')]
    reduce_scatter x1 -> x0, waiting for transfers between devices: 57.9 us -> none  [on_device(): lax.psum_scatter(lax.dot_general(logit_grad, output_vocab_matrix, (((1,),...]
    pmax x1 -> x0, blocking collectives: 31.5 us -> none  [on_device(): peak = lax.pmax(jnp.max(scaled, axis=1), 'vocab')]
    ppermute x0 -> x23, starting transfers between devices: none -> 28.8 us  [swap(): return lax.ppermute(value, 'vocab', [(i, i ^ m) for i in range(self.count)])]
    ppermute x0 -> x23, waiting for transfers between devices: none -> 26.7 us  [swap(): return lax.ppermute(value, 'vocab', [(i, i ^ m) for i in range(self.count)])]
    all_gather x1 -> x0, waiting for transfers between devices: 25.9 us -> none  [on_device(): lax.all_gather(backbone_feature_matrix, 'vocab', axis=0, tiled=True)]
    unnamed x1 -> x0, blocking collectives: 13.7 us -> none
    unnamed x9 -> x13, local copies, waits for them, and re-layouts: 2.95 us -> 0.15 us
  transfers between devices with their start and end apart: 2 -> 23, of which waited for: 2 -> 14; matrix products, arithmetic and copies ran while one was open for 2% -> 2% of each run, Pallas kernels for 0% -> 0%
where the time goes in v1:
time: 89.3 us; the launch traced here: 89 us
  starting transfers between devices  28.8 us (32%)
  waiting for transfers between devices  26.7 us (30%)
  matrix products  15.9 us (18%)
  other arithmetic  8.57 us (10%)
  between operations  5.95 us (7%)
  local copies, waits for them, and re-layouts  3.1 us (3%)
    ppermute x23, starting transfers between devices, swap(): return lax.ppermute(value, 'vocab', [(i, i ^ m) for i in range(self.count)])  28.8 us
    ppermute x23, waiting for transfers between devices, swap(): return lax.ppermute(value, 'vocab', [(i, i ^ m) for i in range(self.count)])  26.7 us
    dot_general x1, matrix products, on_device(): lax.dot_general(logit_grad, output_vocab_matrix, (((1,), (1,)), ((), ()))...  9.2 us
    dot_general x1, matrix products, on_device(): logits = jnp.dot(normed, output_vocab_matrix, preferred_element_type=f32)  6.69 us
  transfers between devices with their start and end apart: 23, of which 14 were waited for; matrix products, arithmetic and copies ran while one was open for 2% of the time, Pallas kernels for 0%

profile of v1, /device:TPU:0, one launch (start us, length us, event | category | flops | bytes accessed | tf_op | source)
XLA Modules:
  0.0 89.0 jit_solution(7974401703873449429)
XLA Ops:
  4.1 5.1 %collective-permute-start.2 = (bf16[8,5248]{1,0:T(8,128)(2,1)S(1)}, bf16[8,5248]{1,0:T(8,128)(2,1)S(1)}, u32[]{:S(2)}, u32[]{:S(2)}) collective-permute-start(bf16[8,5248]{1,0:T(8,128)(2,1)S(1)} %get-tuple-element.39), channel_id=1, source_target_pairs={{0,12},{1,13},{2,14},{3,15},{4,8},{5,9},{6,10},{7,11},{8,4},{9,5},... | collective-permute-start | bytes 251912 | tf_op jit(solution)/shard_map/ppermute | solution.py:25
  9.2 1.5 %collective-permute-start = (bf16[8,5248]{1,0:T(8,128)(2,1)S(1)}, bf16[8,5248]{1,0:T(8,128)(2,1)S(1)}, u32[]{:S(2)}, u32[]{:S(2)}) collective-permute-start(bf16[8,5248]{1,0:T(8,128)(2,1)S(1)} %get-tuple-element.39), channel_id=1, source_target_pairs={{0,2},{1,3},{2,0},{3,1},{4,6},{5,7},{6,4},{7,5},{8,10},{9,11},{10,... | collective-permute-start | bytes 251912 | tf_op jit(solution)/shard_map/ppermute | solution.py:25
  12.9 3.5 %collective-permute-done.1 = bf16[8,5248]{1,0:T(8,128)(2,1)S(1)} collective-permute-done((bf16[8,5248]{1,0:T(8,128)(2,1)S(1)}, bf16[8,5248]{1,0:T(8,128)(2,1)S(1)}, u32[]{:S(2)}, u32[]{:S(2)}) %collective-permute-start.1) | collective-permute-done | bytes 84000 | tf_op jit(solution)/shard_map/ppermute | solution.py:25
  16.7 1.2 %collective-permute-start.4 = (bf16[24,5248]{1,0:T(8,128)(2,1)S(1)}, bf16[24,5248]{1,0:T(8,128)(2,1)S(1)}, u32[]{:S(2)}, u32[]{:S(2)}) collective-permute-start(bf16[24,5248]{1,0:T(8,128)(2,1)S(1)} %pad_maximum_fusion), channel_id=1, source_target_pairs={{0,2},{1,3},{2,0},{3,1},{4,6},{5,7},{6,4},{7,5},{8,10},{9,11},{10,... | collective-permute-start | bytes 755720 | tf_op jit(solution)/shard_map/ppermute | solution.py:25
  18.1 5.6 %collective-permute-done.4 = bf16[24,5248]{1,0:T(8,128)(2,1)S(1)} collective-permute-done((bf16[24,5248]{1,0:T(8,128)(2,1)S(1)}, bf16[24,5248]{1,0:T(8,128)(2,1)S(1)}, u32[]{:S(2)}, u32[]{:S(2)}) %collective-permute-start.4) | collective-permute-done | bytes 251936 | tf_op jit(solution)/shard_map/ppermute | solution.py:25
  23.7 1.4 %collective-permute-done.6 = bf16[24,5248]{1,0:T(8,128)(2,1)S(1)} collective-permute-done((bf16[24,5248]{1,0:T(8,128)(2,1)S(1)}, bf16[24,5248]{1,0:T(8,128)(2,1)S(1)}, u32[]{:S(2)}, u32[]{:S(2)}) %collective-permute-start.6) | collective-permute-done | bytes 251936 | tf_op jit(solution)/shard_map/ppermute | solution.py:25
  25.6 6.7 %fusion.42 = (f32[128]{0:T(128)S(1)}, f32[128,1280]{1,0:T(8,128)S(1)}) fusion(f32[]{:T(128)} %bitcast.20, bf16[5120,1280]{1,0:T(8,128)(2,1)} %param.9, bf16[128,5248]{1,0:T(8,128)(2,1)S(1)} %constant_dynamic-update-slice_fusion.5), kind=kOutput, calls=%fused_computation.156 | convolution fusion | flops 1678049152 | bytes 15073796 | tf_op jit(solution)/shard_map/dot_general | solution.py:127
  33.4 2.1 %collective-permute-start.9 = (f32[4,128]{1,0:T(4,128)S(1)}, f32[4,128]{1,0:T(4,128)S(1)}, u32[]{:S(2)}, u32[]{:S(2)}) collective-permute-start(f32[4,128]{1,0:T(4,128)S(1)} %slice.215), channel_id=1, source_target_pairs={{0,12},{1,13},{2,14},{3,15},{4,8},{5,9},{6,10},{7,11},{8,4},{9,5},... | collective-permute-start | bytes 6152 | tf_op jit(solution)/shard_map/ppermute | solution.py:25
  35.6 2.3 %collective-permute-start.7 = (f32[4,128]{1,0:T(4,128)S(1)}, f32[4,128]{1,0:T(4,128)S(1)}, u32[]{:S(2)}, u32[]{:S(2)}) collective-permute-start(f32[4,128]{1,0:T(4,128)S(1)} %slice.215), channel_id=1, source_target_pairs={{0,4},{1,5},{2,6},{3,7},{4,0},{5,1},{6,2},{7,3},{8,12},{9,13},{10,... | collective-permute-start | bytes 6152 | tf_op jit(solution)/shard_map/ppermute | solution.py:25
  41.4 1.6 %collective-permute-start.10 = (f32[4,128]{1,0:T(4,128)S(1)}, f32[4,128]{1,0:T(4,128)S(1)}, u32[]{:S(2)}, u32[]{:S(2)}) collective-permute-start(f32[4,128]{1,0:T(4,128)S(1)} %pad_maximum_fusion.5), channel_id=1, source_target_pairs={{0,2},{1,3},{2,0},{3,1},{4,6},{5,7},{6,4},{7,5},{8,10},{9,11},{10,... | collective-permute-start | bytes 6152 | tf_op jit(solution)/shard_map/ppermute | solution.py:25
  43.0 2.1 %collective-permute-done.10 = f32[4,128]{1,0:T(4,128)S(1)} collective-permute-done((f32[4,128]{1,0:T(4,128)S(1)}, f32[4,128]{1,0:T(4,128)S(1)}, u32[]{:S(2)}, u32[]{:S(2)}) %collective-permute-start.10) | collective-permute-done | bytes 2080 | tf_op jit(solution)/shard_map/ppermute | solution.py:25
  49.2 9.2 %multiply_reduce_fusion = (f32[5120]{0:T(1024)S(1)}, f32[128,5120]{1,0:T(8,128)S(1)}) fusion(bf16[128,5248]{1,0:T(8,128)(2,1)S(1)} %constant_dynamic-update-slice_fusion.5, bf16[5120,1280]{1,0:T(8,128)(2,1)} %param.9, f32[128,1280]{1,0:T(8,128)S(1)} %get-tuple-element.74, f32[128]{0:T(128)S(1)} %div.90, f32[128]{0:T(128)S(1)} %sub.85, f32[128]{0:T(128)S(1)} %fusion.34, ...), kind=kOutput, calls=%fused_computation | convolution fusion | flops 1680829440 | bytes 17722368 | tf_op jit(solution)/shard_map/dot_general | solution.py:179
  58.7 1.9 %collective-permute-done.12 = bf16[64,5120]{1,0:T(8,128)(2,1)S(1)} collective-permute-done((bf16[64,5120]{1,0:T(8,128)(2,1)S(1)}, bf16[64,5120]{1,0:T(8,128)(2,1)S(1)}, u32[]{:S(2)}, u32[]{:S(2)}) %collective-permute-start.12) | collective-permute-done | bytes 655392 | tf_op jit(solution)/shard_map/ppermute | solution.py:25
  60.8 1.6 %collective-permute-start.16 = (bf16[8,5120]{1,0:T(8,128)(2,1)S(1)}, bf16[8,5120]{1,0:T(8,128)(2,1)S(1)}, u32[]{:S(2)}, u32[]{:S(2)}) collective-permute-start(bf16[8,5120]{1,0:T(8,128)(2,1)S(1)} %get-tuple-element.26), channel_id=1, source_target_pairs={{0,2},{1,3},{2,0},{3,1},{4,6},{5,7},{6,4},{7,5},{8,10},{9,11},{10,... | collective-permute-start | bytes 245768 | tf_op jit(solution)/shard_map/ppermute | solution.py:25
  63.0 2.9 %collective-permute-done.16 = bf16[8,5120]{1,0:T(8,128)(2,1)S(1)} collective-permute-done((bf16[8,5120]{1,0:T(8,128)(2,1)S(1)}, bf16[8,5120]{1,0:T(8,128)(2,1)S(1)}, u32[]{:S(2)}, u32[]{:S(2)}) %collective-permute-start.16) | collective-permute-done | bytes 81952 | tf_op jit(solution)/shard_map/ppermute | solution.py:25
  66.0 1.3 %collective-permute-start.17 = (bf16[8,5120]{1,0:T(8,128)(2,1)S(1)}, bf16[8,5120]{1,0:T(8,128)(2,1)S(1)}, u32[]{:S(2)}, u32[]{:S(2)}) collective-permute-start(bf16[8,5120]{1,0:T(8,128)(2,1)S(1)} %fusion.23), channel_id=1, source_target_pairs={{0,4},{1,5},{2,6},{3,7},{4,0},{5,1},{6,2},{7,3},{8,12},{9,13},{10,... | collective-permute-start | bytes 245768 | tf_op jit(solution)/shard_map/ppermute | solution.py:25
  67.3 2.1 %collective-permute-start.13 = (bf16[8,5120]{1,0:T(8,128)(2,1)S(1)}, bf16[8,5120]{1,0:T(8,128)(2,1)S(1)}, u32[]{:S(2)}, u32[]{:S(2)}) collective-permute-start(bf16[8,5120]{1,0:T(8,128)(2,1)S(1)} %get-tuple-element.25), channel_id=1, source_target_pairs={{0,2},{1,3},{2,0},{3,1},{4,6},{5,7},{6,4},{7,5},{8,10},{9,11},{10,... | collective-permute-start | bytes 245768 | tf_op jit(solution)/shard_map/ppermute | solution.py:25
  70.5 1.3 %collective-permute-start.15 = (bf16[8,5120]{1,0:T(8,128)(2,1)S(1)}, bf16[8,5120]{1,0:T(8,128)(2,1)S(1)}, u32[]{:S(2)}, u32[]{:S(2)}) collective-permute-start(bf16[8,5120]{1,0:T(8,128)(2,1)S(1)} %get-tuple-element.23), channel_id=1, source_target_pairs={{0,4},{1,5},{2,6},{3,7},{4,0},{5,1},{6,2},{7,3},{8,12},{9,13},{10,... | collective-permute-start | bytes 245768 | tf_op jit(solution)/shard_map/ppermute | solution.py:25
  72.8 2.1 %collective-permute-start.20 = (f32[5120]{0:T(1024)S(1)}, f32[5120]{0:T(1024)S(1)}, u32[]{:S(2)}, u32[]{:S(2)}) collective-permute-start(f32[5120]{0:T(1024)S(1)} %add.221), channel_id=1, source_target_pairs={{0,2},{1,3},{2,0},{3,1},{4,6},{5,7},{6,4},{7,5},{8,10},{9,11},{10,... | collective-permute-start | bytes 61448 | tf_op jit(solution)/shard_map/ppermute | solution.py:25
  74.9 1.8 %collective-permute-done.20 = f32[5120]{0:T(1024)S(1)} collective-permute-done((f32[5120]{0:T(1024)S(1)}, f32[5120]{0:T(1024)S(1)}, u32[]{:S(2)}, u32[]{:S(2)}) %collective-permute-start.20) | collective-permute-done | bytes 20512 | tf_op jit(solution)/shard_map/ppermute | solution.py:25
  76.6 1.8 %collective-permute-start.21 = (f32[5120]{0:T(1024)S(1)}, f32[5120]{0:T(1024)S(1)}, u32[]{:S(2)}, u32[]{:S(2)}) collective-permute-start(f32[5120]{0:T(1024)S(1)} %add.222), channel_id=1, source_target_pairs={{0,4},{1,5},{2,6},{3,7},{4,0},{5,1},{6,2},{7,3},{8,12},{9,13},{10,... | collective-permute-start | bytes 61448 | tf_op jit(solution)/shard_map/ppermute | solution.py:25
  78.4 2.0 %collective-permute-done.21 = f32[5120]{0:T(1024)S(1)} collective-permute-done((f32[5120]{0:T(1024)S(1)}, f32[5120]{0:T(1024)S(1)}, u32[]{:S(2)}, u32[]{:S(2)}) %collective-permute-start.21) | collective-permute-done | bytes 20512 | tf_op jit(solution)/shard_map/ppermute | solution.py:25
  80.4 2.0 %collective-permute-start.22 = (f32[5120]{0:T(1024)S(1)}, f32[5120]{0:T(1024)S(1)}, u32[]{:S(2)}, u32[]{:S(2)}) collective-permute-start(f32[5120]{0:T(1024)S(1)} %add.223), channel_id=1, source_target_pairs={{0,8},{1,9},{2,10},{3,11},{4,12},{5,13},{6,14},{7,15},{8,0},{9,1},... | collective-permute-start | bytes 61448 | tf_op jit(solution)/shard_map/ppermute | solution.py:25
  83.8 1.4 %collective-permute-done.22 = f32[5120]{0:T(1024)S(1)} collective-permute-done((f32[5120]{0:T(1024)S(1)}, f32[5120]{0:T(1024)S(1)}, u32[]{:S(2)}, u32[]{:S(2)}) %collective-permute-start.22) | collective-permute-done | bytes 20512 | tf_op jit(solution)/shard_map/ppermute | solution.py:25
  (125 shorter events, 18.6 us)
Async XLA Ops:
  4.1 8.8 %collective-permute-start.2 = (bf16[8,5248]{1,0:T(8,128)(2,1)S(1)}, bf16[8,5248]{1,0:T(8,128)(2,1)S(1)}, u32[]{:S(2)}, u32[]{:S(2)}) collective-permute-start(bf16[8,5248]{1,0:T(8,128)(2,1)S(1)} %get-tuple-element.39), channel_id=1, source_target_pairs={{0,12},{1,13},{2,14},{3,15},{4,8},{5,9},{6,10},{7,11},{8,4},{9,5},... | collective-permute-start | bytes 251912 | tf_op jit(solution)/shard_map/ppermute | solution.py:25
  9.2 7.1 %collective-permute-start.1 = (bf16[8,5248]{1,0:T(8,128)(2,1)S(1)}, bf16[8,5248]{1,0:T(8,128)(2,1)S(1)}, u32[]{:S(2)}, u32[]{:S(2)}) collective-permute-start(bf16[8,5248]{1,0:T(8,128)(2,1)S(1)} %get-tuple-element.39), channel_id=1, source_target_pairs={{0,8},{1,9},{2,10},{3,11},{4,12},{5,13},{6,14},{7,15},{8,0},{9,1},... | collective-permute-start | bytes 251912 | tf_op jit(solution)/shard_map/ppermute | solution.py:25
  9.2 8.6 %collective-permute-start = (bf16[8,5248]{1,0:T(8,128)(2,1)S(1)}, bf16[8,5248]{1,0:T(8,128)(2,1)S(1)}, u32[]{:S(2)}, u32[]{:S(2)}) collective-permute-start(bf16[8,5248]{1,0:T(8,128)(2,1)S(1)} %get-tuple-element.39), channel_id=1, source_target_pairs={{0,2},{1,3},{2,0},{3,1},{4,6},{5,7},{6,4},{7,5},{8,10},{9,11},{10,... | collective-permute-start | bytes 251912 | tf_op jit(solution)/shard_map/ppermute | solution.py:25
  10.8 5.9 %collective-permute-start.3 = (bf16[8,5248]{1,0:T(8,128)(2,1)S(1)}, bf16[8,5248]{1,0:T(8,128)(2,1)S(1)}, u32[]{:S(2)}, u32[]{:S(2)}) collective-permute-start(bf16[8,5248]{1,0:T(8,128)(2,1)S(1)} %get-tuple-element.39), channel_id=1, source_target_pairs={{0,4},{1,5},{2,6},{3,7},{4,0},{5,1},{6,2},{7,3},{8,12},{9,13},{10,... | collective-permute-start | bytes 251912 | tf_op jit(solution)/shard_map/ppermute | solution.py:25
  16.7 6.9 %collective-permute-start.4 = (bf16[24,5248]{1,0:T(8,128)(2,1)S(1)}, bf16[24,5248]{1,0:T(8,128)(2,1)S(1)}, u32[]{:S(2)}, u32[]{:S(2)}) collective-permute-start(bf16[24,5248]{1,0:T(8,128)(2,1)S(1)} %pad_maximum_fusion), channel_id=1, source_target_pairs={{0,2},{1,3},{2,0},{3,1},{4,6},{5,7},{6,4},{7,5},{8,10},{9,11},{10,... | collective-permute-start | bytes 755720 | tf_op jit(solution)/shard_map/ppermute | solution.py:25
  18.0 5.7 %collective-permute-start.5 = (bf16[40,5248]{1,0:T(8,128)(2,1)S(1)}, bf16[40,5248]{1,0:T(8,128)(2,1)S(1)}, u32[]{:S(2)}, u32[]{:S(2)}) collective-permute-start(bf16[40,5248]{1,0:T(8,128)(2,1)S(1)} %get-tuple-element.29), channel_id=1, source_target_pairs={{0,1},{1,0},{2,3},{3,2},{4,5},{5,4},{6,7},{7,6},{8,9},{9,8},{10,11... | collective-permute-start | bytes 1259528 | tf_op jit(solution)/shard_map/ppermute | solution.py:25
  23.6 1.5 %collective-permute-start.6 = (bf16[24,5248]{1,0:T(8,128)(2,1)S(1)}, bf16[24,5248]{1,0:T(8,128)(2,1)S(1)}, u32[]{:S(2)}, u32[]{:S(2)}) collective-permute-start(bf16[24,5248]{1,0:T(8,128)(2,1)S(1)} %collective-permute-done.4), channel_id=1, source_target_pairs={{0,1},{1,0},{2,3},{3,2},{4,5},{5,4},{6,7},{7,6},{8,9},{9,8},{10,11... | collective-permute-start | bytes 755720 | tf_op jit(solution)/shard_map/ppermute | solution.py:25
  33.4 5.4 %collective-permute-start.9 = (f32[4,128]{1,0:T(4,128)S(1)}, f32[4,128]{1,0:T(4,128)S(1)}, u32[]{:S(2)}, u32[]{:S(2)}) collective-permute-start(f32[4,128]{1,0:T(4,128)S(1)} %slice.215), channel_id=1, source_target_pairs={{0,12},{1,13},{2,14},{3,15},{4,8},{5,9},{6,10},{7,11},{8,4},{9,5},... | collective-permute-start | bytes 6152 | tf_op jit(solution)/shard_map/ppermute | solution.py:25
  35.5 4.5 %collective-permute-start.8 = (f32[4,128]{1,0:T(4,128)S(1)}, f32[4,128]{1,0:T(4,128)S(1)}, u32[]{:S(2)}, u32[]{:S(2)}) collective-permute-start(f32[4,128]{1,0:T(4,128)S(1)} %slice.215), channel_id=1, source_target_pairs={{0,8},{1,9},{2,10},{3,11},{4,12},{5,13},{6,14},{7,15},{8,0},{9,1},... | collective-permute-start | bytes 6152 | tf_op jit(solution)/shard_map/ppermute | solution.py:25
  35.6 4.5 %collective-permute-start.7 = (f32[4,128]{1,0:T(4,128)S(1)}, f32[4,128]{1,0:T(4,128)S(1)}, u32[]{:S(2)}, u32[]{:S(2)}) collective-permute-start(f32[4,128]{1,0:T(4,128)S(1)} %slice.215), channel_id=1, source_target_pairs={{0,4},{1,5},{2,6},{3,7},{4,0},{5,1},{6,2},{7,3},{8,12},{9,13},{10,... | collective-permute-start | bytes 6152 | tf_op jit(solution)/shard_map/ppermute | solution.py:25
  41.4 3.7 %collective-permute-start.10 = (f32[4,128]{1,0:T(4,128)S(1)}, f32[4,128]{1,0:T(4,128)S(1)}, u32[]{:S(2)}, u32[]{:S(2)}) collective-permute-start(f32[4,128]{1,0:T(4,128)S(1)} %pad_maximum_fusion.5), channel_id=1, source_target_pairs={{0,2},{1,3},{2,0},{3,1},{4,6},{5,7},{6,4},{7,5},{8,10},{9,11},{10,... | collective-permute-start | bytes 6152 | tf_op jit(solution)/shard_map/ppermute | solution.py:25
  45.1 1.2 %collective-permute-start.11 = (f32[4,128]{1,0:T(4,128)S(1)}, f32[4,128]{1,0:T(4,128)S(1)}, u32[]{:S(2)}, u32[]{:S(2)}) collective-permute-start(f32[4,128]{1,0:T(4,128)S(1)} %pad_maximum_fusion.6), channel_id=1, source_target_pairs={{0,1},{1,0},{2,3},{3,2},{4,5},{5,4},{6,7},{7,6},{8,9},{9,8},{10,11... | collective-permute-start | bytes 6152 | tf_op jit(solution)/shard_map/ppermute | solution.py:25
  58.5 2.2 %collective-permute-start.12 = (bf16[64,5120]{1,0:T(8,128)(2,1)S(1)}, bf16[64,5120]{1,0:T(8,128)(2,1)S(1)}, u32[]{:S(2)}, u32[]{:S(2)}) collective-permute-start(bf16[64,5120]{1,0:T(8,128)(2,1)S(1)} %slice.411), channel_id=1, source_target_pairs={{0,1},{1,0},{2,3},{3,2},{4,5},{5,4},{6,7},{7,6},{8,9},{9,8},{10,11... | collective-permute-start | bytes 1966088 | tf_op jit(solution)/shard_map/ppermute | solution.py:25
  60.8 24.9 %copy-start = (bf16[8,5120]{1,0:T(8,128)(2,1)S(1)}, bf16[8,5120]{1,0:T(8,128)(2,1)}, u32[]{:S(2)}) copy-start(bf16[8,5120]{1,0:T(8,128)(2,1)} %param.7) | copy-start | bytes 245764
  60.8 5.1 %collective-permute-start.16 = (bf16[8,5120]{1,0:T(8,128)(2,1)S(1)}, bf16[8,5120]{1,0:T(8,128)(2,1)S(1)}, u32[]{:S(2)}, u32[]{:S(2)}) collective-permute-start(bf16[8,5120]{1,0:T(8,128)(2,1)S(1)} %get-tuple-element.26), channel_id=1, source_target_pairs={{0,2},{1,3},{2,0},{3,1},{4,6},{5,7},{6,4},{7,5},{8,10},{9,11},{10,... | collective-permute-start | bytes 245768 | tf_op jit(solution)/shard_map/ppermute | solution.py:25
  62.4 7.0 %collective-permute-start.14 = (bf16[16,5120]{1,0:T(8,128)(2,1)S(1)}, bf16[16,5120]{1,0:T(8,128)(2,1)S(1)}, u32[]{:S(2)}, u32[]{:S(2)}) collective-permute-start(bf16[16,5120]{1,0:T(8,128)(2,1)S(1)} %pad_maximum_fusion.1), channel_id=1, source_target_pairs={{0,2},{1,3},{2,0},{3,1},{4,6},{5,7},{6,4},{7,5},{8,10},{9,11},{10,... | collective-permute-start | bytes 491528 | tf_op jit(solution)/shard_map/ppermute | solution.py:25
  66.0 4.5 %collective-permute-start.17 = (bf16[8,5120]{1,0:T(8,128)(2,1)S(1)}, bf16[8,5120]{1,0:T(8,128)(2,1)S(1)}, u32[]{:S(2)}, u32[]{:S(2)}) collective-permute-start(bf16[8,5120]{1,0:T(8,128)(2,1)S(1)} %fusion.23), channel_id=1, source_target_pairs={{0,4},{1,5},{2,6},{3,7},{4,0},{5,1},{6,2},{7,3},{8,12},{9,13},{10,... | collective-permute-start | bytes 245768 | tf_op jit(solution)/shard_map/ppermute | solution.py:25
  67.3 5.5 %collective-permute-start.19 = (f32[5120]{0:T(1024)S(1)}, f32[5120]{0:T(1024)S(1)}, u32[]{:S(2)}, u32[]{:S(2)}) collective-permute-start(f32[5120]{0:T(1024)S(1)} %div.95), channel_id=1, source_target_pairs={{0,1},{1,0},{2,3},{3,2},{4,5},{5,4},{6,7},{7,6},{8,9},{9,8},{10,11... | collective-permute-start | bytes 61448 | tf_op jit(solution)/shard_map/ppermute | solution.py:25
  67.3 18.4 %collective-permute-start.13 = (bf16[8,5120]{1,0:T(8,128)(2,1)S(1)}, bf16[8,5120]{1,0:T(8,128)(2,1)S(1)}, u32[]{:S(2)}, u32[]{:S(2)}) collective-permute-start(bf16[8,5120]{1,0:T(8,128)(2,1)S(1)} %get-tuple-element.25), channel_id=1, source_target_pairs={{0,2},{1,3},{2,0},{3,1},{4,6},{5,7},{6,4},{7,5},{8,10},{9,11},{10,... | collective-permute-start | bytes 245768 | tf_op jit(solution)/shard_map/ppermute | solution.py:25
  70.5 15.2 %collective-permute-start.15 = (bf16[8,5120]{1,0:T(8,128)(2,1)S(1)}, bf16[8,5120]{1,0:T(8,128)(2,1)S(1)}, u32[]{:S(2)}, u32[]{:S(2)}) collective-permute-start(bf16[8,5120]{1,0:T(8,128)(2,1)S(1)} %get-tuple-element.23), channel_id=1, source_target_pairs={{0,4},{1,5},{2,6},{3,7},{4,0},{5,1},{6,2},{7,3},{8,12},{9,13},{10,... | collective-permute-start | bytes 245768 | tf_op jit(solution)/shard_map/ppermute | solution.py:25
  71.8 13.9 %collective-permute-start.18 = (bf16[8,5120]{1,0:T(8,128)(2,1)S(1)}, bf16[8,5120]{1,0:T(8,128)(2,1)S(1)}, u32[]{:S(2)}, u32[]{:S(2)}) collective-permute-start(bf16[8,5120]{1,0:T(8,128)(2,1)S(1)} %get-tuple-element.24), channel_id=1, source_target_pairs={{0,8},{1,9},{2,10},{3,11},{4,12},{5,13},{6,14},{7,15},{8,0},{9,1},... | collective-permute-start | bytes 245768 | tf_op jit(solution)/shard_map/ppermute | solution.py:25
  72.8 3.9 %collective-permute-start.20 = (f32[5120]{0:T(1024)S(1)}, f32[5120]{0:T(1024)S(1)}, u32[]{:S(2)}, u32[]{:S(2)}) collective-permute-start(f32[5120]{0:T(1024)S(1)} %add.221), channel_id=1, source_target_pairs={{0,2},{1,3},{2,0},{3,1},{4,6},{5,7},{6,4},{7,5},{8,10},{9,11},{10,... | collective-permute-start | bytes 61448 | tf_op jit(solution)/shard_map/ppermute | solution.py:25
  76.6 3.8 %collective-permute-start.21 = (f32[5120]{0:T(1024)S(1)}, f32[5120]{0:T(1024)S(1)}, u32[]{:S(2)}, u32[]{:S(2)}) collective-permute-start(f32[5120]{0:T(1024)S(1)} %add.222), channel_id=1, source_target_pairs={{0,4},{1,5},{2,6},{3,7},{4,0},{5,1},{6,2},{7,3},{8,12},{9,13},{10,... | collective-permute-start | bytes 61448 | tf_op jit(solution)/shard_map/ppermute | solution.py:25
  80.4 4.7 %collective-permute-start.22 = (f32[5120]{0:T(1024)S(1)}, f32[5120]{0:T(1024)S(1)}, u32[]{:S(2)}, u32[]{:S(2)}) collective-permute-start(f32[5120]{0:T(1024)S(1)} %add.223), channel_id=1, source_target_pairs={{0,8},{1,9},{2,10},{3,11},{4,12},{5,13},{6,14},{7,15},{8,0},{9,1},... | collective-permute-start | bytes 61448 | tf_op jit(solution)/shard_map/ppermute | solution.py:25
  (1 other events, 8.8 us)

commit v2 on v0

v2 whole, which is shorter than its diff:
```python
import functools

import jax
import jax.numpy as jnp
from jax import lax
from jax.experimental import pallas as pl
from jax.experimental.pallas import tpu as pltpu
from jax.sharding import PartitionSpec as P

epsilon = 1e-06
f32 = jnp.float32
bf16 = jnp.bfloat16
LANES = 128
DIGIT_BITS = 7
DIGIT = 1 << DIGIT_BITS
MIB = 1 << 20
STACK_FLOPS = 20 * 10**9


def cat(*parts):
    return jnp.concatenate(parts, 0)


def bits_of(count):
    return [1 << b for b in range(count.bit_length() - 1)]


class Links:
    def __init__(self, count):
        self.count = count

    def swap(self, value, m):
        return lax.ppermute(value, "vocab", [(i, i ^ m) for i in range(self.count)])

    def gather(self, own):
        swap = self.swap
        if self.count == 16:
            far, diagonal, near, side = swap(own, 8), swap(own, 12), swap(own, 4), swap(own, 2)
            column = stack_blocks(far, diagonal, near)
            across = swap(column, 2)
            twin = swap(cat(own, side, column), 1)
            twin_across = swap(across, 1)
            return cat(own, side, column, across, twin, twin_across)
        blocks = own
        for m in reversed(bits_of(self.count)):
            blocks = cat(blocks, swap(blocks, m))
        return blocks

    def codes(self):
        if self.count == 16:
            first = [0, 2, 8, 12, 4, 10, 14, 6]
            return first + [c ^ 1 for c in first]
        codes = [0]
        for m in reversed(bits_of(self.count)):
            codes = codes + [c ^ m for c in codes]
        return codes

    def gather_small(self, own):
        swap = self.swap
        if self.count == 16:
            column = cat(own, swap(own, 4), swap(own, 8), swap(own, 12))
            return cat(column, swap(column, 1), swap(column, 2), swap(column, 3))
        tiles = own
        for m in bits_of(self.count):
            tiles = cat(tiles, swap(tiles, m))
        return tiles

    def small_place(self, code):
        if self.count == 16:
            return (code & 3) * 4 + (code >> 2)
        return code


def spec(space=pltpu.VMEM):
    return pl.BlockSpec(memory_space=space)


SMEM, VMEM, HBM = spec(pltpu.SMEM), spec(), spec(pltpu.HBM)


def call(kernel, outs, ins, scratch=(), flops=0, moved=0, limit=24):
    return pl.pallas_call(
        kernel,
        out_shape=outs,
        in_specs=ins,
        out_specs=jax.tree.map(lambda _: spec(), outs),
        scratch_shapes=list(scratch),
        compiler_params=pltpu.CompilerParams(vmem_limit_bytes=limit * MIB),
        cost_estimate=pl.CostEstimate(flops=flops, bytes_accessed=moved, transcendentals=0),
    )


def shaped(shape, dtype):
    return jax.ShapeDtypeStruct(shape, dtype)


def norm_kernel(ids_hbm, flags_hbm, rows_hbm, gain_hbm, out_ref, ids, flags, rows, gain, sems):
    copies = [
        pltpu.make_async_copy(src, dst, sems.at[k])
        for k, (src, dst) in enumerate(
            [(rows_hbm, rows), (gain_hbm, gain), (ids_hbm, ids), (flags_hbm, flags)]
        )
    ]
    for copy in copies:
        copy.start()
    for copy in copies:
        copy.wait()
    raw = rows[...].astype(f32)
    own_count, width = raw.shape
    inv_rms = lax.rsqrt(jnp.mean(raw * raw, axis=1, keepdims=True) + epsilon)
    out_ref[:, :width] = (raw * inv_rms * gain[...]).astype(bf16)
    row = lax.broadcasted_iota(jnp.int32, (own_count, LANES), 0)
    lane = lax.broadcasted_iota(jnp.int32, (own_count, LANES), 1)
    notes = jnp.zeros((own_count, LANES), jnp.int32)
    for r in range(own_count):
        label = ids[r]
        digits = (
            label & (DIGIT - 1),
            (label >> DIGIT_BITS) & (DIGIT - 1),
            label >> (2 * DIGIT_BITS),
            flags[r],
        )
        for k, digit in enumerate(digits):
            notes = jnp.where((row == r) & (lane == k), digit, notes)
    out_ref[:, width:] = notes.astype(f32).astype(bf16)


def stack_kernel(*refs):
    ins, out_ref = refs[:-1], refs[-1]
    out_ref[...] = cat(*[ref[...].astype(f32) for ref in ins]).astype(out_ref.dtype)


def stack_blocks(*blocks):
    rows, width = blocks[0].shape
    return call(
        stack_kernel,
        shaped((len(blocks) * rows, width), bf16),
        [VMEM] * len(blocks),
        flops=STACK_FLOPS,
    )(*blocks)


def fold(row):
    c = row.shape[1] // 8
    return cat(*[row[:, k * c : (k + 1) * c] for k in range(8)])


def two_parts(value):
    high = value.astype(bf16).astype(f32)
    return jnp.concatenate([high, value - high], 1)


def one_value(parts):
    c = parts.shape[1] // 2
    return parts[:, :c] + parts[:, c:]


def read_notes(noted):
    label = noted[:, 0:1] + DIGIT * noted[:, 1:2] + DIGIT * DIGIT * noted[:, 2:3]
    return label.astype(jnp.int32), noted[:, 3:4]


def owned_mask(labels, me, slab_width):
    column = lax.broadcasted_iota(jnp.int32, (labels.shape[0], slab_width), 1)
    return column == labels - me * slab_width


def logits_kernel(codes, divisor_ref, rows_ref, head_ref, scaled_ref, stats_ref, blocks):
    me = lax.axis_index("vocab")
    width, slab_width = head_ref.shape
    token_count = rows_ref.shape[0]
    own_count = token_count // len(codes)
    scaled_ref[...] = (
        jnp.dot(rows_ref[:, :width], head_ref[...], preferred_element_type=f32) / divisor_ref[0]
    )
    chunk = 128
    for c in range(token_count // chunk):
        band = slice(c * chunk, (c + 1) * chunk)
        scaled = scaled_ref[band, :]
        labels, mask_f = read_notes(rows_ref[band, width:].astype(f32))
        owned = owned_mask(labels, me, slab_width)
        peak = jnp.max(scaled, axis=1, keepdims=True)
        exp_terms = jnp.exp(scaled - peak)
        columns = (
            peak,
            jnp.sum(exp_terms, axis=1, keepdims=True),
            jnp.sum(exp_terms * scaled, axis=1, keepdims=True),
            jnp.sum(jnp.where(owned, scaled, 0.0), axis=1, keepdims=True),
            mask_f,
        )
        lane = lax.broadcasted_iota(jnp.int32, (chunk, LANES), 1)
        tile = jnp.zeros((chunk, LANES), f32)
        for k, column in enumerate(columns):
            tile = jnp.where(lane == k, column, tile)
        for b in range(chunk // own_count):
            owner = me ^ codes[c * (chunk // own_count) + b]
            blocks[owner] = tile[b * own_count : (b + 1) * own_count]
    for c in range(token_count // chunk):
        per = chunk // own_count
        shared = blocks[c * per : (c + 1) * per].reshape(chunk, LANES)
        stats_ref[:, c * chunk : (c + 1) * chunk] = shared.T[:8]


def slab_kernel(
    codes,
    place,
    divisor_ref,
    tiles_ref,
    rows_ref,
    scaled_ref,
    head_ref,
    gain_ref,
    scalars_ref,
    parts_ref,
    kept_ref,
    sent_ref,
    turned,
    coefs,
    turned_coefs,
    gain_grad,
):
    me = lax.axis_index("vocab")
    count = len(codes)
    width, slab_width = head_ref.shape
    token_count = rows_ref.shape[0]
    own_count = token_count // count
    half = token_count // 2

    def tile(device):
        start = place(device ^ me) * 8
        return tiles_ref[pl.ds(pl.multiple_of(start, 8), 8), :]

    peak = tile(0)[0:1]
    for j in range(1, count):
        peak = jnp.maximum(peak, tile(j)[0:1])
    totals = moments = target_z = jnp.zeros_like(peak)
    for j in range(count):
        t = tile(j)
        fade = jnp.exp(t[0:1] - peak)
        totals += t[1:2] * fade
        moments += t[2:3] * fade
        target_z += t[3:4]
    mask_f = tile(me)[4:5]
    divisor = divisor_ref[0]
    counted = jnp.maximum(jnp.sum(mask_f, axis=1, keepdims=True), 1.0)
    loss = jnp.sum(mask_f * (peak + jnp.log(totals) - target_z), axis=1, keepdims=True) / counted
    temp = -jnp.sum(mask_f * (moments / totals - target_z), axis=1, keepdims=True) / (
        counted * divisor
    )
    lane = lax.broadcasted_iota(jnp.int32, (8, LANES), 1)
    scalars_ref[...] = jnp.where(lane == 0, loss, jnp.where(lane == 1, temp, 0.0))

    factor = mask_f * (token_count / counted) / divisor
    terms = cat(peak, totals, factor, jnp.zeros((LANES - 3, token_count), f32))
    turned[...] = terms.T.reshape(count, own_count, LANES)
    chunk = 64
    per = chunk // own_count
    for c in range(token_count // chunk):
        band = slice(c * chunk, (c + 1) * chunk)
        w = cat(*[turned[me ^ code] for code in codes[c * per : (c + 1) * per]])
        labels, _ = read_notes(rows_ref[band, width:].astype(f32))
        owned = owned_mask(labels, me, slab_width).astype(f32)
        shares = jnp.exp(scaled_ref[band, :] - w[:, 0:1]) / w[:, 1:2]
        coefs[band, :] = w[:, 2:3] * (shares - owned)
    turned_coefs[...] = coefs[...].T.astype(bf16)
    step = width // 2

    @pl.loop(0, width // step)
    def _(n):
        here = pl.ds(pl.multiple_of(n * step, step), step)
        out = jnp.dot(head_ref[here, :], turned_coefs[...], preferred_element_type=f32).T
        kept_ref[:, here] = out[:half]
        sent_ref[:half, here] = out[half:].astype(bf16)
        gain_grad[:, here] = (
            jnp.sum(out * rows_ref[:, here].astype(f32), axis=0, keepdims=True) / gain_ref[:, here]
        )

    parts = two_parts(fold(gain_grad[...])).astype(bf16)
    parts_ref[...] = parts
    sent_ref[half:, : parts.shape[1]] = parts
    sent_ref[half:, parts.shape[1] :] = jnp.zeros((8, width - parts.shape[1]), bf16)


def with_parts(block, gain_sum):
    return jnp.concatenate([block, two_parts(gain_sum)], 1).astype(bf16)


def pair_kernel(order, kept_ref, twin_ref, parts_ref, kept_out, more_out, first_out):
    count = len(order[0]) + len(order[1]) + 1
    half, width = kept_ref.shape
    own_count = half // count
    blocks = [None] * count
    for k in range(count // 2):
        band = slice(2 * k * own_count, 2 * (k + 1) * own_count)
        total = kept_ref[band, :] + twin_ref[band, :].astype(f32)
        blocks[2 * k], blocks[2 * k + 1] = total[:own_count], total[own_count:]
    twin_parts = twin_ref[half:, : parts_ref.shape[1]].astype(f32)
    gain_sum = one_value(parts_ref[...].astype(f32)) + one_value(twin_parts)
    kept_out[...] = cat(*[blocks[k] for k in order[0]])
    more_out[...] = cat(*[blocks[k] for k in order[1]]).astype(bf16)
    first_out[...] = with_parts(blocks[order[2]], gain_sum)


def hop_kernel(at, sent_ref, got_ref, kept_ref, *refs):
    more, out_ref = refs[:-1], refs[-1]
    own_count = sent_ref.shape[0]
    width = kept_ref.shape[1]
    block = kept_ref[at * own_count : (at + 1) * own_count, :] + got_ref[:, :width].astype(f32)
    for ref in more:
        block = block + ref[...].astype(f32)[:own_count]
    gain_sum = one_value(sent_ref[:, width:].astype(f32)) + one_value(
        got_ref[:, width:].astype(f32)
    )
    out_ref[...] = with_parts(block, gain_sum)


def hidden_kernel(places, rows_ref, gain_ref, kept_ref, sent_ref, got_ref, *refs):
    more, (out_ref, gain_out) = refs[:-2], refs[-2:]
    rows = rows_ref[...].astype(f32)
    own_count, width = rows.shape
    inv_rms = lax.rsqrt(jnp.mean(rows * rows, axis=1, keepdims=True) + epsilon)
    units = rows * inv_rms
    grad = kept_ref[:own_count, :] + got_ref[:, :width].astype(f32)
    for ref, at in zip(more, places):
        grad = grad + ref[...].astype(f32)[at * own_count : (at + 1) * own_count]
    grad = grad * gain_ref[...]
    inner_dot = jnp.sum(grad * units, axis=1, keepdims=True)
    out_ref[...] = (inv_rms * (grad - units * inner_dot / width)).astype(bf16)
    gain_sum = one_value(sent_ref[:, width:].astype(f32)) + one_value(
        got_ref[:, width:].astype(f32)
    )
    c = width // 8
    for k in range(8):
        gain_out[:, k * c : (k + 1) * c] = gain_sum[k : k + 1, :]


def on_device(
    backbone_feature_matrix,
    closing_rmsnorm_multiplier,
    output_vocab_matrix,
    softness_divisor,
    correct_label_ids,
    included_place_flags,
):
    count = lax.axis_size("vocab")
    links = Links(count)
    swap = links.swap
    codes = links.codes()
    own_count, width = backbone_feature_matrix.shape
    token_count = own_count * count
    half = token_count // 2
    slab_width = output_vocab_matrix.shape[1]
    gain = closing_rmsnorm_multiplier[None, :]
    head_bytes = 2 * width * slab_width
    product = 2 * token_count * width * slab_width

    own = call(
        norm_kernel,
        shaped((own_count, width + LANES), bf16),
        [HBM] * 4,
        [
            pltpu.SMEM((own_count,), jnp.int32),
            pltpu.SMEM((own_count,), jnp.int32),
            pltpu.VMEM((own_count, width), bf16),
            pltpu.VMEM((1, width), f32),
            pltpu.SemaphoreType.DMA((4,)),
        ],
        limit=63,
    )(correct_label_ids, included_place_flags, backbone_feature_matrix, gain)
    rows = links.gather(own)

    scaled, stats = call(
        functools.partial(logits_kernel, codes),
        (shaped((token_count, slab_width), f32), shaped((8, token_count), f32)),
        [SMEM, VMEM, VMEM],
        [pltpu.VMEM((count, own_count, LANES), f32)],
        flops=product,
        moved=head_bytes,
    )(softness_divisor, rows, output_vocab_matrix)
    tiles = links.gather_small(stats)
    parts_shape = (8, width // 4)
    scalars, parts, kept, sent = call(
        functools.partial(slab_kernel, codes, links.small_place),
        (
            shaped((8, LANES), f32),
            shaped(parts_shape, bf16),
            shaped((half, width), f32),
            shaped((half + 8, width), bf16),
        ),
        [SMEM] + [VMEM] * 5,
        [
            pltpu.VMEM((count, own_count, LANES), f32),
            pltpu.VMEM((token_count, slab_width), f32),
            pltpu.VMEM((slab_width, token_count), bf16),
            pltpu.VMEM((1, width), f32),
        ],
        flops=product,
        moved=head_bytes,
        limit=32,
    )(softness_divisor, tiles, rows, scaled, output_vocab_matrix, gain)
    twin = swap(sent, 1)

    tagged = shaped((own_count, width + parts_shape[1]), bf16)
    if count == 16:
        order = ((0, 2, 4, 3), (5, 7, 1), 6)
        kept, others, first = call(
            functools.partial(pair_kernel, order),
            (
                shaped((4 * own_count, width), f32),
                shaped((3 * own_count, width), bf16),
                tagged,
            ),
            [VMEM] * 3,
            limit=16,
        )(kept, twin, parts)
        got12 = swap(first, 2)
        got = swap(others, 2)
        second = call(functools.partial(hop_kernel, 3), tagged, [VMEM] * 3, limit=8)(
            first, got12, kept
        )
        got8 = swap(second, 4)
        third = call(functools.partial(hop_kernel, 1), tagged, [VMEM] * 4, limit=8)(
            second, got8, kept, got
        )
        last = swap(third, 8)
        b = own_count
        near = swap((kept[2 * b : 3 * b] + got[b : 2 * b].astype(f32)).astype(bf16), 4)
        more, places = [got, near], [2, 0]
    else:
        b = own_count
        kept = kept + twin[:half].astype(f32)
        gain_parts = one_value(parts.astype(f32)) + one_value(
            twin[half:, : parts_shape[1]].astype(f32)
        )
        for m in bits_of(count)[1:]:
            cut = kept.shape[0] // 2
            last = swap(kept[cut:].astype(bf16), m)
            third = two_parts(gain_parts).astype(bf16)
            arrived = swap(third, m)
            if cut > b:
                kept = kept[:cut] + last.astype(f32)
                gain_parts = one_value(third.astype(f32)) + one_value(arrived.astype(f32))
        third = jnp.concatenate([jnp.zeros((b, width), bf16), third], 1)
        last = jnp.concatenate([last, arrived], 1)
        more, places = [], []
    grad_hidden, grad_gain = call(
        functools.partial(hidden_kernel, places),
        (shaped((own_count, width), bf16), shaped((1, width), f32)),
        [VMEM] * (5 + len(more)),
        limit=8,
    )(backbone_feature_matrix, gain, kept, third, last, *more)
    return (grad_hidden, grad_gain[0], scalars[0, 1:2], scalars[0, 0:1])


def solution(mesh):
    in_specs = (
        P(("groups", "vocab"), None),
        P("groups"),
        P("groups", "vocab"),
        P("groups"),
        P(("groups", "vocab")),
        P(("groups", "vocab")),
    )
    out_specs = (P(("groups", "vocab"), None), P("groups"), P("groups"), P("groups"))
    return jax.shard_map(
        on_device, mesh=mesh, in_specs=in_specs, out_specs=out_specs, check_vma=False
    )
```

time: 266 us -> 70 us (0.26)
  blocking collectives: 133 us -> 0 us
  waiting for transfers between devices: 84.5 us -> 35.5 us
  starting transfers between devices: 0.08 us -> 21.3 us
  between operations: 19.8 us -> 1.64 us
  matrix products: 17.8 us -> 0 us
  Pallas kernels: 0 us -> 9.6 us
  other arithmetic: 7.36 us -> 0.06 us
    psum x2 -> x0, blocking collectives: 87.5 us -> none  [the longest x1 58 us: on_device(): grad_gain = lax.psum(jnp.sum(normed_grad * own_units, axis=0), 'vocab')]
    reduce_scatter x1 -> x0, waiting for transfers between devices: 57.9 us -> none  [on_device(): lax.psum_scatter(lax.dot_general(logit_grad, output_vocab_matrix, (((1,),...]
    ppermute x0 -> x19, waiting for transfers between devices: none -> 35.5 us  [swap(): return lax.ppermute(value, 'vocab', [(i, i ^ m) for i in range(self.count)])]
    pmax x1 -> x0, blocking collectives: 31.5 us -> none  [on_device(): peak = lax.pmax(jnp.max(scaled, axis=1), 'vocab')]
    all_gather x1 -> x0, waiting for transfers between devices: 25.9 us -> none  [on_device(): lax.all_gather(backbone_feature_matrix, 'vocab', axis=0, tiled=True)]
    ppermute x0 -> x19, starting transfers between devices: none -> 21.3 us  [swap(): return lax.ppermute(value, 'vocab', [(i, i ^ m) for i in range(self.count)])]
    dot_general x2 -> x0, matrix products: 17.8 us -> none  [the longest x1 10.7 us: on_device(): lax.dot_general(logit_grad, output_vocab_matrix, (((1,), (1,)), ((), ()))...]
    unnamed x1 -> x0, blocking collectives: 13.7 us -> none
  transfers between devices with their start and end apart: 2 -> 19, of which waited for: 2 -> 11; matrix products, arithmetic and copies ran while one was open for 2% -> 2% of each run, Pallas kernels for 0% -> 0%
where the time goes in v2:
time: 70 us; the launch traced here: 69.8 us
  waiting for transfers between devices  35.5 us (51%)
  starting transfers between devices  21.3 us (30%)
  Pallas kernels  9.6 us (14%)
  local copies, waits for them, and re-layouts  1.68 us (2%)
  between operations  1.64 us (2%)
    ppermute x19, waiting for transfers between devices, swap(): return lax.ppermute(value, 'vocab', [(i, i ^ m) for i in range(self.count)])  35.5 us
    ppermute x19, starting transfers between devices, swap(): return lax.ppermute(value, 'vocab', [(i, i ^ m) for i in range(self.count)])  21.3 us
    pallas_call x1, Pallas kernels, on_device(): call(functools.partial(slab_kernel, codes, links.small_place), (shaped((8...  4.57 us
    pallas_call x1, Pallas kernels, on_device(): call(functools.partial(logits_kernel, codes), (shaped((token_count, slab_...  2.19 us
    pallas_call x1, Pallas kernels, on_device(): call(norm_kernel, shaped((own_count, width + LANES), bf16), [HBM] * 4, [p...  1.71 us
  transfers between devices with their start and end apart: 19, of which 11 were waited for; matrix products, arithmetic and copies ran while one was open for 2% of the time, Pallas kernels for 0%

profile of v2, /device:TPU:0, one launch (start us, length us, event | category | flops | bytes accessed | tf_op | source)
XLA Modules:
  0.0 69.8 jit_solution(156169349157513911)
XLA Ops:
  0.6 1.7 %shard_map.93 = bf16[8,5248]{1,0:T(8,128)(2,1)} custom-call(s32[8]{0:T(128)} %ids_hbm.1, s32[8]{0:T(128)} %flags_hbm.1, bf16[8,5120]{1,0:T(8,128)(2,1)} %rows_ref.1, f32[1,5120]{1,0:T(1,128)} %bitcast.6), custom_call_target="tpu_custom_call" | custom-call | tf_op jit(solution)/shard_map/pallas_call | solution.py:357
  2.4 3.1 %collective-permute-start.3 = (bf16[8,5248]{1,0:T(8,128)(2,1)}, bf16[8,5248]{1,0:T(8,128)(2,1)S(1)}, u32[]{:S(2)}, u32[]{:S(2)}) collective-permute-start(bf16[8,5248]{1,0:T(8,128)(2,1)} %shard_map.93), channel_id=1, source_target_pairs={{0,4},{1,5},{2,6},{3,7},{4,0},{5,1},{6,2},{7,3},{8,12},{9,13},{10,... | collective-permute-start | bytes 251912 | tf_op jit(solution)/shard_map/ppermute | solution.py:33
  5.4 2.5 %collective-permute-start.2 = (bf16[8,5248]{1,0:T(8,128)(2,1)}, bf16[8,5248]{1,0:T(8,128)(2,1)S(1)}, u32[]{:S(2)}, u32[]{:S(2)}) collective-permute-start(bf16[8,5248]{1,0:T(8,128)(2,1)} %shard_map.93), channel_id=1, source_target_pairs={{0,12},{1,13},{2,14},{3,15},{4,8},{5,9},{6,10},{7,11},{8,4},{9,5},... | collective-permute-start | bytes 251912 | tf_op jit(solution)/shard_map/ppermute | solution.py:33
  8.0 1.5 %collective-permute-start = (bf16[8,5248]{1,0:T(8,128)(2,1)}, bf16[8,5248]{1,0:T(8,128)(2,1)S(1)}, u32[]{:S(2)}, u32[]{:S(2)}) collective-permute-start(bf16[8,5248]{1,0:T(8,128)(2,1)} %shard_map.93), channel_id=1, source_target_pairs={{0,2},{1,3},{2,0},{3,1},{4,6},{5,7},{6,4},{7,5},{8,10},{9,11},{10,... | collective-permute-start | bytes 251912 | tf_op jit(solution)/shard_map/ppermute | solution.py:33
  9.6 0.9 %constant_dynamic-update-slice_fusion.5 = bf16[128,5248]{1,0:T(8,128)(2,1)S(1)} fusion(bf16[8,5248]{1,0:T(8,128)(2,1)} %shard_map.93), kind=kLoop, calls=%fused_computation.7 | loop fusion | bytes 167936
  11.3 2.0 %collective-permute-done.2.refs_1_ = bf16[8,5248]{1,0:T(8,128)(2,1)S(1)} collective-permute-done((bf16[8,5248]{1,0:T(8,128)(2,1)}, bf16[8,5248]{1,0:T(8,128)(2,1)S(1)}, u32[]{:S(2)}, u32[]{:S(2)}) %collective-permute-start.2) | collective-permute-done | bytes 84000 | tf_op jit(solution)/shard_map/ppermute | solution.py:33
  13.3 2.7 %collective-permute-done.1.refs_0_ = bf16[8,5248]{1,0:T(8,128)(2,1)S(1)} collective-permute-done((bf16[8,5248]{1,0:T(8,128)(2,1)}, bf16[8,5248]{1,0:T(8,128)(2,1)S(1)}, u32[]{:S(2)}, u32[]{:S(2)}) %collective-permute-start.1) | collective-permute-done | bytes 84000 | tf_op jit(solution)/shard_map/ppermute | solution.py:33
  16.0 1.6 %collective-permute-start.4 = (bf16[24,5248]{1,0:T(8,128)(2,1)S(1)}, bf16[24,5248]{1,0:T(8,128)(2,1)S(1)}, u32[]{:S(2)}, u32[]{:S(2)}) collective-permute-start(bf16[24,5248]{1,0:T(8,128)(2,1)S(1)} %shard_map.94), channel_id=1, source_target_pairs={{0,2},{1,3},{2,0},{3,1},{4,6},{5,7},{6,4},{7,5},{8,10},{9,11},{10,... | collective-permute-start | bytes 755720 | tf_op jit(solution)/shard_map/ppermute | solution.py:33
  17.8 6.1 %collective-permute-done.4 = bf16[24,5248]{1,0:T(8,128)(2,1)S(1)} collective-permute-done((bf16[24,5248]{1,0:T(8,128)(2,1)S(1)}, bf16[24,5248]{1,0:T(8,128)(2,1)S(1)}, u32[]{:S(2)}, u32[]{:S(2)}) %collective-permute-start.4) | collective-permute-done | bytes 251936 | tf_op jit(solution)/shard_map/ppermute | solution.py:33
  23.9 1.4 %collective-permute-done.6 = bf16[24,5248]{1,0:T(8,128)(2,1)S(1)} collective-permute-done((bf16[24,5248]{1,0:T(8,128)(2,1)S(1)}, bf16[24,5248]{1,0:T(8,128)(2,1)S(1)}, u32[]{:S(2)}, u32[]{:S(2)}) %collective-permute-start.6) | collective-permute-done | bytes 251936 | tf_op jit(solution)/shard_map/ppermute | solution.py:33
  25.4 2.2 %shard_map.95 = (f32[128,1280]{1,0:T(8,128)S(1)}, f32[8,128]{1,0:T(8,128)S(1)}) custom-call(f32[1]{0:T(128)S(6)} %copy.24.divisor_ref, bf16[128,5248]{1,0:T(8,128)(2,1)S(1)} %constant_dynamic-update-slice_fusion.rows_ref, bf16[5120,1280]{1,0:T(8,128)(2,1)S(1)} %bitcast.5), custom_call_target="tpu_custom_call" | custom-call | flops 1677721600 | bytes 13107200 | tf_op jit(solution)/shard_map/pallas_call | solution.py:372
  27.6 1.7 %collective-permute-start.9 = (f32[8,128]{1,0:T(8,128)S(1)}, f32[8,128]{1,0:T(8,128)S(1)}, u32[]{:S(2)}, u32[]{:S(2)}) collective-permute-start(f32[8,128]{1,0:T(8,128)S(1)} %get-tuple-element.15), channel_id=1, source_target_pairs={{0,12},{1,13},{2,14},{3,15},{4,8},{5,9},{6,10},{7,11},{8,4},{9,5},... | collective-permute-start | bytes 12296 | tf_op jit(solution)/shard_map/ppermute | solution.py:33
  29.3 2.8 %collective-permute-start.7 = (f32[8,128]{1,0:T(8,128)S(1)}, f32[8,128]{1,0:T(8,128)S(1)}, u32[]{:S(2)}, u32[]{:S(2)}) collective-permute-start(f32[8,128]{1,0:T(8,128)S(1)} %get-tuple-element.15), channel_id=1, source_target_pairs={{0,4},{1,5},{2,6},{3,7},{4,0},{5,1},{6,2},{7,3},{8,12},{9,13},{10,... | collective-permute-start | bytes 12296 | tf_op jit(solution)/shard_map/ppermute | solution.py:33
  32.0 1.6 %collective-permute-done.7 = f32[8,128]{1,0:T(8,128)S(1)} collective-permute-done((f32[8,128]{1,0:T(8,128)S(1)}, f32[8,128]{1,0:T(8,128)S(1)}, u32[]{:S(2)}, u32[]{:S(2)}) %collective-permute-start.7) | collective-permute-done | bytes 4128 | tf_op jit(solution)/shard_map/ppermute | solution.py:33
  33.9 1.6 %collective-permute-start.12 = (f32[32,128]{1,0:T(8,128)S(1)}, f32[32,128]{1,0:T(8,128)S(1)}, u32[]{:S(2)}, u32[]{:S(2)}) collective-permute-start(f32[32,128]{1,0:T(8,128)S(1)} %get-tuple-element.28), channel_id=1, source_target_pairs={{0,3},{1,2},{2,1},{3,0},{4,7},{5,6},{6,5},{7,4},{8,11},{9,10},{10,... | collective-permute-start | bytes 49160 | tf_op jit(solution)/shard_map/ppermute | solution.py:33
  36.0 3.2 %collective-permute-done.11 = f32[32,128]{1,0:T(8,128)S(1)} collective-permute-done((f32[32,128]{1,0:T(8,128)S(1)}, f32[32,128]{1,0:T(8,128)S(1)}, u32[]{:S(2)}, u32[]{:S(2)}) %collective-permute-start.11) | collective-permute-done | bytes 16416 | tf_op jit(solution)/shard_map/ppermute | solution.py:33
  39.3 4.6 %shard_map.96 = (f32[8,128]{1,0:T(8,128)S(1)}, bf16[8,1280]{1,0:T(8,128)(2,1)S(1)}, f32[64,5120]{1,0:T(8,128)S(1)}, bf16[72,5120]{1,0:T(8,128)(2,1)S(1)}) custom-call(f32[1]{0:T(128)S(6)} %copy.24.divisor_ref, f32[128,128]{1,0:T(8,128)S(1)} %constant_dynamic-update-slice_fusion.10.tiles_ref, ...), custom_call_target="tpu_custom_call" | custom-call | flops 1677721600 | bytes 13107200 | tf_op jit(solution)/shard_map/pallas_call | solution.py:382
  43.9 2.2 %collective-permute-done.13.twin_ref = bf16[72,5120]{1,0:T(8,128)(2,1)S(1)} collective-permute-done((bf16[72,5120]{1,0:T(8,128)(2,1)S(1)}, bf16[72,5120]{1,0:T(8,128)(2,1)S(1)}, u32[]{:S(2)}, u32[]{:S(2)}) %collective-permute-start.13) | collective-permute-done | bytes 737312 | tf_op jit(solution)/shard_map/ppermute | solution.py:33
  46.8 1.5 %collective-permute-start.14 = (bf16[8,6400]{1,0:T(8,128)(2,1)S(1)}, bf16[8,6400]{1,0:T(8,128)(2,1)S(1)}, u32[]{:S(2)}, u32[]{:S(2)}) collective-permute-start(bf16[8,6400]{1,0:T(8,128)(2,1)S(1)} %get-tuple-element.21.sent_ref), channel_id=1, source_target_pairs={{0,2},{1,3},{2,0},{3,1},{4,6},{5,7},{6,4},{7,5},{8,10},{9,11},{10,... | collective-permute-start | bytes 307208 | tf_op jit(solution)/shard_map/ppermute | solution.py:33
  48.3 8.2 %collective-permute-done.14.got_ref = bf16[8,6400]{1,0:T(8,128)(2,1)S(1)} collective-permute-done((bf16[8,6400]{1,0:T(8,128)(2,1)S(1)}, bf16[8,6400]{1,0:T(8,128)(2,1)S(1)}, u32[]{:S(2)}, u32[]{:S(2)}) %collective-permute-start.14) | collective-permute-done | bytes 102432 | tf_op jit(solution)/shard_map/ppermute | solution.py:33
  56.5 1.9 %collective-permute-start.15 = (bf16[8,6400]{1,0:T(8,128)(2,1)S(1)}, bf16[8,6400]{1,0:T(8,128)(2,1)S(1)}, u32[]{:S(2)}, u32[]{:S(2)}) collective-permute-start(bf16[8,6400]{1,0:T(8,128)(2,1)S(1)} %shard_map.98.sent_ref), channel_id=1, source_target_pairs={{0,4},{1,5},{2,6},{3,7},{4,0},{5,1},{6,2},{7,3},{8,12},{9,13},{10,... | collective-permute-start | bytes 307208 | tf_op jit(solution)/shard_map/ppermute | solution.py:33
  58.7 3.4 %collective-permute-done.15.got_ref = bf16[8,6400]{1,0:T(8,128)(2,1)S(1)} collective-permute-done((bf16[8,6400]{1,0:T(8,128)(2,1)S(1)}, bf16[8,6400]{1,0:T(8,128)(2,1)S(1)}, u32[]{:S(2)}, u32[]{:S(2)}) %collective-permute-start.15) | collective-permute-done | bytes 102432 | tf_op jit(solution)/shard_map/ppermute | solution.py:33
  62.2 1.5 %collective-permute-start.17 = (bf16[8,6400]{1,0:T(8,128)(2,1)S(1)}, bf16[8,6400]{1,0:T(8,128)(2,1)S(1)}, u32[]{:S(2)}, u32[]{:S(2)}) collective-permute-start(bf16[8,6400]{1,0:T(8,128)(2,1)S(1)} %shard_map.99.sent_ref), channel_id=1, source_target_pairs={{0,8},{1,9},{2,10},{3,11},{4,12},{5,13},{6,14},{7,15},{8,0},{9,1},... | collective-permute-start | bytes 307208 | tf_op jit(solution)/shard_map/ppermute | solution.py:33
  64.3 4.6 %collective-permute-done.17.got_ref = bf16[8,6400]{1,0:T(8,128)(2,1)S(1)} collective-permute-done((bf16[8,6400]{1,0:T(8,128)(2,1)S(1)}, bf16[8,6400]{1,0:T(8,128)(2,1)S(1)}, u32[]{:S(2)}, u32[]{:S(2)}) %collective-permute-start.17) | collective-permute-done | bytes 102432 | tf_op jit(solution)/shard_map/ppermute | solution.py:33
  (53 shorter events, 3.7 us)
Async XLA Ops:
  2.4 9.0 %collective-permute-start.3 = (bf16[8,5248]{1,0:T(8,128)(2,1)}, bf16[8,5248]{1,0:T(8,128)(2,1)S(1)}, u32[]{:S(2)}, u32[]{:S(2)}) collective-permute-start(bf16[8,5248]{1,0:T(8,128)(2,1)} %shard_map.93), channel_id=1, source_target_pairs={{0,4},{1,5},{2,6},{3,7},{4,0},{5,1},{6,2},{7,3},{8,12},{9,13},{10,... | collective-permute-start | bytes 251912 | tf_op jit(solution)/shard_map/ppermute | solution.py:33
  5.4 7.9 %collective-permute-start.2 = (bf16[8,5248]{1,0:T(8,128)(2,1)}, bf16[8,5248]{1,0:T(8,128)(2,1)S(1)}, u32[]{:S(2)}, u32[]{:S(2)}) collective-permute-start(bf16[8,5248]{1,0:T(8,128)(2,1)} %shard_map.93), channel_id=1, source_target_pairs={{0,12},{1,13},{2,14},{3,15},{4,8},{5,9},{6,10},{7,11},{8,4},{9,5},... | collective-permute-start | bytes 251912 | tf_op jit(solution)/shard_map/ppermute | solution.py:33
  7.9 8.1 %collective-permute-start.1 = (bf16[8,5248]{1,0:T(8,128)(2,1)}, bf16[8,5248]{1,0:T(8,128)(2,1)S(1)}, u32[]{:S(2)}, u32[]{:S(2)}) collective-permute-start(bf16[8,5248]{1,0:T(8,128)(2,1)} %shard_map.93), channel_id=1, source_target_pairs={{0,8},{1,9},{2,10},{3,11},{4,12},{5,13},{6,14},{7,15},{8,0},{9,1},... | collective-permute-start | bytes 251912 | tf_op jit(solution)/shard_map/ppermute | solution.py:33
  8.0 9.5 %collective-permute-start = (bf16[8,5248]{1,0:T(8,128)(2,1)}, bf16[8,5248]{1,0:T(8,128)(2,1)S(1)}, u32[]{:S(2)}, u32[]{:S(2)}) collective-permute-start(bf16[8,5248]{1,0:T(8,128)(2,1)} %shard_map.93), channel_id=1, source_target_pairs={{0,2},{1,3},{2,0},{3,1},{4,6},{5,7},{6,4},{7,5},{8,10},{9,11},{10,... | collective-permute-start | bytes 251912 | tf_op jit(solution)/shard_map/ppermute | solution.py:33
  10.5 14.9 %slice-start = ((s8[13107200]{0:T(1024)(128)(4,1)}), s8[4194304]{0:T(1024)(128)(4,1)S(1)}, s32[]{:S(2)}) async-start(s8[13107200]{0:T(1024)(128)(4,1)} %bitcast.4), calls=%async_computation | async-start | bytes 8388608
  11.3 14.1 %slice-start.1 = ((s8[13107200]{0:T(1024)(128)(4,1)}), s8[4194304]{0:T(1024)(128)(4,1)S(1)}, s32[]{:S(2)}) async-start(s8[13107200]{0:T(1024)(128)(4,1)} %bitcast.4), calls=%async_computation.1 | async-start | bytes 8388608
  11.3 14.1 %slice-start.2 = ((s8[13107200]{0:T(1024)(128)(4,1)}), s8[4194304]{0:T(1024)(128)(4,1)S(1)}, s32[]{:S(2)}) async-start(s8[13107200]{0:T(1024)(128)(4,1)} %bitcast.4), calls=%async_computation.2 | async-start | bytes 8388608
  11.3 14.1 %slice-start.3 = ((s8[13107200]{0:T(1024)(128)(4,1)}), s8[524288]{0:T(1024)(128)(4,1)S(1)}, s32[]{:S(2)}) async-start(s8[13107200]{0:T(1024)(128)(4,1)} %bitcast.4), calls=%async_computation.3 | async-start | bytes 1048576
  16.0 7.8 %collective-permute-start.4 = (bf16[24,5248]{1,0:T(8,128)(2,1)S(1)}, bf16[24,5248]{1,0:T(8,128)(2,1)S(1)}, u32[]{:S(2)}, u32[]{:S(2)}) collective-permute-start(bf16[24,5248]{1,0:T(8,128)(2,1)S(1)} %shard_map.94), channel_id=1, source_target_pairs={{0,2},{1,3},{2,0},{3,1},{4,6},{5,7},{6,4},{7,5},{8,10},{9,11},{10,... | collective-permute-start | bytes 755720 | tf_op jit(solution)/shard_map/ppermute | solution.py:33
  17.6 6.2 %collective-permute-start.5 = (bf16[40,5248]{1,0:T(8,128)(2,1)S(1)}, bf16[40,5248]{1,0:T(8,128)(2,1)S(1)}, u32[]{:S(2)}, u32[]{:S(2)}) collective-permute-start(bf16[40,5248]{1,0:T(8,128)(2,1)S(1)} %pad_maximum_fusion), channel_id=1, source_target_pairs={{0,1},{1,0},{2,3},{3,2},{4,5},{5,4},{6,7},{7,6},{8,9},{9,8},{10,11... | collective-permute-start | bytes 1259528 | tf_op jit(solution)/shard_map/ppermute | solution.py:33
  23.8 1.5 %collective-permute-start.6 = (bf16[24,5248]{1,0:T(8,128)(2,1)S(1)}, bf16[24,5248]{1,0:T(8,128)(2,1)S(1)}, u32[]{:S(2)}, u32[]{:S(2)}) collective-permute-start(bf16[24,5248]{1,0:T(8,128)(2,1)S(1)} %collective-permute-done.4), channel_id=1, source_target_pairs={{0,1},{1,0},{2,3},{3,2},{4,5},{5,4},{6,7},{7,6},{8,9},{9,8},{10,11... | collective-permute-start | bytes 755720 | tf_op jit(solution)/shard_map/ppermute | solution.py:33
  27.6 6.2 %collective-permute-start.9 = (f32[8,128]{1,0:T(8,128)S(1)}, f32[8,128]{1,0:T(8,128)S(1)}, u32[]{:S(2)}, u32[]{:S(2)}) collective-permute-start(f32[8,128]{1,0:T(8,128)S(1)} %get-tuple-element.15), channel_id=1, source_target_pairs={{0,12},{1,13},{2,14},{3,15},{4,8},{5,9},{6,10},{7,11},{8,4},{9,5},... | collective-permute-start | bytes 12296 | tf_op jit(solution)/shard_map/ppermute | solution.py:33
  29.3 4.5 %collective-permute-start.8 = (f32[8,128]{1,0:T(8,128)S(1)}, f32[8,128]{1,0:T(8,128)S(1)}, u32[]{:S(2)}, u32[]{:S(2)}) collective-permute-start(f32[8,128]{1,0:T(8,128)S(1)} %get-tuple-element.15), channel_id=1, source_target_pairs={{0,8},{1,9},{2,10},{3,11},{4,12},{5,13},{6,14},{7,15},{8,0},{9,1},... | collective-permute-start | bytes 12296 | tf_op jit(solution)/shard_map/ppermute | solution.py:33
  29.3 4.3 %collective-permute-start.7 = (f32[8,128]{1,0:T(8,128)S(1)}, f32[8,128]{1,0:T(8,128)S(1)}, u32[]{:S(2)}, u32[]{:S(2)}) collective-permute-start(f32[8,128]{1,0:T(8,128)S(1)} %get-tuple-element.15), channel_id=1, source_target_pairs={{0,4},{1,5},{2,6},{3,7},{4,0},{5,1},{6,2},{7,3},{8,12},{9,13},{10,... | collective-permute-start | bytes 12296 | tf_op jit(solution)/shard_map/ppermute | solution.py:33
  33.8 2.2 %collective-permute-start.10 = (f32[32,128]{1,0:T(8,128)S(1)}, f32[32,128]{1,0:T(8,128)S(1)}, u32[]{:S(2)}, u32[]{:S(2)}) collective-permute-start(f32[32,128]{1,0:T(8,128)S(1)} %get-tuple-element.28), channel_id=1, source_target_pairs={{0,1},{1,0},{2,3},{3,2},{4,5},{5,4},{6,7},{7,6},{8,9},{9,8},{10,11... | collective-permute-start | bytes 49160 | tf_op jit(solution)/shard_map/ppermute | solution.py:33
  33.9 5.4 %collective-permute-start.12 = (f32[32,128]{1,0:T(8,128)S(1)}, f32[32,128]{1,0:T(8,128)S(1)}, u32[]{:S(2)}, u32[]{:S(2)}) collective-permute-start(f32[32,128]{1,0:T(8,128)S(1)} %get-tuple-element.28), channel_id=1, source_target_pairs={{0,3},{1,2},{2,1},{3,0},{4,7},{5,6},{6,5},{7,4},{8,11},{9,10},{10,... | collective-permute-start | bytes 49160 | tf_op jit(solution)/shard_map/ppermute | solution.py:33
  35.5 3.7 %collective-permute-start.11 = (f32[32,128]{1,0:T(8,128)S(1)}, f32[32,128]{1,0:T(8,128)S(1)}, u32[]{:S(2)}, u32[]{:S(2)}) collective-permute-start(f32[32,128]{1,0:T(8,128)S(1)} %get-tuple-element.28), channel_id=1, source_target_pairs={{0,2},{1,3},{2,0},{3,1},{4,6},{5,7},{6,4},{7,5},{8,10},{9,11},{10,... | collective-permute-start | bytes 49160 | tf_op jit(solution)/shard_map/ppermute | solution.py:33
  43.8 2.3 %collective-permute-start.13 = (bf16[72,5120]{1,0:T(8,128)(2,1)S(1)}, bf16[72,5120]{1,0:T(8,128)(2,1)S(1)}, u32[]{:S(2)}, u32[]{:S(2)}) collective-permute-start(bf16[72,5120]{1,0:T(8,128)(2,1)S(1)} %get-tuple-element.18), channel_id=1, source_target_pairs={{0,1},{1,0},{2,3},{3,2},{4,5},{5,4},{6,7},{7,6},{8,9},{9,8},{10,11... | collective-permute-start | bytes 2211848 | tf_op jit(solution)/shard_map/ppermute | solution.py:33
  46.2 22.7 %copy-start = (bf16[8,5120]{1,0:T(8,128)(2,1)S(1)}, bf16[8,5120]{1,0:T(8,128)(2,1)}, u32[]{:S(2)}) copy-start(bf16[8,5120]{1,0:T(8,128)(2,1)} %rows_ref.1) | copy-start | bytes 245764
  46.2 12.2 %collective-permute-start.16 = (bf16[24,5120]{1,0:T(8,128)(2,1)S(1)}, bf16[24,5120]{1,0:T(8,128)(2,1)S(1)}, u32[]{:S(2)}, u32[]{:S(2)}) collective-permute-start(bf16[24,5120]{1,0:T(8,128)(2,1)S(1)} %get-tuple-element.22), channel_id=1, source_target_pairs={{0,2},{1,3},{2,0},{3,1},{4,6},{5,7},{6,4},{7,5},{8,10},{9,11},{10,... | collective-permute-start | bytes 737288 | tf_op jit(solution)/shard_map/ppermute | solution.py:33
  46.8 9.7 %collective-permute-start.14 = (bf16[8,6400]{1,0:T(8,128)(2,1)S(1)}, bf16[8,6400]{1,0:T(8,128)(2,1)S(1)}, u32[]{:S(2)}, u32[]{:S(2)}) collective-permute-start(bf16[8,6400]{1,0:T(8,128)(2,1)S(1)} %get-tuple-element.21.sent_ref), channel_id=1, source_target_pairs={{0,2},{1,3},{2,0},{3,1},{4,6},{5,7},{6,4},{7,5},{8,10},{9,11},{10,... | collective-permute-start | bytes 307208 | tf_op jit(solution)/shard_map/ppermute | solution.py:33
  56.5 5.6 %collective-permute-start.15 = (bf16[8,6400]{1,0:T(8,128)(2,1)S(1)}, bf16[8,6400]{1,0:T(8,128)(2,1)S(1)}, u32[]{:S(2)}, u32[]{:S(2)}) collective-permute-start(bf16[8,6400]{1,0:T(8,128)(2,1)S(1)} %shard_map.98.sent_ref), channel_id=1, source_target_pairs={{0,4},{1,5},{2,6},{3,7},{4,0},{5,1},{6,2},{7,3},{8,12},{9,13},{10,... | collective-permute-start | bytes 307208 | tf_op jit(solution)/shard_map/ppermute | solution.py:33
  58.5 5.8 %collective-permute-start.18 = (bf16[8,5120]{1,0:T(8,128)(2,1)S(1)}, bf16[8,5120]{1,0:T(8,128)(2,1)S(1)}, u32[]{:S(2)}, u32[]{:S(2)}) collective-permute-start(bf16[8,5120]{1,0:T(8,128)(2,1)S(1)} %add_convert_fusion), channel_id=1, source_target_pairs={{0,4},{1,5},{2,6},{3,7},{4,0},{5,1},{6,2},{7,3},{8,12},{9,13},{10,... | collective-permute-start | bytes 245768 | tf_op jit(solution)/shard_map/ppermute | solution.py:33
  62.2 6.7 %collective-permute-start.17 = (bf16[8,6400]{1,0:T(8,128)(2,1)S(1)}, bf16[8,6400]{1,0:T(8,128)(2,1)S(1)}, u32[]{:S(2)}, u32[]{:S(2)}) collective-permute-start(bf16[8,6400]{1,0:T(8,128)(2,1)S(1)} %shard_map.99.sent_ref), channel_id=1, source_target_pairs={{0,8},{1,9},{2,10},{3,11},{4,12},{5,13},{6,14},{7,15},{8,0},{9,1},... | collective-permute-start | bytes 307208 | tf_op jit(solution)/shard_map/ppermute | solution.py:33
  (2 other events, 20.1 us)

commit v3 on v2

--- a/solution.py
+++ b/solution.py
@@ -15,6 +15,8 @@
 DIGIT = 1 << DIGIT_BITS
 MIB = 1 << 20
 STACK_FLOPS = 20 * 10**9
+REST_FLOPS = 3 * 10**9
+TURN_FLOPS = 3 * 10**9
 
 
 def cat(*parts):
@@ -40,11 +42,11 @@
             across = swap(column, 2)
             twin = swap(cat(own, side, column), 1)
             twin_across = swap(across, 1)
-            return cat(own, side, column, across, twin, twin_across)
+            return cat(own, side, column, across, twin, twin_across), column
         blocks = own
         for m in reversed(bits_of(self.count)):
             blocks = cat(blocks, swap(blocks, m))
-        return blocks
+        return blocks, own
 
     def codes(self):
         if self.count == 16:
@@ -58,8 +60,8 @@
     def gather_small(self, own):
         swap = self.swap
         if self.count == 16:
-            column = cat(own, swap(own, 4), swap(own, 8), swap(own, 12))
-            return cat(column, swap(column, 1), swap(column, 2), swap(column, 3))
+            column = cat(own, swap(own, 12), swap(own, 8), swap(own, 4))
+            return cat(column, swap(column, 3), swap(column, 2), swap(column, 1))
         tiles = own
         for m in bits_of(self.count):
             tiles = cat(tiles, swap(tiles, m))
@@ -67,7 +69,7 @@
 
     def small_place(self, code):
         if self.count == 16:
-            return (code & 3) * 4 + (code >> 2)
+            return ((4 - (code & 3)) & 3) * 4 + ((4 - (code >> 2)) & 3)
         return code
 
 
@@ -155,6 +157,16 @@
     return parts[:, :c] + parts[:, c:]
 
 
+def turn_kernel(head_ref, order_ref, out_ref):
+    step = 512
+    width = head_ref.shape[0]
+
+    @pl.loop(0, width // step)
+    def _(n):
+        here = pl.ds(pl.multiple_of(n * step, step), step)
+        out_ref[:, here] = head_ref[here, :].T
+
+
 def read_notes(noted):
     label = noted[:, 0:1] + DIGIT * noted[:, 1:2] + DIGIT * DIGIT * noted[:, 2:3]
     return label.astype(jnp.int32), noted[:, 3:4]
@@ -165,7 +177,9 @@
     return column == labels - me * slab_width
 
 
-def logits_kernel(codes, divisor_ref, rows_ref, head_ref, scaled_ref, stats_ref, blocks):
+def logits_kernel(
+    codes, divisor_ref, rows_ref, head_ref, order_ref, scaled_ref, stats_ref, blocks
+):
     me = lax.axis_index("vocab")
     width, slab_width = head_ref.shape
     token_count = rows_ref.shape[0]
@@ -216,12 +230,10 @@
     sent_ref,
     turned,
     coefs,
-    turned_coefs,
-    gain_grad,
 ):
     me = lax.axis_index("vocab")
     count = len(codes)
-    width, slab_width = head_ref.shape
+    slab_width, width = head_ref.shape
     token_count = rows_ref.shape[0]
     own_count = token_count // count
     half = token_count // 2
@@ -261,77 +273,57 @@
         labels, _ = read_notes(rows_ref[band, width:].astype(f32))
         owned = owned_mask(labels, me, slab_width).astype(f32)
         shares = jnp.exp(scaled_ref[band, :] - w[:, 0:1]) / w[:, 1:2]
-        coefs[band, :] = w[:, 2:3] * (shares - owned)
-    turned_coefs[...] = coefs[...].T.astype(bf16)
-    step = width // 2
-
-    @pl.loop(0, width // step)
-    def _(n):
-        here = pl.ds(pl.multiple_of(n * step, step), step)
-        out = jnp.dot(head_ref[here, :], turned_coefs[...], preferred_element_type=f32).T
-        kept_ref[:, here] = out[:half]
-        sent_ref[:half, here] = out[half:].astype(bf16)
-        gain_grad[:, here] = (
-            jnp.sum(out * rows_ref[:, here].astype(f32), axis=0, keepdims=True) / gain_ref[:, here]
-        )
-
-    parts = two_parts(fold(gain_grad[...])).astype(bf16)
+        coefs[band, :] = (w[:, 2:3] * (shares - owned)).astype(bf16)
+    out = jnp.dot(coefs[...], head_ref[...], preferred_element_type=f32)
+    kept_ref[...] = out[:half]
+    sent_ref[:half, :] = out[half:].astype(bf16)
+    gain_grad = (
+        jnp.sum(out * rows_ref[:, :width].astype(f32), axis=0, keepdims=True) / gain_ref[...]
+    )
+
+    parts = two_parts(fold(gain_grad)).astype(bf16)
     parts_ref[...] = parts
     sent_ref[half:, : parts.shape[1]] = parts
     sent_ref[half:, parts.shape[1] :] = jnp.zeros((8, width - parts.shape[1]), bf16)
 
 
-def with_parts(block, gain_sum):
-    return jnp.concatenate([block, two_parts(gain_sum)], 1).astype(bf16)
-
-
-def pair_kernel(order, kept_ref, twin_ref, parts_ref, kept_out, more_out, first_out):
-    count = len(order[0]) + len(order[1]) + 1
-    half, width = kept_ref.shape
-    own_count = half // count
-    blocks = [None] * count
-    for k in range(count // 2):
-        band = slice(2 * k * own_count, 2 * (k + 1) * own_count)
-        total = kept_ref[band, :] + twin_ref[band, :].astype(f32)
-        blocks[2 * k], blocks[2 * k + 1] = total[:own_count], total[own_count:]
-    twin_parts = twin_ref[half:, : parts_ref.shape[1]].astype(f32)
-    gain_sum = one_value(parts_ref[...].astype(f32)) + one_value(twin_parts)
-    kept_out[...] = cat(*[blocks[k] for k in order[0]])
-    more_out[...] = cat(*[blocks[k] for k in order[1]]).astype(bf16)
-    first_out[...] = with_parts(blocks[order[2]], gain_sum)
-
-
-def hop_kernel(at, sent_ref, got_ref, kept_ref, *refs):
+def pair_kernel(order, own_count, kept_ref, twin_ref, *outs):
+    for o, out in zip(order, outs):
+        blocks = []
+        for k in o:
+            even = k // 2 * 2 * own_count
+            band = slice(even, even + 2 * own_count)
+            total = kept_ref[band, :] + twin_ref[band, :].astype(f32)
+            blocks.append(total[k % 2 * own_count : (k % 2 + 1) * own_count])
+        out[...] = cat(*blocks).astype(out.dtype)
+
+
+def rest_kernel(order, own_count, order_ref, kept_ref, twin_ref, parts_ref, gain_out, *outs):
+    pair_kernel(order, own_count, kept_ref, twin_ref, *outs)
+    parts = parts_ref[...].astype(f32)
+    twin_parts = twin_ref[twin_ref.shape[0] - 8 :, : parts.shape[1]].astype(f32)
+    gain_sum = one_value(parts) + one_value(twin_parts)
+    c = gain_out.shape[1] // 8
+    for k in range(8):
+        gain_out[:, k * c : (k + 1) * c] = gain_sum[k : k + 1, :]
+
+
+def sum_kernel(order_ref, own_ref, near_ref, mid_ref, far_ref, out_ref):
+    out_ref[...] = (own_ref[...] + near_ref[...]) + (mid_ref[...] + far_ref[...])
+
+
+def hidden_kernel(rows_ref, gain_ref, kept_ref, *refs):
     more, out_ref = refs[:-1], refs[-1]
-    own_count = sent_ref.shape[0]
-    width = kept_ref.shape[1]
-    block = kept_ref[at * own_count : (at + 1) * own_count, :] + got_ref[:, :width].astype(f32)
-    for ref in more:
-        block = block + ref[...].astype(f32)[:own_count]
-    gain_sum = one_value(sent_ref[:, width:].astype(f32)) + one_value(
-        got_ref[:, width:].astype(f32)
-    )
-    out_ref[...] = with_parts(block, gain_sum)
-
-
-def hidden_kernel(places, rows_ref, gain_ref, kept_ref, sent_ref, got_ref, *refs):
-    more, (out_ref, gain_out) = refs[:-2], refs[-2:]
     rows = rows_ref[...].astype(f32)
     own_count, width = rows.shape
     inv_rms = lax.rsqrt(jnp.mean(rows * rows, axis=1, keepdims=True) + epsilon)
     units = rows * inv_rms
-    grad = kept_ref[:own_count, :] + got_ref[:, :width].astype(f32)
-    for ref, at in zip(more, places):
-        grad = grad + ref[...].astype(f32)[at * own_count : (at + 1) * own_count]
+    grad = kept_ref[:own_count, :]
+    for ref in more:
+        grad = grad + ref[...].astype(f32)
     grad = grad * gain_ref[...]
     inner_dot = jnp.sum(grad * units, axis=1, keepdims=True)
     out_ref[...] = (inv_rms * (grad - units * inner_dot / width)).astype(bf16)
-    gain_sum = one_value(sent_ref[:, width:].astype(f32)) + one_value(
-        got_ref[:, width:].astype(f32)
-    )
-    c = width // 8
-    for k in range(8):
-        gain_out[:, k * c : (k + 1) * c] = gain_sum[k : k + 1, :]
 
 
 def on_device(
@@ -367,16 +359,24 @@
         ],
         limit=63,
     )(correct_label_ids, included_place_flags, backbone_feature_matrix, gain)
-    rows = links.gather(own)
+    rows, early = links.gather(own)
+    head_t = call(
+        turn_kernel,
+        shaped((slab_width, width), bf16),
+        [VMEM, spec(pl.ANY)],
+        flops=TURN_FLOPS,
+        moved=2 * head_bytes,
+        limit=4,
+    )(output_vocab_matrix, early)
 
     scaled, stats = call(
         functools.partial(logits_kernel, codes),
         (shaped((token_count, slab_width), f32), shaped((8, token_count), f32)),
-        [SMEM, VMEM, VMEM],
+        [SMEM, VMEM, VMEM, spec(pl.ANY)],
         [pltpu.VMEM((count, own_count, LANES), f32)],
         flops=product,
         moved=head_bytes,
-    )(softness_divisor, rows, output_vocab_matrix)
+    )(softness_divisor, rows, output_vocab_matrix, head_t)
     tiles = links.gather_small(stats)
     parts_shape = (8, width // 4)
     scalars, parts, kept, sent = call(
@@ -390,66 +390,59 @@
         [SMEM] + [VMEM] * 5,
         [
             pltpu.VMEM((count, own_count, LANES), f32),
-            pltpu.VMEM((token_count, slab_width), f32),
-            pltpu.VMEM((slab_width, token_count), bf16),
-            pltpu.VMEM((1, width), f32),
+            pltpu.VMEM((token_count, slab_width), bf16),
         ],
         flops=product,
         moved=head_bytes,
         limit=32,
-    )(softness_divisor, tiles, rows, scaled, output_vocab_matrix, gain)
+    )(softness_divisor, tiles, rows, scaled, head_t, gain)
     twin = swap(sent, 1)
 
-    tagged = shaped((own_count, width + parts_shape[1]), bf16)
+    b = own_count
     if count == 16:
-        order = ((0, 2, 4, 3), (5, 7, 1), 6)
-        kept, others, first = call(
-            functools.partial(pair_kernel, order),
-            (
-                shaped((4 * own_count, width), f32),
-                shaped((3 * own_count, width), bf16),
-                tagged,
-            ),
-            [VMEM] * 3,
-            limit=16,
-        )(kept, twin, parts)
-        got12 = swap(first, 2)
-        got = swap(others, 2)
-        second = call(functools.partial(hop_kernel, 3), tagged, [VMEM] * 3, limit=8)(
-            first, got12, kept
-        )
-        got8 = swap(second, 4)
-        third = call(functools.partial(hop_kernel, 1), tagged, [VMEM] * 4, limit=8)(
-            second, got8, kept, got
-        )
-        last = swap(third, 8)
-        b = own_count
-        near = swap((kept[2 * b : 3 * b] + got[b : 2 * b].astype(f32)).astype(bf16), 4)
-        more, places = [got, near], [2, 0]
+        going_order = (7, 5, 6)
+        rest_order = ((0, 4, 2, 3), (1,))
+        sizes = [(4, f32), (1, bf16)]
     else:
-        b = own_count
-        kept = kept + twin[:half].astype(f32)
-        gain_parts = one_value(parts.astype(f32)) + one_value(
-            twin[half:, : parts_shape[1]].astype(f32)
-        )
+        quarter = count // 4
+        going_order = tuple(range(quarter, 2 * quarter))
+        rest_order = (tuple(range(quarter)),)
+        sizes = [(quarter, f32)]
+    going = call(
+        functools.partial(pair_kernel, (going_order,), b),
+        shaped((len(going_order) * b, width), bf16),
+        [VMEM] * 2,
+    )(kept, twin)
+    gain_grad, kept, *rest = call(
+        functools.partial(rest_kernel, rest_order, b),
+        (shaped((1, width), f32),) + tuple(shaped((k * b, width), t) for k, t in sizes),
+        [spec(pl.ANY)] + [VMEM] * 3,
+        flops=REST_FLOPS,
+    )(going, kept, twin, parts)
+    if count == 16:
+        crossed = swap(going, 2)
+        beside = swap(rest[0], 2)
+        gain_far, gain_mid, gain_near = [swap(gain_grad, m) for m in (12, 8, 4)]
+        gain_grad = call(
+            sum_kernel, shaped((1, width), f32), [spec(pl.ANY)] + [VMEM] * 4, limit=8
+        )(crossed, gain_grad, gain_near, gain_mid, gain_far)
+        gain_grad = gain_grad + swap(gain_grad, 2)
+        column = (kept[b:] + crossed.astype(f32)).astype(bf16)
+        more = [beside] + [
+            swap(column[k * b : (k + 1) * b], m) for k, m in ((2, 12), (1, 8), (0, 4))
+        ]
+    else:
         for m in bits_of(count)[1:]:
+            gain_grad = gain_grad + swap(gain_grad, m)
+        for m in bits_of(count)[1:-1]:
+            kept = kept + swap(going, m).astype(f32)
             cut = kept.shape[0] // 2
-            last = swap(kept[cut:].astype(bf16), m)
-            third = two_parts(gain_parts).astype(bf16)
-            arrived = swap(third, m)
-            if cut > b:
-                kept = kept[:cut] + last.astype(f32)
-                gain_parts = one_value(third.astype(f32)) + one_value(arrived.astype(f32))
-        third = jnp.concatenate([jnp.zeros((b, width), bf16), third], 1)
-        last = jnp.concatenate([last, arrived], 1)
-        more, places = [], []
-    grad_hidden, grad_gain = call(
-        functools.partial(hidden_kernel, places),
-        (shaped((own_count, width), bf16), shaped((1, width), f32)),
-        [VMEM] * (5 + len(more)),
-        limit=8,
-    )(backbone_feature_matrix, gain, kept, third, last, *more)
-    return (grad_hidden, grad_gain[0], scalars[0, 1:2], scalars[0, 0:1])
+            kept, going = kept[:cut], kept[cut:].astype(bf16)
+        more = [swap(going, count // 2)]
+    grad_hidden = call(
+        hidden_kernel, shaped((b, width), bf16), [VMEM] * (3 + len(more)), limit=8
+    )(backbone_feature_matrix, gain, kept, *more)
+    return (grad_hidden, gain_grad[0], scalars[0, 1:2], scalars[0, 0:1])
 
 
 def solution(mesh):

time: 70 us -> 64.9 us (0.927)
  waiting for transfers between devices: 35.5 us -> 22.1 us
  starting transfers between devices: 21.3 us -> 26.7 us
  Pallas kernels: 9.6 us -> 11.8 us
    ppermute x19 -> x23, waiting for transfers between devices: 35.5 us -> 22.1 us  [swap(): return lax.ppermute(value, 'vocab', [(i, i ^ m) for i in range(self.count)])]
    ppermute x19 -> x23, starting transfers between devices: 21.3 us -> 26.7 us  [swap(): return lax.ppermute(value, 'vocab', [(i, i ^ m) for i in range(self.count)])]
    pallas_call x4 -> x5, Pallas kernels: 1.11 us -> 5.32 us  [the longest x1 4.22 us: on_device(): call(turn_kernel, shaped((slab_width, width), bf16), [VMEM, spec(pl.ANY)]...]
    pallas_call x1, Pallas kernels: 4.57 us -> 2.45 us  [on_device(): call(functools.partial(slab_kernel, codes, links.small_place), (shaped((8...]
  transfers between devices with their start and end apart: 19 -> 23, of which waited for: 11 -> 10; matrix products, arithmetic and copies ran while one was open for 2% -> 4% of each run, Pallas kernels for 0% -> 7%
where the time goes in v3:
time: 64.9 us; the launch traced here: 64.7 us
  starting transfers between devices  26.7 us (41%)
  waiting for transfers between devices  22.1 us (34%)
  Pallas kernels  11.8 us (18%)
  local copies, waits for them, and re-layouts  1.7 us (3%)
  between operations  1.7 us (3%)
  other arithmetic  0.73 us (1%)
    ppermute x23, starting transfers between devices, swap(): return lax.ppermute(value, 'vocab', [(i, i ^ m) for i in range(self.count)])  26.7 us
    ppermute x23, waiting for transfers between devices, swap(): return lax.ppermute(value, 'vocab', [(i, i ^ m) for i in range(self.count)])  22.1 us
    pallas_call x1, Pallas kernels, on_device(): call(turn_kernel, shaped((slab_width, width), bf16), [VMEM, spec(pl.ANY)]...  4.22 us
    pallas_call x1, Pallas kernels, on_device(): call(functools.partial(slab_kernel, codes, links.small_place), (shaped((8...  2.45 us
    pallas_call x1, Pallas kernels, on_device(): call(functools.partial(logits_kernel, codes), (shaped((token_count, slab_...  2.32 us
    pallas_call x1, Pallas kernels, on_device(): call(norm_kernel, shaped((own_count, width + LANES), bf16), [HBM] * 4, [p...  1.71 us
  transfers between devices with their start and end apart: 23, of which 10 were waited for; matrix products, arithmetic and copies ran while one was open for 4% of the time, Pallas kernels for 7%

profile of v3, /device:TPU:0, one launch (start us, length us, event | category | flops | bytes accessed | tf_op | source)
XLA Modules:
  0.0 64.7 jit_solution(17829272289995758695)
XLA Ops:
  0.6 1.7 %shard_map.93 = bf16[8,5248]{1,0:T(8,128)(2,1)} custom-call(s32[8]{0:T(128)} %ids_hbm.1, s32[8]{0:T(128)} %flags_hbm.1, bf16[8,5120]{1,0:T(8,128)(2,1)} %rows_ref.1, f32[1,5120]{1,0:T(1,128)} %bitcast.6), custom_call_target="tpu_custom_call" | custom-call | tf_op jit(solution)/shard_map/pallas_call | solution.py:349
  2.3 3.1 %collective-permute-start.3 = (bf16[8,5248]{1,0:T(8,128)(2,1)}, bf16[8,5248]{1,0:T(8,128)(2,1)S(1)}, u32[]{:S(2)}, u32[]{:S(2)}) collective-permute-start(bf16[8,5248]{1,0:T(8,128)(2,1)} %shard_map.93), channel_id=1, source_target_pairs={{0,4},{1,5},{2,6},{3,7},{4,0},{5,1},{6,2},{7,3},{8,12},{9,13},{10,... | collective-permute-start | bytes 251912 | tf_op jit(solution)/shard_map/ppermute | solution.py:35
  5.4 2.5 %collective-permute-start.2 = (bf16[8,5248]{1,0:T(8,128)(2,1)}, bf16[8,5248]{1,0:T(8,128)(2,1)S(1)}, u32[]{:S(2)}, u32[]{:S(2)}) collective-permute-start(bf16[8,5248]{1,0:T(8,128)(2,1)} %shard_map.93), channel_id=1, source_target_pairs={{0,12},{1,13},{2,14},{3,15},{4,8},{5,9},{6,10},{7,11},{8,4},{9,5},... | collective-permute-start | bytes 251912 | tf_op jit(solution)/shard_map/ppermute | solution.py:35
  8.0 1.5 %collective-permute-start = (bf16[8,5248]{1,0:T(8,128)(2,1)}, bf16[8,5248]{1,0:T(8,128)(2,1)S(1)}, u32[]{:S(2)}, u32[]{:S(2)}) collective-permute-start(bf16[8,5248]{1,0:T(8,128)(2,1)} %shard_map.93), channel_id=1, source_target_pairs={{0,2},{1,3},{2,0},{3,1},{4,6},{5,7},{6,4},{7,5},{8,10},{9,11},{10,... | collective-permute-start | bytes 251912 | tf_op jit(solution)/shard_map/ppermute | solution.py:35
  11.3 2.0 %collective-permute-done.2.refs_1_ = bf16[8,5248]{1,0:T(8,128)(2,1)S(1)} collective-permute-done((bf16[8,5248]{1,0:T(8,128)(2,1)}, bf16[8,5248]{1,0:T(8,128)(2,1)S(1)}, u32[]{:S(2)}, u32[]{:S(2)}) %collective-permute-start.2) | collective-permute-done | bytes 84000 | tf_op jit(solution)/shard_map/ppermute | solution.py:35
  13.3 2.7 %collective-permute-done.1.refs_0_ = bf16[8,5248]{1,0:T(8,128)(2,1)S(1)} collective-permute-done((bf16[8,5248]{1,0:T(8,128)(2,1)}, bf16[8,5248]{1,0:T(8,128)(2,1)S(1)}, u32[]{:S(2)}, u32[]{:S(2)}) %collective-permute-start.1) | collective-permute-done | bytes 84000 | tf_op jit(solution)/shard_map/ppermute | solution.py:35
  16.0 1.6 %collective-permute-start.4 = (bf16[24,5248]{1,0:T(8,128)(2,1)S(1)}, bf16[24,5248]{1,0:T(8,128)(2,1)S(1)}, u32[]{:S(2)}, u32[]{:S(2)}) collective-permute-start(bf16[24,5248]{1,0:T(8,128)(2,1)S(1)} %shard_map.94.order_ref), channel_id=1, source_target_pairs={{0,2},{1,3},{2,0},{3,1},{4,6},{5,7},{6,4},{7,5},{8,10},{9,11},{10,... | collective-permute-start | bytes 755720 | tf_op jit(solution)/shard_map/ppermute | solution.py:35
  17.8 4.2 %shard_map.95.order_ref.head_ref = bf16[1280,5120]{1,0:T(8,128)(2,1)S(1)} custom-call(bf16[5120,1280]{1,0:T(8,128)(2,1)S(1)} %bitcast.5, bf16[24,5248]{1,0:T(8,128)(2,1)S(1)} %shard_map.94.order_ref), custom_call_target="tpu_custom_call" | custom-call | flops 3000000000 | bytes 26214400 | tf_op jit(solution)/shard_map/pallas_call | solution.py:363
  22.0 1.8 %collective-permute-done.4 = bf16[24,5248]{1,0:T(8,128)(2,1)S(1)} collective-permute-done((bf16[24,5248]{1,0:T(8,128)(2,1)S(1)}, bf16[24,5248]{1,0:T(8,128)(2,1)S(1)}, u32[]{:S(2)}, u32[]{:S(2)}) %collective-permute-start.4) | collective-permute-done | bytes 251936 | tf_op jit(solution)/shard_map/ppermute | solution.py:35
  23.9 1.4 %collective-permute-done.6 = bf16[24,5248]{1,0:T(8,128)(2,1)S(1)} collective-permute-done((bf16[24,5248]{1,0:T(8,128)(2,1)S(1)}, bf16[24,5248]{1,0:T(8,128)(2,1)S(1)}, u32[]{:S(2)}, u32[]{:S(2)}) %collective-permute-start.6) | collective-permute-done | bytes 251936 | tf_op jit(solution)/shard_map/ppermute | solution.py:35
  25.4 2.3 %shard_map.96 = (f32[128,1280]{1,0:T(8,128)S(1)}, f32[8,128]{1,0:T(8,128)S(1)}) custom-call(f32[1]{0:T(128)S(6)} %copy.24.divisor_ref, bf16[128,5248]{1,0:T(8,128)(2,1)S(1)} %constant_dynamic-update-slice_fusion.rows_ref, bf16[5120,1280]{1,0:T(8,128)(2,1)S(1)} %bitcast.5, bf16[1280,5120]{1,0:T(8,128)(2,1)S(1)} %shard_map.95.order_ref.head_ref), custom_call_target="tpu_custom_call" | custom-call | flops 1677721600 | bytes 13107200 | tf_op jit(solution)/shard_map/pallas_call | solution.py:372
  27.7 2.2 %collective-permute-start.8 = (f32[8,128]{1,0:T(8,128)S(1)}, f32[8,128]{1,0:T(8,128)S(1)}, u32[]{:S(2)}, u32[]{:S(2)}) collective-permute-start(f32[8,128]{1,0:T(8,128)S(1)} %get-tuple-element.13), channel_id=1, source_target_pairs={{0,8},{1,9},{2,10},{3,11},{4,12},{5,13},{6,14},{7,15},{8,0},{9,1},... | collective-permute-start | bytes 12296 | tf_op jit(solution)/shard_map/ppermute | solution.py:35
  29.9 2.2 %collective-permute-start.7 = (f32[8,128]{1,0:T(8,128)S(1)}, f32[8,128]{1,0:T(8,128)S(1)}, u32[]{:S(2)}, u32[]{:S(2)}) collective-permute-start(f32[8,128]{1,0:T(8,128)S(1)} %get-tuple-element.13), channel_id=1, source_target_pairs={{0,12},{1,13},{2,14},{3,15},{4,8},{5,9},{6,10},{7,11},{8,4},{9,5},... | collective-permute-start | bytes 12296 | tf_op jit(solution)/shard_map/ppermute | solution.py:35
  32.1 3.2 %collective-permute-done.7 = f32[8,128]{1,0:T(8,128)S(1)} collective-permute-done((f32[8,128]{1,0:T(8,128)S(1)}, f32[8,128]{1,0:T(8,128)S(1)}, u32[]{:S(2)}, u32[]{:S(2)}) %collective-permute-start.7) | collective-permute-done | bytes 4128 | tf_op jit(solution)/shard_map/ppermute | solution.py:35
  35.4 1.6 %collective-permute-start.12 = (f32[32,128]{1,0:T(8,128)S(1)}, f32[32,128]{1,0:T(8,128)S(1)}, u32[]{:S(2)}, u32[]{:S(2)}) collective-permute-start(f32[32,128]{1,0:T(8,128)S(1)} %get-tuple-element.27), channel_id=1, source_target_pairs={{0,1},{1,0},{2,3},{3,2},{4,5},{5,4},{6,7},{7,6},{8,9},{9,8},{10,11... | collective-permute-start | bytes 49160 | tf_op jit(solution)/shard_map/ppermute | solution.py:35
  38.7 2.1 %collective-permute-done.11 = f32[32,128]{1,0:T(8,128)S(1)} collective-permute-done((f32[32,128]{1,0:T(8,128)S(1)}, f32[32,128]{1,0:T(8,128)S(1)}, u32[]{:S(2)}, u32[]{:S(2)}) %collective-permute-start.11) | collective-permute-done | bytes 16416 | tf_op jit(solution)/shard_map/ppermute | solution.py:35
  40.8 2.4 %shard_map.97 = (f32[8,128]{1,0:T(8,128)S(1)}, bf16[8,1280]{1,0:T(8,128)(2,1)S(1)}, f32[64,5120]{1,0:T(8,128)S(1)}, bf16[72,5120]{1,0:T(8,128)(2,1)S(1)}) custom-call(f32[1]{0:T(128)S(6)} %copy.24.divisor_ref, f32[128,128]{1,0:T(8,128)S(1)} %constant_dynamic-update-slice_fusion.10.tiles_ref, ...), custom_call_target="tpu_custom_call" | custom-call | flops 1677721600 | bytes 13107200 | tf_op jit(solution)/shard_map/pallas_call | solution.py:382
  43.3 2.2 %collective-permute-done.13.twin_ref = bf16[72,5120]{1,0:T(8,128)(2,1)S(1)} collective-permute-done((bf16[72,5120]{1,0:T(8,128)(2,1)S(1)}, bf16[72,5120]{1,0:T(8,128)(2,1)S(1)}, u32[]{:S(2)}, u32[]{:S(2)}) %collective-permute-start.13) | collective-permute-done | bytes 737312 | tf_op jit(solution)/shard_map/ppermute | solution.py:35
  46.3 2.3 %collective-permute-start.21 = (f32[1,5120]{1,0:T(1,128)S(1)}, f32[1,5120]{1,0:T(1,128)S(1)}, u32[]{:S(2)}, u32[]{:S(2)}) collective-permute-start(f32[1,5120]{1,0:T(1,128)S(1)} %get-tuple-element.20.own_ref), channel_id=1, source_target_pairs={{0,12},{1,13},{2,14},{3,15},{4,8},{5,9},{6,10},{7,11},{8,4},{9,5},... | collective-permute-start | bytes 61448 | tf_op jit(solution)/shard_map/ppermute | solution.py:35
  48.6 2.2 %collective-permute-start.19 = (f32[1,5120]{1,0:T(1,128)S(1)}, f32[1,5120]{1,0:T(1,128)S(1)}, u32[]{:S(2)}, u32[]{:S(2)}) collective-permute-start(f32[1,5120]{1,0:T(1,128)S(1)} %get-tuple-element.20.own_ref), channel_id=1, source_target_pairs={{0,4},{1,5},{2,6},{3,7},{4,0},{5,1},{6,2},{7,3},{8,12},{9,13},{10,... | collective-permute-start | bytes 61448 | tf_op jit(solution)/shard_map/ppermute | solution.py:35
  50.8 1.5 %collective-permute-start.14 = (bf16[8,5120]{1,0:T(8,128)(2,1)S(1)}, bf16[8,5120]{1,0:T(8,128)(2,1)S(1)}, u32[]{:S(2)}, u32[]{:S(2)}) collective-permute-start(bf16[8,5120]{1,0:T(8,128)(2,1)S(1)} %get-tuple-element.19), channel_id=1, source_target_pairs={{0,2},{1,3},{2,0},{3,1},{4,6},{5,7},{6,4},{7,5},{8,10},{9,11},{10,... | collective-permute-start | bytes 245768 | tf_op jit(solution)/shard_map/ppermute | solution.py:35
  52.3 2.2 %collective-permute-done.15.order_ref = bf16[24,5120]{1,0:T(8,128)(2,1)S(1)} collective-permute-done((bf16[24,5120]{1,0:T(8,128)(2,1)S(1)}, bf16[24,5120]{1,0:T(8,128)(2,1)S(1)}, u32[]{:S(2)}, u32[]{:S(2)}) %collective-permute-start.15) | collective-permute-done | bytes 245792 | tf_op jit(solution)/shard_map/ppermute | solution.py:35
  57.5 1.7 %collective-permute-start.16 = (bf16[8,5120]{1,0:T(8,128)(2,1)S(1)}, bf16[8,5120]{1,0:T(8,128)(2,1)S(1)}, u32[]{:S(2)}, u32[]{:S(2)}) collective-permute-start(bf16[8,5120]{1,0:T(8,128)(2,1)S(1)} %get-tuple-element.24), channel_id=1, source_target_pairs={{0,12},{1,13},{2,14},{3,15},{4,8},{5,9},{6,10},{7,11},{8,4},{9,5},... | collective-permute-start | bytes 245768 | tf_op jit(solution)/shard_map/ppermute | solution.py:35
  60.5 3.3 %collective-permute-done.17.refs_2_ = bf16[8,5120]{1,0:T(8,128)(2,1)S(1)} collective-permute-done((bf16[8,5120]{1,0:T(8,128)(2,1)S(1)}, bf16[8,5120]{1,0:T(8,128)(2,1)S(1)}, u32[]{:S(2)}, u32[]{:S(2)}) %collective-permute-start.17) | collective-permute-done | bytes 81952 | tf_op jit(solution)/shard_map/ppermute | solution.py:35
  (64 shorter events, 9.1 us)
Async XLA Ops:
  2.3 9.0 %collective-permute-start.3 = (bf16[8,5248]{1,0:T(8,128)(2,1)}, bf16[8,5248]{1,0:T(8,128)(2,1)S(1)}, u32[]{:S(2)}, u32[]{:S(2)}) collective-permute-start(bf16[8,5248]{1,0:T(8,128)(2,1)} %shard_map.93), channel_id=1, source_target_pairs={{0,4},{1,5},{2,6},{3,7},{4,0},{5,1},{6,2},{7,3},{8,12},{9,13},{10,... | collective-permute-start | bytes 251912 | tf_op jit(solution)/shard_map/ppermute | solution.py:35
  5.4 7.9 %collective-permute-start.2 = (bf16[8,5248]{1,0:T(8,128)(2,1)}, bf16[8,5248]{1,0:T(8,128)(2,1)S(1)}, u32[]{:S(2)}, u32[]{:S(2)}) collective-permute-start(bf16[8,5248]{1,0:T(8,128)(2,1)} %shard_map.93), channel_id=1, source_target_pairs={{0,12},{1,13},{2,14},{3,15},{4,8},{5,9},{6,10},{7,11},{8,4},{9,5},... | collective-permute-start | bytes 251912 | tf_op jit(solution)/shard_map/ppermute | solution.py:35
  7.9 8.1 %collective-permute-start.1 = (bf16[8,5248]{1,0:T(8,128)(2,1)}, bf16[8,5248]{1,0:T(8,128)(2,1)S(1)}, u32[]{:S(2)}, u32[]{:S(2)}) collective-permute-start(bf16[8,5248]{1,0:T(8,128)(2,1)} %shard_map.93), channel_id=1, source_target_pairs={{0,8},{1,9},{2,10},{3,11},{4,12},{5,13},{6,14},{7,15},{8,0},{9,1},... | collective-permute-start | bytes 251912 | tf_op jit(solution)/shard_map/ppermute | solution.py:35
  8.0 9.5 %collective-permute-start = (bf16[8,5248]{1,0:T(8,128)(2,1)}, bf16[8,5248]{1,0:T(8,128)(2,1)S(1)}, u32[]{:S(2)}, u32[]{:S(2)}) collective-permute-start(bf16[8,5248]{1,0:T(8,128)(2,1)} %shard_map.93), channel_id=1, source_target_pairs={{0,2},{1,3},{2,0},{3,1},{4,6},{5,7},{6,4},{7,5},{8,10},{9,11},{10,... | collective-permute-start | bytes 251912 | tf_op jit(solution)/shard_map/ppermute | solution.py:35
  16.0 7.8 %collective-permute-start.4 = (bf16[24,5248]{1,0:T(8,128)(2,1)S(1)}, bf16[24,5248]{1,0:T(8,128)(2,1)S(1)}, u32[]{:S(2)}, u32[]{:S(2)}) collective-permute-start(bf16[24,5248]{1,0:T(8,128)(2,1)S(1)} %shard_map.94.order_ref), channel_id=1, source_target_pairs={{0,2},{1,3},{2,0},{3,1},{4,6},{5,7},{6,4},{7,5},{8,10},{9,11},{10,... | collective-permute-start | bytes 755720 | tf_op jit(solution)/shard_map/ppermute | solution.py:35
  17.6 6.2 %collective-permute-start.5 = (bf16[40,5248]{1,0:T(8,128)(2,1)S(1)}, bf16[40,5248]{1,0:T(8,128)(2,1)S(1)}, u32[]{:S(2)}, u32[]{:S(2)}) collective-permute-start(bf16[40,5248]{1,0:T(8,128)(2,1)S(1)} %pad_maximum_fusion), channel_id=1, source_target_pairs={{0,1},{1,0},{2,3},{3,2},{4,5},{5,4},{6,7},{7,6},{8,9},{9,8},{10,11... | collective-permute-start | bytes 1259528 | tf_op jit(solution)/shard_map/ppermute | solution.py:35
  23.8 1.5 %collective-permute-start.6 = (bf16[24,5248]{1,0:T(8,128)(2,1)S(1)}, bf16[24,5248]{1,0:T(8,128)(2,1)S(1)}, u32[]{:S(2)}, u32[]{:S(2)}) collective-permute-start(bf16[24,5248]{1,0:T(8,128)(2,1)S(1)} %collective-permute-done.4), channel_id=1, source_target_pairs={{0,1},{1,0},{2,3},{3,2},{4,5},{5,4},{6,7},{7,6},{8,9},{9,8},{10,11... | collective-permute-start | bytes 755720 | tf_op jit(solution)/shard_map/ppermute | solution.py:35
  27.7 7.6 %collective-permute-start.9 = (f32[8,128]{1,0:T(8,128)S(1)}, f32[8,128]{1,0:T(8,128)S(1)}, u32[]{:S(2)}, u32[]{:S(2)}) collective-permute-start(f32[8,128]{1,0:T(8,128)S(1)} %get-tuple-element.13), channel_id=1, source_target_pairs={{0,4},{1,5},{2,6},{3,7},{4,0},{5,1},{6,2},{7,3},{8,12},{9,13},{10,... | collective-permute-start | bytes 12296 | tf_op jit(solution)/shard_map/ppermute | solution.py:35
  27.7 7.6 %collective-permute-start.8 = (f32[8,128]{1,0:T(8,128)S(1)}, f32[8,128]{1,0:T(8,128)S(1)}, u32[]{:S(2)}, u32[]{:S(2)}) collective-permute-start(f32[8,128]{1,0:T(8,128)S(1)} %get-tuple-element.13), channel_id=1, source_target_pairs={{0,8},{1,9},{2,10},{3,11},{4,12},{5,13},{6,14},{7,15},{8,0},{9,1},... | collective-permute-start | bytes 12296 | tf_op jit(solution)/shard_map/ppermute | solution.py:35
  29.9 5.4 %collective-permute-start.7 = (f32[8,128]{1,0:T(8,128)S(1)}, f32[8,128]{1,0:T(8,128)S(1)}, u32[]{:S(2)}, u32[]{:S(2)}) collective-permute-start(f32[8,128]{1,0:T(8,128)S(1)} %get-tuple-element.13), channel_id=1, source_target_pairs={{0,12},{1,13},{2,14},{3,15},{4,8},{5,9},{6,10},{7,11},{8,4},{9,5},... | collective-permute-start | bytes 12296 | tf_op jit(solution)/shard_map/ppermute | solution.py:35
  35.4 3.3 %collective-permute-start.10 = (f32[32,128]{1,0:T(8,128)S(1)}, f32[32,128]{1,0:T(8,128)S(1)}, u32[]{:S(2)}, u32[]{:S(2)}) collective-permute-start(f32[32,128]{1,0:T(8,128)S(1)} %get-tuple-element.27), channel_id=1, source_target_pairs={{0,3},{1,2},{2,1},{3,0},{4,7},{5,6},{6,5},{7,4},{8,11},{9,10},{10,... | collective-permute-start | bytes 49160 | tf_op jit(solution)/shard_map/ppermute | solution.py:35
  35.4 5.4 %collective-permute-start.12 = (f32[32,128]{1,0:T(8,128)S(1)}, f32[32,128]{1,0:T(8,128)S(1)}, u32[]{:S(2)}, u32[]{:S(2)}) collective-permute-start(f32[32,128]{1,0:T(8,128)S(1)} %get-tuple-element.27), channel_id=1, source_target_pairs={{0,1},{1,0},{2,3},{3,2},{4,5},{5,4},{6,7},{7,6},{8,9},{9,8},{10,11... | collective-permute-start | bytes 49160 | tf_op jit(solution)/shard_map/ppermute | solution.py:35
  37.1 3.7 %collective-permute-start.11 = (f32[32,128]{1,0:T(8,128)S(1)}, f32[32,128]{1,0:T(8,128)S(1)}, u32[]{:S(2)}, u32[]{:S(2)}) collective-permute-start(f32[32,128]{1,0:T(8,128)S(1)} %get-tuple-element.27), channel_id=1, source_target_pairs={{0,2},{1,3},{2,0},{3,1},{4,6},{5,7},{6,4},{7,5},{8,10},{9,11},{10,... | collective-permute-start | bytes 49160 | tf_op jit(solution)/shard_map/ppermute | solution.py:35
  43.3 2.3 %collective-permute-start.13 = (bf16[72,5120]{1,0:T(8,128)(2,1)S(1)}, bf16[72,5120]{1,0:T(8,128)(2,1)S(1)}, u32[]{:S(2)}, u32[]{:S(2)}) collective-permute-start(bf16[72,5120]{1,0:T(8,128)(2,1)S(1)} %get-tuple-element.16), channel_id=1, source_target_pairs={{0,1},{1,0},{2,3},{3,2},{4,5},{5,4},{6,7},{7,6},{8,9},{9,8},{10,11... | collective-permute-start | bytes 2211848 | tf_op jit(solution)/shard_map/ppermute | solution.py:35
  45.6 8.9 %collective-permute-start.15 = (bf16[24,5120]{1,0:T(8,128)(2,1)S(1)}, bf16[24,5120]{1,0:T(8,128)(2,1)S(1)}, u32[]{:S(2)}, u32[]{:S(2)}) collective-permute-start(bf16[24,5120]{1,0:T(8,128)(2,1)S(1)} %shard_map.98.order_ref), channel_id=1, source_target_pairs={{0,2},{1,3},{2,0},{3,1},{4,6},{5,7},{6,4},{7,5},{8,10},{9,11},{10,... | collective-permute-start | bytes 737288 | tf_op jit(solution)/shard_map/ppermute | solution.py:35
  46.3 17.5 %copy-start = (bf16[8,5120]{1,0:T(8,128)(2,1)S(1)}, bf16[8,5120]{1,0:T(8,128)(2,1)}, u32[]{:S(2)}) copy-start(bf16[8,5120]{1,0:T(8,128)(2,1)} %rows_ref.1) | copy-start | bytes 245764
  46.3 8.3 %collective-permute-start.21 = (f32[1,5120]{1,0:T(1,128)S(1)}, f32[1,5120]{1,0:T(1,128)S(1)}, u32[]{:S(2)}, u32[]{:S(2)}) collective-permute-start(f32[1,5120]{1,0:T(1,128)S(1)} %get-tuple-element.20.own_ref), channel_id=1, source_target_pairs={{0,12},{1,13},{2,14},{3,15},{4,8},{5,9},{6,10},{7,11},{8,4},{9,5},... | collective-permute-start | bytes 61448 | tf_op jit(solution)/shard_map/ppermute | solution.py:35
  48.6 6.0 %collective-permute-start.20 = (f32[1,5120]{1,0:T(1,128)S(1)}, f32[1,5120]{1,0:T(1,128)S(1)}, u32[]{:S(2)}, u32[]{:S(2)}) collective-permute-start(f32[1,5120]{1,0:T(1,128)S(1)} %get-tuple-element.20.own_ref), channel_id=1, source_target_pairs={{0,8},{1,9},{2,10},{3,11},{4,12},{5,13},{6,14},{7,15},{8,0},{9,1},... | collective-permute-start | bytes 61448 | tf_op jit(solution)/shard_map/ppermute | solution.py:35
  48.6 6.0 %collective-permute-start.19 = (f32[1,5120]{1,0:T(1,128)S(1)}, f32[1,5120]{1,0:T(1,128)S(1)}, u32[]{:S(2)}, u32[]{:S(2)}) collective-permute-start(f32[1,5120]{1,0:T(1,128)S(1)} %get-tuple-element.20.own_ref), channel_id=1, source_target_pairs={{0,4},{1,5},{2,6},{3,7},{4,0},{5,1},{6,2},{7,3},{8,12},{9,13},{10,... | collective-permute-start | bytes 61448 | tf_op jit(solution)/shard_map/ppermute | solution.py:35
  50.8 9.7 %collective-permute-start.14 = (bf16[8,5120]{1,0:T(8,128)(2,1)S(1)}, bf16[8,5120]{1,0:T(8,128)(2,1)S(1)}, u32[]{:S(2)}, u32[]{:S(2)}) collective-permute-start(bf16[8,5120]{1,0:T(8,128)(2,1)S(1)} %get-tuple-element.19), channel_id=1, source_target_pairs={{0,2},{1,3},{2,0},{3,1},{4,6},{5,7},{6,4},{7,5},{8,10},{9,11},{10,... | collective-permute-start | bytes 245768 | tf_op jit(solution)/shard_map/ppermute | solution.py:35
  54.6 5.2 %collective-permute-start.22 = (f32[1,5120]{1,0:T(1,128)S(1)}, f32[1,5120]{1,0:T(1,128)S(1)}, u32[]{:S(2)}, u32[]{:S(2)}) collective-permute-start(f32[1,5120]{1,0:T(1,128)S(1)} %shard_map.101), channel_id=1, source_target_pairs={{0,2},{1,3},{2,0},{3,1},{4,6},{5,7},{6,4},{7,5},{8,10},{9,11},{10,... | collective-permute-start | bytes 61448 | tf_op jit(solution)/shard_map/ppermute | solution.py:35
  54.9 5.6 %collective-permute-start.18 = (bf16[8,5120]{1,0:T(8,128)(2,1)S(1)}, bf16[8,5120]{1,0:T(8,128)(2,1)S(1)}, u32[]{:S(2)}, u32[]{:S(2)}) collective-permute-start(bf16[8,5120]{1,0:T(8,128)(2,1)S(1)} %get-tuple-element.22), channel_id=1, source_target_pairs={{0,4},{1,5},{2,6},{3,7},{4,0},{5,1},{6,2},{7,3},{8,12},{9,13},{10,... | collective-permute-start | bytes 245768 | tf_op jit(solution)/shard_map/ppermute | solution.py:35
  56.1 7.7 %collective-permute-start.17 = (bf16[8,5120]{1,0:T(8,128)(2,1)S(1)}, bf16[8,5120]{1,0:T(8,128)(2,1)S(1)}, u32[]{:S(2)}, u32[]{:S(2)}) collective-permute-start(bf16[8,5120]{1,0:T(8,128)(2,1)S(1)} %get-tuple-element.23), channel_id=1, source_target_pairs={{0,8},{1,9},{2,10},{3,11},{4,12},{5,13},{6,14},{7,15},{8,0},{9,1},... | collective-permute-start | bytes 245768 | tf_op jit(solution)/shard_map/ppermute | solution.py:35
  57.5 6.3 %collective-permute-start.16 = (bf16[8,5120]{1,0:T(8,128)(2,1)S(1)}, bf16[8,5120]{1,0:T(8,128)(2,1)S(1)}, u32[]{:S(2)}, u32[]{:S(2)}) collective-permute-start(bf16[8,5120]{1,0:T(8,128)(2,1)S(1)} %get-tuple-element.24), channel_id=1, source_target_pairs={{0,12},{1,13},{2,14},{3,15},{4,8},{5,9},{6,10},{7,11},{8,4},{9,5},... | collective-permute-start | bytes 245768 | tf_op jit(solution)/shard_map/ppermute | solution.py:35
  (6 other events, 48.4 us)

commit v4 on v3

--- a/solution.py
+++ b/solution.py
@@ -34,38 +34,41 @@
     def swap(self, value, m):
         return lax.ppermute(value, "vocab", [(i, i ^ m) for i in range(self.count)])
 
-    def gather(self, own):
+    def gather(self, own, meanwhile):
         swap = self.swap
         if self.count == 16:
-            far, diagonal, near, side = swap(own, 8), swap(own, 12), swap(own, 4), swap(own, 2)
-            column = stack_blocks(far, diagonal, near)
-            across = swap(column, 2)
-            twin = swap(cat(own, side, column), 1)
-            twin_across = swap(across, 1)
-            return cat(own, side, column, across, twin, twin_across), column
-        blocks = own
+            far, near, side = swap(own, 8), swap(own, 4), swap(own, 2)
+            across = stack_blocks([far, near], flops=STACK_FLOPS)
+            crossed = swap(across, 2)
+            beyond, diagonal = swap(side, 12), swap(far, 4)
+            result = meanwhile(across)
+            chips = stack_blocks([own, side, far, near, beyond, diagonal, crossed], after=result)
+            return cat(chips, swap(chips, 1)), result
+        blocks, result = own, meanwhile(own)
         for m in reversed(bits_of(self.count)):
             blocks = cat(blocks, swap(blocks, m))
-        return blocks, own
+        return blocks, result
 
     def codes(self):
         if self.count == 16:
-            first = [0, 2, 8, 12, 4, 10, 14, 6]
+            first = [0, 2, 8, 4, 14, 12, 10, 6]
             return first + [c ^ 1 for c in first]
         codes = [0]
         for m in reversed(bits_of(self.count)):
             codes = codes + [c ^ m for c in codes]
         return codes
 
-    def gather_small(self, own):
+    def gather_small(self, own, meanwhile):
         swap = self.swap
+        result = meanwhile(own)
         if self.count == 16:
-            column = cat(own, swap(own, 12), swap(own, 8), swap(own, 4))
-            return cat(column, swap(column, 3), swap(column, 2), swap(column, 1))
+            far = [swap(own, m) for m in (12, 8, 4)]
+            column = stack_blocks([own] + far, after=result)
+            return cat(column, swap(column, 3), swap(column, 2), swap(column, 1)), result
         tiles = own
         for m in bits_of(self.count):
             tiles = cat(tiles, swap(tiles, m))
-        return tiles
+        return tiles, result
 
     def small_place(self, code):
         if self.count == 16:
@@ -80,7 +83,7 @@
 SMEM, VMEM, HBM = spec(pltpu.SMEM), spec(), spec(pltpu.HBM)
 
 
-def call(kernel, outs, ins, scratch=(), flops=0, moved=0, limit=24):
+def call(kernel, outs, ins, scratch=(), flops=0, moved=0, limit=20):
     return pl.pallas_call(
         kernel,
         out_shape=outs,
@@ -127,19 +130,20 @@
     out_ref[:, width:] = notes.astype(f32).astype(bf16)
 
 
-def stack_kernel(*refs):
-    ins, out_ref = refs[:-1], refs[-1]
-    out_ref[...] = cat(*[ref[...].astype(f32) for ref in ins]).astype(out_ref.dtype)
-
-
-def stack_blocks(*blocks):
-    rows, width = blocks[0].shape
+def stack_kernel(count, *refs):
+    refs[-1][...] = cat(*[ref[...].astype(f32) for ref in refs[:count]]).astype(refs[-1].dtype)
+
+
+def stack_blocks(blocks, after=None, flops=0):
+    rows = sum(block.shape[0] for block in blocks)
+    more = [] if after is None else [after]
     return call(
-        stack_kernel,
-        shaped((len(blocks) * rows, width), bf16),
-        [VMEM] * len(blocks),
-        flops=STACK_FLOPS,
-    )(*blocks)
+        functools.partial(stack_kernel, len(blocks)),
+        shaped((rows, blocks[0].shape[1]), blocks[0].dtype),
+        [VMEM] * len(blocks) + [spec(pl.ANY)] * len(more),
+        flops=flops,
+        limit=8,
+    )(*blocks, *more)
 
 
 def fold(row):
@@ -157,14 +161,15 @@
     return parts[:, :c] + parts[:, c:]
 
 
-def turn_kernel(head_ref, order_ref, out_ref):
+def turn_kernel(part, head_ref, order_ref, out_ref):
     step = 512
     width = head_ref.shape[0]
+    rows = out_ref.shape[0]
 
     @pl.loop(0, width // step)
     def _(n):
         here = pl.ds(pl.multiple_of(n * step, step), step)
-        out_ref[:, here] = head_ref[here, :].T
+        out_ref[:, here] = head_ref[here, part * rows : (part + 1) * rows].T
 
 
 def read_notes(noted):
@@ -223,6 +228,7 @@
     rows_ref,
     scaled_ref,
     head_ref,
+    head2_ref,
     gain_ref,
     scalars_ref,
     parts_ref,
@@ -233,7 +239,8 @@
 ):
     me = lax.axis_index("vocab")
     count = len(codes)
-    slab_width, width = head_ref.shape
+    width = head_ref.shape[1]
+    cut, slab_width = head_ref.shape[0], 2 * head_ref.shape[0]
     token_count = rows_ref.shape[0]
     own_count = token_count // count
     half = token_count // 2
@@ -274,7 +281,9 @@
         owned = owned_mask(labels, me, slab_width).astype(f32)
         shares = jnp.exp(scaled_ref[band, :] - w[:, 0:1]) / w[:, 1:2]
         coefs[band, :] = (w[:, 2:3] * (shares - owned)).astype(bf16)
-    out = jnp.dot(coefs[...], head_ref[...], preferred_element_type=f32)
+    out = jnp.dot(coefs[:, :cut], head_ref[...], preferred_element_type=f32) + jnp.dot(
+        coefs[:, cut:], head2_ref[...], preferred_element_type=f32
+    )
     kept_ref[...] = out[:half]
     sent_ref[:half, :] = out[half:].astype(bf16)
     gain_grad = (
@@ -359,15 +368,17 @@
         ],
         limit=63,
     )(correct_label_ids, included_place_flags, backbone_feature_matrix, gain)
-    rows, early = links.gather(own)
-    head_t = call(
-        turn_kernel,
-        shaped((slab_width, width), bf16),
-        [VMEM, spec(pl.ANY)],
-        flops=TURN_FLOPS,
-        moved=2 * head_bytes,
-        limit=4,
-    )(output_vocab_matrix, early)
+    def turn(order, part):
+        return call(
+            functools.partial(turn_kernel, part),
+            shaped((slab_width // 2, width), bf16),
+            [VMEM, spec(pl.ANY)],
+            flops=TURN_FLOPS,
+            moved=head_bytes,
+            limit=4,
+        )(output_vocab_matrix, order)
+
+    rows, left = links.gather(own, lambda order: turn(order, 0))
 
     scaled, stats = call(
         functools.partial(logits_kernel, codes),
@@ -376,8 +387,8 @@
         [pltpu.VMEM((count, own_count, LANES), f32)],
         flops=product,
         moved=head_bytes,
-    )(softness_divisor, rows, output_vocab_matrix, head_t)
-    tiles = links.gather_small(stats)
+    )(softness_divisor, rows, output_vocab_matrix, left)
+    tiles, right = links.gather_small(stats, lambda order: turn(order, 1))
     parts_shape = (8, width // 4)
     scalars, parts, kept, sent = call(
         functools.partial(slab_kernel, codes, links.small_place),
@@ -387,21 +398,21 @@
             shaped((half, width), f32),
             shaped((half + 8, width), bf16),
         ),
-        [SMEM] + [VMEM] * 5,
+        [SMEM] + [VMEM] * 6,
         [
             pltpu.VMEM((count, own_count, LANES), f32),
             pltpu.VMEM((token_count, slab_width), bf16),
         ],
         flops=product,
         moved=head_bytes,
-        limit=32,
-    )(softness_divisor, tiles, rows, scaled, head_t, gain)
+        limit=28,
+    )(softness_divisor, tiles, rows, scaled, left, right, gain)
     twin = swap(sent, 1)
 
     b = own_count
     if count == 16:
-        going_order = (7, 5, 6)
-        rest_order = ((0, 4, 2, 3), (1,))
+        going_order = (7, 6, 4)
+        rest_order = ((0, 3, 2, 5), (1,))
         sizes = [(4, f32), (1, bf16)]
     else:
         quarter = count // 4

time: 64.9 us -> 62.4 us (0.961)
  waiting for transfers between devices: 22.1 us -> 15.7 us
  starting transfers between devices: 26.7 us -> 30.9 us
  local copies, waits for them, and re-layouts: 1.7 us -> 0.91 us
    ppermute x23, waiting for transfers between devices: 22.1 us -> 15.7 us  [swap(): return lax.ppermute(value, 'vocab', [(i, i ^ m) for i in range(self.count)])]
    ppermute x23, starting transfers between devices: 26.7 us -> 30.9 us  [swap(): return lax.ppermute(value, 'vocab', [(i, i ^ m) for i in range(self.count)])]
    unnamed x24 -> x8, local copies, waits for them, and re-layouts: 1.07 us -> 0.31 us
    pallas_call x2 -> x5, Pallas kernels: 4.23 us -> 4.74 us  [the longest x2 4.68 us: turn(): call(functools.partial(turn_kernel, part), shaped((slab_width // 2, width...]
  transfers between devices with their start and end apart: 23 -> 23, of which waited for: 10 -> 9; matrix products, arithmetic and copies ran while one was open for 4% -> 2% of each run, Pallas kernels for 7% -> 8%
where the time goes in v4:
time: 62.4 us; the launch traced here: 62.2 us
  starting transfers between devices  30.9 us (50%)
  waiting for transfers between devices  15.7 us (25%)
  Pallas kernels  12.4 us (20%)
  between operations  1.46 us (2%)
  local copies, waits for them, and re-layouts  0.91 us (1%)
  other arithmetic  0.77 us (1%)
    ppermute x23, starting transfers between devices, swap(): return lax.ppermute(value, 'vocab', [(i, i ^ m) for i in range(self.count)])  30.9 us
    ppermute x23, waiting for transfers between devices, swap(): return lax.ppermute(value, 'vocab', [(i, i ^ m) for i in range(self.count)])  15.7 us
    pallas_call x2, Pallas kernels, turn(): call(functools.partial(turn_kernel, part), shaped((slab_width // 2, width...  4.68 us
    pallas_call x1, Pallas kernels, on_device(): call(functools.partial(slab_kernel, codes, links.small_place), (shaped((8...  2.73 us
    pallas_call x1, Pallas kernels, on_device(): call(functools.partial(logits_kernel, codes), (shaped((token_count, slab_...  2.19 us
    pallas_call x1, Pallas kernels, on_device(): call(norm_kernel, shaped((own_count, width + LANES), bf16), [HBM] * 4, [p...  1.73 us
  transfers between devices with their start and end apart: 23, of which 9 were waited for; matrix products, arithmetic and copies ran while one was open for 2% of the time, Pallas kernels for 8%

profile of v4, /device:TPU:0, one launch (start us, length us, event | category | flops | bytes accessed | tf_op | source)
XLA Modules:
  0.0 62.2 jit_solution(11722096838580468506)
XLA Ops:
  0.6 1.7 %shard_map.93.refs_0_ = bf16[8,5248]{1,0:T(8,128)(2,1)} custom-call(s32[8]{0:T(128)} %ids_hbm.1, s32[8]{0:T(128)} %flags_hbm.1, bf16[8,5120]{1,0:T(8,128)(2,1)} %rows_ref.1, f32[1,5120]{1,0:T(1,128)} %bitcast.4), custom_call_target="tpu_custom_call" | custom-call | tf_op jit(solution)/shard_map/pallas_call | solution.py:358
  2.4 3.1 %collective-permute-start.2 = (bf16[8,5248]{1,0:T(8,128)(2,1)}, bf16[8,5248]{1,0:T(8,128)(2,1)S(1)}, u32[]{:S(2)}, u32[]{:S(2)}) collective-permute-start(bf16[8,5248]{1,0:T(8,128)(2,1)} %shard_map.93.refs_0_), channel_id=1, source_target_pairs={{0,4},{1,5},{2,6},{3,7},{4,0},{5,1},{6,2},{7,3},{8,12},{9,13},{10,... | collective-permute-start | bytes 251912 | tf_op jit(solution)/shard_map/ppermute | solution.py:35
  5.5 2.6 %collective-permute-start.1 = (bf16[8,5248]{1,0:T(8,128)(2,1)}, bf16[8,5248]{1,0:T(8,128)(2,1)S(1)}, u32[]{:S(2)}, u32[]{:S(2)}) collective-permute-start(bf16[8,5248]{1,0:T(8,128)(2,1)} %shard_map.93.refs_0_), channel_id=1, source_target_pairs={{0,8},{1,9},{2,10},{3,11},{4,12},{5,13},{6,14},{7,15},{8,0},{9,1},... | collective-permute-start | bytes 251912 | tf_op jit(solution)/shard_map/ppermute | solution.py:35
  8.0 1.5 %collective-permute-start = (bf16[8,5248]{1,0:T(8,128)(2,1)}, bf16[8,5248]{1,0:T(8,128)(2,1)S(1)}, u32[]{:S(2)}, u32[]{:S(2)}) collective-permute-start(bf16[8,5248]{1,0:T(8,128)(2,1)} %shard_map.93.refs_0_), channel_id=1, source_target_pairs={{0,2},{1,3},{2,0},{3,1},{4,6},{5,7},{6,4},{7,5},{8,10},{9,11},{10,... | collective-permute-start | bytes 251912 | tf_op jit(solution)/shard_map/ppermute | solution.py:35
  9.6 2.8 %collective-permute-done.1.refs_0_.refs_2_ = bf16[8,5248]{1,0:T(8,128)(2,1)S(1)} collective-permute-done((bf16[8,5248]{1,0:T(8,128)(2,1)}, bf16[8,5248]{1,0:T(8,128)(2,1)S(1)}, u32[]{:S(2)}, u32[]{:S(2)}) %collective-permute-start.1) | collective-permute-done | bytes 84000 | tf_op jit(solution)/shard_map/ppermute | solution.py:35
  12.4 1.6 %collective-permute-start.5 = (bf16[16,5248]{1,0:T(8,128)(2,1)S(1)}, bf16[16,5248]{1,0:T(8,128)(2,1)S(1)}, u32[]{:S(2)}, u32[]{:S(2)}) collective-permute-start(bf16[16,5248]{1,0:T(8,128)(2,1)S(1)} %shard_map.94.order_ref), channel_id=1, source_target_pairs={{0,2},{1,3},{2,0},{3,1},{4,6},{5,7},{6,4},{7,5},{8,10},{9,11},{10,... | collective-permute-start | bytes 503816 | tf_op jit(solution)/shard_map/ppermute | solution.py:35
  14.3 2.5 %collective-permute-start.3 = (bf16[8,5248]{1,0:T(8,128)(2,1)S(1)}, bf16[8,5248]{1,0:T(8,128)(2,1)S(1)}, u32[]{:S(2)}, u32[]{:S(2)}) collective-permute-start(bf16[8,5248]{1,0:T(8,128)(2,1)S(1)} %collective-permute-done.refs_1_), channel_id=1, source_target_pairs={{0,12},{1,13},{2,14},{3,15},{4,8},{5,9},{6,10},{7,11},{8,4},{9,5},... | collective-permute-start | bytes 251912 | tf_op jit(solution)/shard_map/ppermute | solution.py:35
  17.1 2.3 %shard_map.95.refs_7_.order_ref.head_ref = bf16[640,5120]{1,0:T(8,128)(2,1)S(1)} custom-call(bf16[5120,1280]{1,0:T(8,128)(2,1)S(1)} %copy-done, bf16[16,5248]{1,0:T(8,128)(2,1)S(1)} %shard_map.94.order_ref), custom_call_target="tpu_custom_call" | custom-call | flops 3000000000 | bytes 13107200 | tf_op jit(solution)/shard_map/pallas_call | solution.py:372
  21.5 1.5 %collective-permute-done.6 = bf16[64,5248]{1,0:T(8,128)(2,1)S(1)} collective-permute-done((bf16[64,5248]{1,0:T(8,128)(2,1)S(1)}, bf16[64,5248]{1,0:T(8,128)(2,1)S(1)}, u32[]{:S(2)}, u32[]{:S(2)}) %collective-permute-start.6) | collective-permute-done | bytes 671776 | tf_op jit(solution)/shard_map/ppermute | solution.py:35
  23.0 2.2 %shard_map.97 = (f32[128,1280]{1,0:T(8,128)S(1)}, f32[8,128]{1,0:T(8,128)S(1)}) custom-call(f32[1]{0:T(128)S(6)} %copy.10.divisor_ref, bf16[128,5248]{1,0:T(8,128)(2,1)S(1)} %pad_maximum_fusion.rows_ref, bf16[5120,1280]{1,0:T(8,128)(2,1)S(1)} %copy-done, bf16[640,5120]{1,0:T(8,128)(2,1)S(1)} %shard_map.95.refs_7_.order_ref.head_ref), custom_call_target="tpu_custom_call" | custom-call | flops 1677721600 | bytes 13107200 | tf_op jit(solution)/shard_map/pallas_call | solution.py:383
  25.9 2.4 %collective-permute-start.8 = (f32[8,128]{1,0:T(8,128)S(1)}, f32[8,128]{1,0:T(8,128)S(1)}, u32[]{:S(2)}, u32[]{:S(2)}) collective-permute-start(f32[8,128]{1,0:T(8,128)S(1)} %get-tuple-element.13.order_ref.refs_0_), channel_id=1, source_target_pairs={{0,8},{1,9},{2,10},{3,11},{4,12},{5,13},{6,14},{7,15},{8,0},{9,1},... | collective-permute-start | bytes 12296 | tf_op jit(solution)/shard_map/ppermute | solution.py:35
  29.6 2.3 %shard_map.98.refs_4_.head2_ref = bf16[640,5120]{1,0:T(8,128)(2,1)S(1)} custom-call(bf16[5120,1280]{1,0:T(8,128)(2,1)S(1)} %copy-done, f32[8,128]{1,0:T(8,128)S(1)} %get-tuple-element.13.order_ref.refs_0_), custom_call_target="tpu_custom_call" | custom-call | flops 3000000000 | bytes 13107200 | tf_op jit(solution)/shard_map/pallas_call | solution.py:372
  32.0 1.7 %collective-permute-done.7.refs_1_ = f32[8,128]{1,0:T(8,128)S(1)} collective-permute-done((f32[8,128]{1,0:T(8,128)S(1)}, f32[8,128]{1,0:T(8,128)S(1)}, u32[]{:S(2)}, u32[]{:S(2)}) %collective-permute-start.7) | collective-permute-done | bytes 4128 | tf_op jit(solution)/shard_map/ppermute | solution.py:35
  35.6 2.0 %collective-permute-done.11 = f32[32,128]{1,0:T(8,128)S(1)} collective-permute-done((f32[32,128]{1,0:T(8,128)S(1)}, f32[32,128]{1,0:T(8,128)S(1)}, u32[]{:S(2)}, u32[]{:S(2)}) %collective-permute-start.11) | collective-permute-done | bytes 16416 | tf_op jit(solution)/shard_map/ppermute | solution.py:35
  37.6 2.7 %shard_map.100 = (f32[8,128]{1,0:T(8,128)S(1)}, bf16[8,1280]{1,0:T(8,128)(2,1)S(1)}, f32[64,5120]{1,0:T(8,128)S(1)}, bf16[72,5120]{1,0:T(8,128)(2,1)S(1)}) custom-call(f32[1]{0:T(128)S(6)} %copy.10.divisor_ref, f32[128,128]{1,0:T(8,128)S(1)} %pad_maximum_fusion.1.tiles_ref, bf16[128,5248]{1,0:T(8,128)(2,1)S(1)} %pad_maximum_fusion.rows_ref, ...), custom_call_target="tpu_custom_call" | custom-call | flops 1677721600 | bytes 13107200 | tf_op jit(solution)/shard_map/pallas_call | solution.py:393
  40.5 2.1 %collective-permute-done.13.twin_ref = bf16[72,5120]{1,0:T(8,128)(2,1)S(1)} collective-permute-done((bf16[72,5120]{1,0:T(8,128)(2,1)S(1)}, bf16[72,5120]{1,0:T(8,128)(2,1)S(1)}, u32[]{:S(2)}, u32[]{:S(2)}) %collective-permute-start.13) | collective-permute-done | bytes 737312 | tf_op jit(solution)/shard_map/ppermute | solution.py:35
  42.6 1.4 %collective-permute-start.15 = (bf16[24,5120]{1,0:T(8,128)(2,1)S(1)}, bf16[24,5120]{1,0:T(8,128)(2,1)S(1)}, u32[]{:S(2)}, u32[]{:S(2)}) collective-permute-start(bf16[24,5120]{1,0:T(8,128)(2,1)S(1)} %shard_map.101.order_ref), channel_id=1, source_target_pairs={{0,2},{1,3},{2,0},{3,1},{4,6},{5,7},{6,4},{7,5},{8,10},{9,11},{10,... | collective-permute-start | bytes 737288 | tf_op jit(solution)/shard_map/ppermute | solution.py:35
  44.1 1.4 %collective-permute-start.21 = (f32[1,5120]{1,0:T(1,128)S(1)}, f32[1,5120]{1,0:T(1,128)S(1)}, u32[]{:S(2)}, u32[]{:S(2)}) collective-permute-start(f32[1,5120]{1,0:T(1,128)S(1)} %get-tuple-element.20.own_ref), channel_id=1, source_target_pairs={{0,12},{1,13},{2,14},{3,15},{4,8},{5,9},{6,10},{7,11},{8,4},{9,5},... | collective-permute-start | bytes 61448 | tf_op jit(solution)/shard_map/ppermute | solution.py:35
  45.5 3.0 %collective-permute-start.19 = (f32[1,5120]{1,0:T(1,128)S(1)}, f32[1,5120]{1,0:T(1,128)S(1)}, u32[]{:S(2)}, u32[]{:S(2)}) collective-permute-start(f32[1,5120]{1,0:T(1,128)S(1)} %get-tuple-element.20.own_ref), channel_id=1, source_target_pairs={{0,4},{1,5},{2,6},{3,7},{4,0},{5,1},{6,2},{7,3},{8,12},{9,13},{10,... | collective-permute-start | bytes 61448 | tf_op jit(solution)/shard_map/ppermute | solution.py:35
  49.3 1.8 %collective-permute-done.15.order_ref = bf16[24,5120]{1,0:T(8,128)(2,1)S(1)} collective-permute-done((bf16[24,5120]{1,0:T(8,128)(2,1)S(1)}, bf16[24,5120]{1,0:T(8,128)(2,1)S(1)}, u32[]{:S(2)}, u32[]{:S(2)}) %collective-permute-start.15) | collective-permute-done | bytes 245792 | tf_op jit(solution)/shard_map/ppermute | solution.py:35
  51.2 1.8 %collective-permute-start.22 = (f32[1,5120]{1,0:T(1,128)S(1)}, f32[1,5120]{1,0:T(1,128)S(1)}, u32[]{:S(2)}, u32[]{:S(2)}) collective-permute-start(f32[1,5120]{1,0:T(1,128)S(1)} %shard_map.104), channel_id=1, source_target_pairs={{0,2},{1,3},{2,0},{3,1},{4,6},{5,7},{6,4},{7,5},{8,10},{9,11},{10,... | collective-permute-start | bytes 61448 | tf_op jit(solution)/shard_map/ppermute | solution.py:35
  53.1 1.8 %collective-permute-start.17 = (bf16[8,5120]{1,0:T(8,128)(2,1)S(1)}, bf16[8,5120]{1,0:T(8,128)(2,1)S(1)}, u32[]{:S(2)}, u32[]{:S(2)}) collective-permute-start(bf16[8,5120]{1,0:T(8,128)(2,1)S(1)} %get-tuple-element.23), channel_id=1, source_target_pairs={{0,8},{1,9},{2,10},{3,11},{4,12},{5,13},{6,14},{7,15},{8,0},{9,1},... | collective-permute-start | bytes 245768 | tf_op jit(solution)/shard_map/ppermute | solution.py:35
  54.9 2.5 %collective-permute-start.16 = (bf16[8,5120]{1,0:T(8,128)(2,1)S(1)}, bf16[8,5120]{1,0:T(8,128)(2,1)S(1)}, u32[]{:S(2)}, u32[]{:S(2)}) collective-permute-start(bf16[8,5120]{1,0:T(8,128)(2,1)S(1)} %get-tuple-element.24), channel_id=1, source_target_pairs={{0,12},{1,13},{2,14},{3,15},{4,8},{5,9},{6,10},{7,11},{8,4},{9,5},... | collective-permute-start | bytes 245768 | tf_op jit(solution)/shard_map/ppermute | solution.py:35
  58.6 1.8 %collective-permute-done.17.refs_2_ = bf16[8,5120]{1,0:T(8,128)(2,1)S(1)} collective-permute-done((bf16[8,5120]{1,0:T(8,128)(2,1)S(1)}, bf16[8,5120]{1,0:T(8,128)(2,1)S(1)}, u32[]{:S(2)}, u32[]{:S(2)}) %collective-permute-start.17) | collective-permute-done | bytes 81952 | tf_op jit(solution)/shard_map/ppermute | solution.py:35
  (48 shorter events, 10.3 us)
Async XLA Ops:
  2.4 7.2 %collective-permute-start.2 = (bf16[8,5248]{1,0:T(8,128)(2,1)}, bf16[8,5248]{1,0:T(8,128)(2,1)S(1)}, u32[]{:S(2)}, u32[]{:S(2)}) collective-permute-start(bf16[8,5248]{1,0:T(8,128)(2,1)} %shard_map.93.refs_0_), channel_id=1, source_target_pairs={{0,4},{1,5},{2,6},{3,7},{4,0},{5,1},{6,2},{7,3},{8,12},{9,13},{10,... | collective-permute-start | bytes 251912 | tf_op jit(solution)/shard_map/ppermute | solution.py:35
  5.5 6.9 %collective-permute-start.1 = (bf16[8,5248]{1,0:T(8,128)(2,1)}, bf16[8,5248]{1,0:T(8,128)(2,1)S(1)}, u32[]{:S(2)}, u32[]{:S(2)}) collective-permute-start(bf16[8,5248]{1,0:T(8,128)(2,1)} %shard_map.93.refs_0_), channel_id=1, source_target_pairs={{0,8},{1,9},{2,10},{3,11},{4,12},{5,13},{6,14},{7,15},{8,0},{9,1},... | collective-permute-start | bytes 251912 | tf_op jit(solution)/shard_map/ppermute | solution.py:35
  8.0 6.3 %collective-permute-start = (bf16[8,5248]{1,0:T(8,128)(2,1)}, bf16[8,5248]{1,0:T(8,128)(2,1)S(1)}, u32[]{:S(2)}, u32[]{:S(2)}) collective-permute-start(bf16[8,5248]{1,0:T(8,128)(2,1)} %shard_map.93.refs_0_), channel_id=1, source_target_pairs={{0,2},{1,3},{2,0},{3,1},{4,6},{5,7},{6,4},{7,5},{8,10},{9,11},{10,... | collective-permute-start | bytes 251912 | tf_op jit(solution)/shard_map/ppermute | solution.py:35
  12.4 8.3 %collective-permute-start.5 = (bf16[16,5248]{1,0:T(8,128)(2,1)S(1)}, bf16[16,5248]{1,0:T(8,128)(2,1)S(1)}, u32[]{:S(2)}, u32[]{:S(2)}) collective-permute-start(bf16[16,5248]{1,0:T(8,128)(2,1)S(1)} %shard_map.94.order_ref), channel_id=1, source_target_pairs={{0,2},{1,3},{2,0},{3,1},{4,6},{5,7},{6,4},{7,5},{8,10},{9,11},{10,... | collective-permute-start | bytes 503816 | tf_op jit(solution)/shard_map/ppermute | solution.py:35
  14.0 5.5 %collective-permute-start.4 = (bf16[8,5248]{1,0:T(8,128)(2,1)S(1)}, bf16[8,5248]{1,0:T(8,128)(2,1)S(1)}, u32[]{:S(2)}, u32[]{:S(2)}) collective-permute-start(bf16[8,5248]{1,0:T(8,128)(2,1)S(1)} %collective-permute-done.1.refs_0_.refs_2_), channel_id=1, source_target_pairs={{0,4},{1,5},{2,6},{3,7},{4,0},{5,1},{6,2},{7,3},{8,12},{9,13},{10,... | collective-permute-start | bytes 251912 | tf_op jit(solution)/shard_map/ppermute | solution.py:35
  14.3 6.4 %collective-permute-start.3 = (bf16[8,5248]{1,0:T(8,128)(2,1)S(1)}, bf16[8,5248]{1,0:T(8,128)(2,1)S(1)}, u32[]{:S(2)}, u32[]{:S(2)}) collective-permute-start(bf16[8,5248]{1,0:T(8,128)(2,1)S(1)} %collective-permute-done.refs_1_), channel_id=1, source_target_pairs={{0,12},{1,13},{2,14},{3,15},{4,8},{5,9},{6,10},{7,11},{8,4},{9,5},... | collective-permute-start | bytes 251912 | tf_op jit(solution)/shard_map/ppermute | solution.py:35
  20.7 2.2 %collective-permute-start.6 = (bf16[64,5248]{1,0:T(8,128)(2,1)S(1)}, bf16[64,5248]{1,0:T(8,128)(2,1)S(1)}, u32[]{:S(2)}, u32[]{:S(2)}) collective-permute-start(bf16[64,5248]{1,0:T(8,128)(2,1)S(1)} %shard_map.96), channel_id=1, source_target_pairs={{0,1},{1,0},{2,3},{3,2},{4,5},{5,4},{6,7},{7,6},{8,9},{9,8},{10,11... | collective-permute-start | bytes 2015240 | tf_op jit(solution)/shard_map/ppermute | solution.py:35
  25.2 6.8 %collective-permute-start.9 = (f32[8,128]{1,0:T(8,128)S(1)}, f32[8,128]{1,0:T(8,128)S(1)}, u32[]{:S(2)}, u32[]{:S(2)}) collective-permute-start(f32[8,128]{1,0:T(8,128)S(1)} %get-tuple-element.13.order_ref.refs_0_), channel_id=1, source_target_pairs={{0,4},{1,5},{2,6},{3,7},{4,0},{5,1},{6,2},{7,3},{8,12},{9,13},{10,... | collective-permute-start | bytes 12296 | tf_op jit(solution)/shard_map/ppermute | solution.py:35
  25.9 6.1 %collective-permute-start.8 = (f32[8,128]{1,0:T(8,128)S(1)}, f32[8,128]{1,0:T(8,128)S(1)}, u32[]{:S(2)}, u32[]{:S(2)}) collective-permute-start(f32[8,128]{1,0:T(8,128)S(1)} %get-tuple-element.13.order_ref.refs_0_), channel_id=1, source_target_pairs={{0,8},{1,9},{2,10},{3,11},{4,12},{5,13},{6,14},{7,15},{8,0},{9,1},... | collective-permute-start | bytes 12296 | tf_op jit(solution)/shard_map/ppermute | solution.py:35
  28.3 5.4 %collective-permute-start.7 = (f32[8,128]{1,0:T(8,128)S(1)}, f32[8,128]{1,0:T(8,128)S(1)}, u32[]{:S(2)}, u32[]{:S(2)}) collective-permute-start(f32[8,128]{1,0:T(8,128)S(1)} %get-tuple-element.13.order_ref.refs_0_), channel_id=1, source_target_pairs={{0,12},{1,13},{2,14},{3,15},{4,8},{5,9},{6,10},{7,11},{8,4},{9,5},... | collective-permute-start | bytes 12296 | tf_op jit(solution)/shard_map/ppermute | solution.py:35
  33.7 1.9 %collective-permute-start.12 = (f32[32,128]{1,0:T(8,128)S(1)}, f32[32,128]{1,0:T(8,128)S(1)}, u32[]{:S(2)}, u32[]{:S(2)}) collective-permute-start(f32[32,128]{1,0:T(8,128)S(1)} %shard_map.99), channel_id=1, source_target_pairs={{0,1},{1,0},{2,3},{3,2},{4,5},{5,4},{6,7},{7,6},{8,9},{9,8},{10,11... | collective-permute-start | bytes 49160 | tf_op jit(solution)/shard_map/ppermute | solution.py:35
  33.7 3.8 %collective-permute-start.11 = (f32[32,128]{1,0:T(8,128)S(1)}, f32[32,128]{1,0:T(8,128)S(1)}, u32[]{:S(2)}, u32[]{:S(2)}) collective-permute-start(f32[32,128]{1,0:T(8,128)S(1)} %shard_map.99), channel_id=1, source_target_pairs={{0,2},{1,3},{2,0},{3,1},{4,6},{5,7},{6,4},{7,5},{8,10},{9,11},{10,... | collective-permute-start | bytes 49160 | tf_op jit(solution)/shard_map/ppermute | solution.py:35
  34.2 3.3 %collective-permute-start.10 = (f32[32,128]{1,0:T(8,128)S(1)}, f32[32,128]{1,0:T(8,128)S(1)}, u32[]{:S(2)}, u32[]{:S(2)}) collective-permute-start(f32[32,128]{1,0:T(8,128)S(1)} %shard_map.99), channel_id=1, source_target_pairs={{0,3},{1,2},{2,1},{3,0},{4,7},{5,6},{6,5},{7,4},{8,11},{9,10},{10,... | collective-permute-start | bytes 49160 | tf_op jit(solution)/shard_map/ppermute | solution.py:35
  40.3 2.3 %collective-permute-start.13 = (bf16[72,5120]{1,0:T(8,128)(2,1)S(1)}, bf16[72,5120]{1,0:T(8,128)(2,1)S(1)}, u32[]{:S(2)}, u32[]{:S(2)}) collective-permute-start(bf16[72,5120]{1,0:T(8,128)(2,1)S(1)} %get-tuple-element.16), channel_id=1, source_target_pairs={{0,1},{1,0},{2,3},{3,2},{4,5},{5,4},{6,7},{7,6},{8,9},{9,8},{10,11... | collective-permute-start | bytes 2211848 | tf_op jit(solution)/shard_map/ppermute | solution.py:35
  42.6 8.4 %collective-permute-start.15 = (bf16[24,5120]{1,0:T(8,128)(2,1)S(1)}, bf16[24,5120]{1,0:T(8,128)(2,1)S(1)}, u32[]{:S(2)}, u32[]{:S(2)}) collective-permute-start(bf16[24,5120]{1,0:T(8,128)(2,1)S(1)} %shard_map.101.order_ref), channel_id=1, source_target_pairs={{0,2},{1,3},{2,0},{3,1},{4,6},{5,7},{6,4},{7,5},{8,10},{9,11},{10,... | collective-permute-start | bytes 737288 | tf_op jit(solution)/shard_map/ppermute | solution.py:35
  44.0 17.2 %copy-start.2 = (bf16[8,5120]{1,0:T(8,128)(2,1)S(1)}, bf16[8,5120]{1,0:T(8,128)(2,1)}, u32[]{:S(2)}) copy-start(bf16[8,5120]{1,0:T(8,128)(2,1)} %rows_ref.1) | copy-start | bytes 245764
  44.1 7.0 %collective-permute-start.21 = (f32[1,5120]{1,0:T(1,128)S(1)}, f32[1,5120]{1,0:T(1,128)S(1)}, u32[]{:S(2)}, u32[]{:S(2)}) collective-permute-start(f32[1,5120]{1,0:T(1,128)S(1)} %get-tuple-element.20.own_ref), channel_id=1, source_target_pairs={{0,12},{1,13},{2,14},{3,15},{4,8},{5,9},{6,10},{7,11},{8,4},{9,5},... | collective-permute-start | bytes 61448 | tf_op jit(solution)/shard_map/ppermute | solution.py:35
  45.5 5.6 %collective-permute-start.20 = (f32[1,5120]{1,0:T(1,128)S(1)}, f32[1,5120]{1,0:T(1,128)S(1)}, u32[]{:S(2)}, u32[]{:S(2)}) collective-permute-start(f32[1,5120]{1,0:T(1,128)S(1)} %get-tuple-element.20.own_ref), channel_id=1, source_target_pairs={{0,8},{1,9},{2,10},{3,11},{4,12},{5,13},{6,14},{7,15},{8,0},{9,1},... | collective-permute-start | bytes 61448 | tf_op jit(solution)/shard_map/ppermute | solution.py:35
  45.5 5.6 %collective-permute-start.19 = (f32[1,5120]{1,0:T(1,128)S(1)}, f32[1,5120]{1,0:T(1,128)S(1)}, u32[]{:S(2)}, u32[]{:S(2)}) collective-permute-start(f32[1,5120]{1,0:T(1,128)S(1)} %get-tuple-element.20.own_ref), channel_id=1, source_target_pairs={{0,4},{1,5},{2,6},{3,7},{4,0},{5,1},{6,2},{7,3},{8,12},{9,13},{10,... | collective-permute-start | bytes 61448 | tf_op jit(solution)/shard_map/ppermute | solution.py:35
  48.6 10.0 %collective-permute-start.14 = (bf16[8,5120]{1,0:T(8,128)(2,1)S(1)}, bf16[8,5120]{1,0:T(8,128)(2,1)S(1)}, u32[]{:S(2)}, u32[]{:S(2)}) collective-permute-start(bf16[8,5120]{1,0:T(8,128)(2,1)S(1)} %get-tuple-element.19), channel_id=1, source_target_pairs={{0,2},{1,3},{2,0},{3,1},{4,6},{5,7},{6,4},{7,5},{8,10},{9,11},{10,... | collective-permute-start | bytes 245768 | tf_op jit(solution)/shard_map/ppermute | solution.py:35
  51.2 6.8 %collective-permute-start.22 = (f32[1,5120]{1,0:T(1,128)S(1)}, f32[1,5120]{1,0:T(1,128)S(1)}, u32[]{:S(2)}, u32[]{:S(2)}) collective-permute-start(f32[1,5120]{1,0:T(1,128)S(1)} %shard_map.104), channel_id=1, source_target_pairs={{0,2},{1,3},{2,0},{3,1},{4,6},{5,7},{6,4},{7,5},{8,10},{9,11},{10,... | collective-permute-start | bytes 61448 | tf_op jit(solution)/shard_map/ppermute | solution.py:35
  53.0 5.6 %collective-permute-start.18 = (bf16[8,5120]{1,0:T(8,128)(2,1)S(1)}, bf16[8,5120]{1,0:T(8,128)(2,1)S(1)}, u32[]{:S(2)}, u32[]{:S(2)}) collective-permute-start(bf16[8,5120]{1,0:T(8,128)(2,1)S(1)} %get-tuple-element.22), channel_id=1, source_target_pairs={{0,4},{1,5},{2,6},{3,7},{4,0},{5,1},{6,2},{7,3},{8,12},{9,13},{10,... | collective-permute-start | bytes 245768 | tf_op jit(solution)/shard_map/ppermute | solution.py:35
  53.1 7.3 %collective-permute-start.17 = (bf16[8,5120]{1,0:T(8,128)(2,1)S(1)}, bf16[8,5120]{1,0:T(8,128)(2,1)S(1)}, u32[]{:S(2)}, u32[]{:S(2)}) collective-permute-start(bf16[8,5120]{1,0:T(8,128)(2,1)S(1)} %get-tuple-element.23), channel_id=1, source_target_pairs={{0,8},{1,9},{2,10},{3,11},{4,12},{5,13},{6,14},{7,15},{8,0},{9,1},... | collective-permute-start | bytes 245768 | tf_op jit(solution)/shard_map/ppermute | solution.py:35
  54.9 6.3 %collective-permute-start.16 = (bf16[8,5120]{1,0:T(8,128)(2,1)S(1)}, bf16[8,5120]{1,0:T(8,128)(2,1)S(1)}, u32[]{:S(2)}, u32[]{:S(2)}) collective-permute-start(bf16[8,5120]{1,0:T(8,128)(2,1)S(1)} %get-tuple-element.24), channel_id=1, source_target_pairs={{0,12},{1,13},{2,14},{3,15},{4,8},{5,9},{6,10},{7,11},{8,4},{9,5},... | collective-permute-start | bytes 245768 | tf_op jit(solution)/shard_map/ppermute | solution.py:35
  (3 other events, 18.6 us)

commit v5 on v4

--- a/solution.py
+++ b/solution.py
@@ -38,7 +38,7 @@
         swap = self.swap
         if self.count == 16:
             far, near, side = swap(own, 8), swap(own, 4), swap(own, 2)
-            across = stack_blocks([far, near], flops=STACK_FLOPS)
+            across = stack_blocks([near, far], flops=STACK_FLOPS)
             crossed = swap(across, 2)
             beyond, diagonal = swap(side, 12), swap(far, 4)
             result = meanwhile(across)
@@ -51,7 +51,7 @@
 
     def codes(self):
         if self.count == 16:
-            first = [0, 2, 8, 4, 14, 12, 10, 6]
+            first = [0, 2, 8, 4, 14, 12, 6, 10]
             return first + [c ^ 1 for c in first]
         codes = [0]
         for m in reversed(bits_of(self.count)):
@@ -62,9 +62,9 @@
         swap = self.swap
         result = meanwhile(own)
         if self.count == 16:
-            far = [swap(own, m) for m in (12, 8, 4)]
-            column = stack_blocks([own] + far, after=result)
-            return cat(column, swap(column, 3), swap(column, 2), swap(column, 1)), result
+            others = [swap(own, m) for m in (4, 8, 12)]
+            column = stack_blocks([own] + others, after=result)
+            return cat(column, swap(column, 1), swap(column, 2), swap(column, 3)), result
         tiles = own
         for m in bits_of(self.count):
             tiles = cat(tiles, swap(tiles, m))
@@ -72,7 +72,7 @@
 
     def small_place(self, code):
         if self.count == 16:
-            return ((4 - (code & 3)) & 3) * 4 + ((4 - (code >> 2)) & 3)
+            return (code & 3) * 4 + (code >> 2)
         return code
 
 
@@ -411,7 +411,7 @@
 
     b = own_count
     if count == 16:
-        going_order = (7, 6, 4)
+        going_order = (6, 7, 4)
         rest_order = ((0, 3, 2, 5), (1,))
         sizes = [(4, f32), (1, bf16)]
     else:
@@ -440,7 +440,7 @@
         gain_grad = gain_grad + swap(gain_grad, 2)
         column = (kept[b:] + crossed.astype(f32)).astype(bf16)
         more = [beside] + [
-            swap(column[k * b : (k + 1) * b], m) for k, m in ((2, 12), (1, 8), (0, 4))
+            swap(column[k * b : (k + 1) * b], m) for k, m in ((0, 4), (1, 8), (2, 12))
         ]
     else:
         for m in bits_of(count)[1:]:

time: 62.4 us -> 61 us (0.978)
  starting transfers between devices: 30.9 us -> 29.5 us
    ppermute x23, starting transfers between devices: 30.9 us -> 29.5 us  [swap(): return lax.ppermute(value, 'vocab', [(i, i ^ m) for i in range(self.count)])]
  transfers between devices with their start and end apart: 23 -> 23, of which waited for: 9 -> 10; matrix products, arithmetic and copies ran while one was open for 2% -> 2% of each run, Pallas kernels for 8% -> 8%
where the time goes in v5:
time: 61 us; the launch traced here: 60.9 us
  starting transfers between devices  29.5 us (48%)
  waiting for transfers between devices  15.8 us (26%)
  Pallas kernels  12.4 us (20%)
  between operations  1.46 us (2%)
  local copies, waits for them, and re-layouts  0.91 us (1%)
  other arithmetic  0.77 us (1%)
    ppermute x23, starting transfers between devices, swap(): return lax.ppermute(value, 'vocab', [(i, i ^ m) for i in range(self.count)])  29.5 us
    ppermute x23, waiting for transfers between devices, swap(): return lax.ppermute(value, 'vocab', [(i, i ^ m) for i in range(self.count)])  15.8 us
    pallas_call x2, Pallas kernels, turn(): call(functools.partial(turn_kernel, part), shaped((slab_width // 2, width...  4.68 us
    pallas_call x1, Pallas kernels, on_device(): call(functools.partial(slab_kernel, codes, links.small_place), (shaped((8...  2.74 us
    pallas_call x1, Pallas kernels, on_device(): call(functools.partial(logits_kernel, codes), (shaped((token_count, slab_...  2.18 us
    pallas_call x1, Pallas kernels, on_device(): call(norm_kernel, shaped((own_count, width + LANES), bf16), [HBM] * 4, [p...  1.73 us
  transfers between devices with their start and end apart: 23, of which 10 were waited for; matrix products, arithmetic and copies ran while one was open for 2% of the time, Pallas kernels for 8%

profile of v5, /device:TPU:0, one launch (start us, length us, event | category | flops | bytes accessed | tf_op | source)
XLA Modules:
  0.0 60.9 jit_solution(10821284217825900961)
XLA Ops:
  0.6 1.7 %shard_map.93.refs_0_ = bf16[8,5248]{1,0:T(8,128)(2,1)} custom-call(s32[8]{0:T(128)} %ids_hbm.1, s32[8]{0:T(128)} %flags_hbm.1, bf16[8,5120]{1,0:T(8,128)(2,1)} %rows_ref.1, f32[1,5120]{1,0:T(1,128)} %bitcast.4), custom_call_target="tpu_custom_call" | custom-call | tf_op jit(solution)/shard_map/pallas_call | solution.py:358
  2.4 3.1 %collective-permute-start.2 = (bf16[8,5248]{1,0:T(8,128)(2,1)}, bf16[8,5248]{1,0:T(8,128)(2,1)S(1)}, u32[]{:S(2)}, u32[]{:S(2)}) collective-permute-start(bf16[8,5248]{1,0:T(8,128)(2,1)} %shard_map.93.refs_0_), channel_id=1, source_target_pairs={{0,4},{1,5},{2,6},{3,7},{4,0},{5,1},{6,2},{7,3},{8,12},{9,13},{10,... | collective-permute-start | bytes 251912 | tf_op jit(solution)/shard_map/ppermute | solution.py:35
  5.5 2.6 %collective-permute-start.1 = (bf16[8,5248]{1,0:T(8,128)(2,1)}, bf16[8,5248]{1,0:T(8,128)(2,1)S(1)}, u32[]{:S(2)}, u32[]{:S(2)}) collective-permute-start(bf16[8,5248]{1,0:T(8,128)(2,1)} %shard_map.93.refs_0_), channel_id=1, source_target_pairs={{0,8},{1,9},{2,10},{3,11},{4,12},{5,13},{6,14},{7,15},{8,0},{9,1},... | collective-permute-start | bytes 251912 | tf_op jit(solution)/shard_map/ppermute | solution.py:35
  8.0 1.5 %collective-permute-start = (bf16[8,5248]{1,0:T(8,128)(2,1)}, bf16[8,5248]{1,0:T(8,128)(2,1)S(1)}, u32[]{:S(2)}, u32[]{:S(2)}) collective-permute-start(bf16[8,5248]{1,0:T(8,128)(2,1)} %shard_map.93.refs_0_), channel_id=1, source_target_pairs={{0,2},{1,3},{2,0},{3,1},{4,6},{5,7},{6,4},{7,5},{8,10},{9,11},{10,... | collective-permute-start | bytes 251912 | tf_op jit(solution)/shard_map/ppermute | solution.py:35
  9.6 2.8 %collective-permute-done.1.refs_1_.refs_2_ = bf16[8,5248]{1,0:T(8,128)(2,1)S(1)} collective-permute-done((bf16[8,5248]{1,0:T(8,128)(2,1)}, bf16[8,5248]{1,0:T(8,128)(2,1)S(1)}, u32[]{:S(2)}, u32[]{:S(2)}) %collective-permute-start.1) | collective-permute-done | bytes 84000 | tf_op jit(solution)/shard_map/ppermute | solution.py:35
  12.4 1.6 %collective-permute-start.5 = (bf16[16,5248]{1,0:T(8,128)(2,1)S(1)}, bf16[16,5248]{1,0:T(8,128)(2,1)S(1)}, u32[]{:S(2)}, u32[]{:S(2)}) collective-permute-start(bf16[16,5248]{1,0:T(8,128)(2,1)S(1)} %shard_map.94.order_ref), channel_id=1, source_target_pairs={{0,2},{1,3},{2,0},{3,1},{4,6},{5,7},{6,4},{7,5},{8,10},{9,11},{10,... | collective-permute-start | bytes 503816 | tf_op jit(solution)/shard_map/ppermute | solution.py:35
  14.3 2.5 %collective-permute-start.3 = (bf16[8,5248]{1,0:T(8,128)(2,1)S(1)}, bf16[8,5248]{1,0:T(8,128)(2,1)S(1)}, u32[]{:S(2)}, u32[]{:S(2)}) collective-permute-start(bf16[8,5248]{1,0:T(8,128)(2,1)S(1)} %collective-permute-done.refs_1_), channel_id=1, source_target_pairs={{0,12},{1,13},{2,14},{3,15},{4,8},{5,9},{6,10},{7,11},{8,4},{9,5},... | collective-permute-start | bytes 251912 | tf_op jit(solution)/shard_map/ppermute | solution.py:35
  17.1 2.3 %shard_map.95.refs_7_.order_ref.head_ref = bf16[640,5120]{1,0:T(8,128)(2,1)S(1)} custom-call(bf16[5120,1280]{1,0:T(8,128)(2,1)S(1)} %copy-done, bf16[16,5248]{1,0:T(8,128)(2,1)S(1)} %shard_map.94.order_ref), custom_call_target="tpu_custom_call" | custom-call | flops 3000000000 | bytes 13107200 | tf_op jit(solution)/shard_map/pallas_call | solution.py:372
  21.5 1.5 %collective-permute-done.6 = bf16[64,5248]{1,0:T(8,128)(2,1)S(1)} collective-permute-done((bf16[64,5248]{1,0:T(8,128)(2,1)S(1)}, bf16[64,5248]{1,0:T(8,128)(2,1)S(1)}, u32[]{:S(2)}, u32[]{:S(2)}) %collective-permute-start.6) | collective-permute-done | bytes 671776 | tf_op jit(solution)/shard_map/ppermute | solution.py:35
  23.0 2.2 %shard_map.97 = (f32[128,1280]{1,0:T(8,128)S(1)}, f32[8,128]{1,0:T(8,128)S(1)}) custom-call(f32[1]{0:T(128)S(6)} %copy.10.divisor_ref, bf16[128,5248]{1,0:T(8,128)(2,1)S(1)} %pad_maximum_fusion.rows_ref, bf16[5120,1280]{1,0:T(8,128)(2,1)S(1)} %copy-done, bf16[640,5120]{1,0:T(8,128)(2,1)S(1)} %shard_map.95.refs_7_.order_ref.head_ref), custom_call_target="tpu_custom_call" | custom-call | flops 1677721600 | bytes 13107200 | tf_op jit(solution)/shard_map/pallas_call | solution.py:383
  25.2 2.5 %collective-permute-start.9 = (f32[8,128]{1,0:T(8,128)S(1)}, f32[8,128]{1,0:T(8,128)S(1)}, u32[]{:S(2)}, u32[]{:S(2)}) collective-permute-start(f32[8,128]{1,0:T(8,128)S(1)} %get-tuple-element.13.order_ref.refs_0_), channel_id=1, source_target_pairs={{0,12},{1,13},{2,14},{3,15},{4,8},{5,9},{6,10},{7,11},{8,4},{9,5},... | collective-permute-start | bytes 12296 | tf_op jit(solution)/shard_map/ppermute | solution.py:35
  27.7 1.9 %collective-permute-start.7 = (f32[8,128]{1,0:T(8,128)S(1)}, f32[8,128]{1,0:T(8,128)S(1)}, u32[]{:S(2)}, u32[]{:S(2)}) collective-permute-start(f32[8,128]{1,0:T(8,128)S(1)} %get-tuple-element.13.order_ref.refs_0_), channel_id=1, source_target_pairs={{0,4},{1,5},{2,6},{3,7},{4,0},{5,1},{6,2},{7,3},{8,12},{9,13},{10,... | collective-permute-start | bytes 12296 | tf_op jit(solution)/shard_map/ppermute | solution.py:35
  29.6 2.3 %shard_map.98.refs_4_.head2_ref = bf16[640,5120]{1,0:T(8,128)(2,1)S(1)} custom-call(bf16[5120,1280]{1,0:T(8,128)(2,1)S(1)} %copy-done, f32[8,128]{1,0:T(8,128)S(1)} %get-tuple-element.13.order_ref.refs_0_), custom_call_target="tpu_custom_call" | custom-call | flops 3000000000 | bytes 13107200 | tf_op jit(solution)/shard_map/pallas_call | solution.py:372
  34.1 1.3 %collective-permute-done.12 = f32[32,128]{1,0:T(8,128)S(1)} collective-permute-done((f32[32,128]{1,0:T(8,128)S(1)}, f32[32,128]{1,0:T(8,128)S(1)}, u32[]{:S(2)}, u32[]{:S(2)}) %collective-permute-start.12) | collective-permute-done | bytes 16416 | tf_op jit(solution)/shard_map/ppermute | solution.py:35
  36.1 2.7 %shard_map.100 = (f32[8,128]{1,0:T(8,128)S(1)}, bf16[8,1280]{1,0:T(8,128)(2,1)S(1)}, f32[64,5120]{1,0:T(8,128)S(1)}, bf16[72,5120]{1,0:T(8,128)(2,1)S(1)}) custom-call(f32[1]{0:T(128)S(6)} %copy.10.divisor_ref, f32[128,128]{1,0:T(8,128)S(1)} %pad_maximum_fusion.1.tiles_ref, bf16[128,5248]{1,0:T(8,128)(2,1)S(1)} %pad_maximum_fusion.rows_ref, ...), custom_call_target="tpu_custom_call" | custom-call | flops 1677721600 | bytes 13107200 | tf_op jit(solution)/shard_map/pallas_call | solution.py:393
  38.9 2.2 %collective-permute-done.13.twin_ref = bf16[72,5120]{1,0:T(8,128)(2,1)S(1)} collective-permute-done((bf16[72,5120]{1,0:T(8,128)(2,1)S(1)}, bf16[72,5120]{1,0:T(8,128)(2,1)S(1)}, u32[]{:S(2)}, u32[]{:S(2)}) %collective-permute-start.13) | collective-permute-done | bytes 737312 | tf_op jit(solution)/shard_map/ppermute | solution.py:35
  42.0 2.5 %collective-permute-start.21 = (f32[1,5120]{1,0:T(1,128)S(1)}, f32[1,5120]{1,0:T(1,128)S(1)}, u32[]{:S(2)}, u32[]{:S(2)}) collective-permute-start(f32[1,5120]{1,0:T(1,128)S(1)} %get-tuple-element.20.own_ref), channel_id=1, source_target_pairs={{0,12},{1,13},{2,14},{3,15},{4,8},{5,9},{6,10},{7,11},{8,4},{9,5},... | collective-permute-start | bytes 61448 | tf_op jit(solution)/shard_map/ppermute | solution.py:35
  44.6 1.9 %collective-permute-start.19 = (f32[1,5120]{1,0:T(1,128)S(1)}, f32[1,5120]{1,0:T(1,128)S(1)}, u32[]{:S(2)}, u32[]{:S(2)}) collective-permute-start(f32[1,5120]{1,0:T(1,128)S(1)} %get-tuple-element.20.own_ref), channel_id=1, source_target_pairs={{0,4},{1,5},{2,6},{3,7},{4,0},{5,1},{6,2},{7,3},{8,12},{9,13},{10,... | collective-permute-start | bytes 61448 | tf_op jit(solution)/shard_map/ppermute | solution.py:35
  46.5 1.3 %collective-permute-start.14 = (bf16[8,5120]{1,0:T(8,128)(2,1)S(1)}, bf16[8,5120]{1,0:T(8,128)(2,1)S(1)}, u32[]{:S(2)}, u32[]{:S(2)}) collective-permute-start(bf16[8,5120]{1,0:T(8,128)(2,1)S(1)} %get-tuple-element.19), channel_id=1, source_target_pairs={{0,2},{1,3},{2,0},{3,1},{4,6},{5,7},{6,4},{7,5},{8,10},{9,11},{10,... | collective-permute-start | bytes 245768 | tf_op jit(solution)/shard_map/ppermute | solution.py:35
  47.8 2.2 %collective-permute-done.15.order_ref = bf16[24,5120]{1,0:T(8,128)(2,1)S(1)} collective-permute-done((bf16[24,5120]{1,0:T(8,128)(2,1)S(1)}, bf16[24,5120]{1,0:T(8,128)(2,1)S(1)}, u32[]{:S(2)}, u32[]{:S(2)}) %collective-permute-start.15) | collective-permute-done | bytes 245792 | tf_op jit(solution)/shard_map/ppermute | solution.py:35
  50.7 2.5 %collective-permute-start.18 = (bf16[8,5120]{1,0:T(8,128)(2,1)S(1)}, bf16[8,5120]{1,0:T(8,128)(2,1)S(1)}, u32[]{:S(2)}, u32[]{:S(2)}) collective-permute-start(bf16[8,5120]{1,0:T(8,128)(2,1)S(1)} %get-tuple-element.22), channel_id=1, source_target_pairs={{0,12},{1,13},{2,14},{3,15},{4,8},{5,9},{6,10},{7,11},{8,4},{9,5},... | collective-permute-start | bytes 245768 | tf_op jit(solution)/shard_map/ppermute | solution.py:35
  53.2 1.9 %collective-permute-start.16 = (bf16[8,5120]{1,0:T(8,128)(2,1)S(1)}, bf16[8,5120]{1,0:T(8,128)(2,1)S(1)}, u32[]{:S(2)}, u32[]{:S(2)}) collective-permute-start(bf16[8,5120]{1,0:T(8,128)(2,1)S(1)} %get-tuple-element.24), channel_id=1, source_target_pairs={{0,4},{1,5},{2,6},{3,7},{4,0},{5,1},{6,2},{7,3},{8,12},{9,13},{10,... | collective-permute-start | bytes 245768 | tf_op jit(solution)/shard_map/ppermute | solution.py:35
  56.3 1.5 %collective-permute-done.18.refs_3_ = bf16[8,5120]{1,0:T(8,128)(2,1)S(1)} collective-permute-done((bf16[8,5120]{1,0:T(8,128)(2,1)S(1)}, bf16[8,5120]{1,0:T(8,128)(2,1)S(1)}, u32[]{:S(2)}, u32[]{:S(2)}) %collective-permute-start.18) | collective-permute-done | bytes 81952 | tf_op jit(solution)/shard_map/ppermute | solution.py:35
  57.8 2.2 %collective-permute-done.17.refs_2_ = bf16[8,5120]{1,0:T(8,128)(2,1)S(1)} collective-permute-done((bf16[8,5120]{1,0:T(8,128)(2,1)S(1)}, bf16[8,5120]{1,0:T(8,128)(2,1)S(1)}, u32[]{:S(2)}, u32[]{:S(2)}) %collective-permute-start.17) | collective-permute-done | bytes 81952 | tf_op jit(solution)/shard_map/ppermute | solution.py:35
  (48 shorter events, 8.6 us)
Async XLA Ops:
  2.4 7.2 %collective-permute-start.2 = (bf16[8,5248]{1,0:T(8,128)(2,1)}, bf16[8,5248]{1,0:T(8,128)(2,1)S(1)}, u32[]{:S(2)}, u32[]{:S(2)}) collective-permute-start(bf16[8,5248]{1,0:T(8,128)(2,1)} %shard_map.93.refs_0_), channel_id=1, source_target_pairs={{0,4},{1,5},{2,6},{3,7},{4,0},{5,1},{6,2},{7,3},{8,12},{9,13},{10,... | collective-permute-start | bytes 251912 | tf_op jit(solution)/shard_map/ppermute | solution.py:35
  5.5 6.9 %collective-permute-start.1 = (bf16[8,5248]{1,0:T(8,128)(2,1)}, bf16[8,5248]{1,0:T(8,128)(2,1)S(1)}, u32[]{:S(2)}, u32[]{:S(2)}) collective-permute-start(bf16[8,5248]{1,0:T(8,128)(2,1)} %shard_map.93.refs_0_), channel_id=1, source_target_pairs={{0,8},{1,9},{2,10},{3,11},{4,12},{5,13},{6,14},{7,15},{8,0},{9,1},... | collective-permute-start | bytes 251912 | tf_op jit(solution)/shard_map/ppermute | solution.py:35
  8.0 6.3 %collective-permute-start = (bf16[8,5248]{1,0:T(8,128)(2,1)}, bf16[8,5248]{1,0:T(8,128)(2,1)S(1)}, u32[]{:S(2)}, u32[]{:S(2)}) collective-permute-start(bf16[8,5248]{1,0:T(8,128)(2,1)} %shard_map.93.refs_0_), channel_id=1, source_target_pairs={{0,2},{1,3},{2,0},{3,1},{4,6},{5,7},{6,4},{7,5},{8,10},{9,11},{10,... | collective-permute-start | bytes 251912 | tf_op jit(solution)/shard_map/ppermute | solution.py:35
  12.4 8.3 %collective-permute-start.5 = (bf16[16,5248]{1,0:T(8,128)(2,1)S(1)}, bf16[16,5248]{1,0:T(8,128)(2,1)S(1)}, u32[]{:S(2)}, u32[]{:S(2)}) collective-permute-start(bf16[16,5248]{1,0:T(8,128)(2,1)S(1)} %shard_map.94.order_ref), channel_id=1, source_target_pairs={{0,2},{1,3},{2,0},{3,1},{4,6},{5,7},{6,4},{7,5},{8,10},{9,11},{10,... | collective-permute-start | bytes 503816 | tf_op jit(solution)/shard_map/ppermute | solution.py:35
  14.0 5.5 %collective-permute-start.4 = (bf16[8,5248]{1,0:T(8,128)(2,1)S(1)}, bf16[8,5248]{1,0:T(8,128)(2,1)S(1)}, u32[]{:S(2)}, u32[]{:S(2)}) collective-permute-start(bf16[8,5248]{1,0:T(8,128)(2,1)S(1)} %collective-permute-done.1.refs_1_.refs_2_), channel_id=1, source_target_pairs={{0,4},{1,5},{2,6},{3,7},{4,0},{5,1},{6,2},{7,3},{8,12},{9,13},{10,... | collective-permute-start | bytes 251912 | tf_op jit(solution)/shard_map/ppermute | solution.py:35
  14.3 6.4 %collective-permute-start.3 = (bf16[8,5248]{1,0:T(8,128)(2,1)S(1)}, bf16[8,5248]{1,0:T(8,128)(2,1)S(1)}, u32[]{:S(2)}, u32[]{:S(2)}) collective-permute-start(bf16[8,5248]{1,0:T(8,128)(2,1)S(1)} %collective-permute-done.refs_1_), channel_id=1, source_target_pairs={{0,12},{1,13},{2,14},{3,15},{4,8},{5,9},{6,10},{7,11},{8,4},{9,5},... | collective-permute-start | bytes 251912 | tf_op jit(solution)/shard_map/ppermute | solution.py:35
  20.7 2.2 %collective-permute-start.6 = (bf16[64,5248]{1,0:T(8,128)(2,1)S(1)}, bf16[64,5248]{1,0:T(8,128)(2,1)S(1)}, u32[]{:S(2)}, u32[]{:S(2)}) collective-permute-start(bf16[64,5248]{1,0:T(8,128)(2,1)S(1)} %shard_map.96), channel_id=1, source_target_pairs={{0,1},{1,0},{2,3},{3,2},{4,5},{5,4},{6,7},{7,6},{8,9},{9,8},{10,11... | collective-permute-start | bytes 2015240 | tf_op jit(solution)/shard_map/ppermute | solution.py:35
  25.2 6.8 %collective-permute-start.9 = (f32[8,128]{1,0:T(8,128)S(1)}, f32[8,128]{1,0:T(8,128)S(1)}, u32[]{:S(2)}, u32[]{:S(2)}) collective-permute-start(f32[8,128]{1,0:T(8,128)S(1)} %get-tuple-element.13.order_ref.refs_0_), channel_id=1, source_target_pairs={{0,12},{1,13},{2,14},{3,15},{4,8},{5,9},{6,10},{7,11},{8,4},{9,5},... | collective-permute-start | bytes 12296 | tf_op jit(solution)/shard_map/ppermute | solution.py:35
  27.7 4.5 %collective-permute-start.8 = (f32[8,128]{1,0:T(8,128)S(1)}, f32[8,128]{1,0:T(8,128)S(1)}, u32[]{:S(2)}, u32[]{:S(2)}) collective-permute-start(f32[8,128]{1,0:T(8,128)S(1)} %get-tuple-element.13.order_ref.refs_0_), channel_id=1, source_target_pairs={{0,8},{1,9},{2,10},{3,11},{4,12},{5,13},{6,14},{7,15},{8,0},{9,1},... | collective-permute-start | bytes 12296 | tf_op jit(solution)/shard_map/ppermute | solution.py:35
  27.7 4.5 %collective-permute-start.7 = (f32[8,128]{1,0:T(8,128)S(1)}, f32[8,128]{1,0:T(8,128)S(1)}, u32[]{:S(2)}, u32[]{:S(2)}) collective-permute-start(f32[8,128]{1,0:T(8,128)S(1)} %get-tuple-element.13.order_ref.refs_0_), channel_id=1, source_target_pairs={{0,4},{1,5},{2,6},{3,7},{4,0},{5,1},{6,2},{7,3},{8,12},{9,13},{10,... | collective-permute-start | bytes 12296 | tf_op jit(solution)/shard_map/ppermute | solution.py:35
  32.2 3.2 %collective-permute-start.12 = (f32[32,128]{1,0:T(8,128)S(1)}, f32[32,128]{1,0:T(8,128)S(1)}, u32[]{:S(2)}, u32[]{:S(2)}) collective-permute-start(f32[32,128]{1,0:T(8,128)S(1)} %shard_map.99), channel_id=1, source_target_pairs={{0,3},{1,2},{2,1},{3,0},{4,7},{5,6},{6,5},{7,4},{8,11},{9,10},{10,... | collective-permute-start | bytes 49160 | tf_op jit(solution)/shard_map/ppermute | solution.py:35
  32.3 3.8 %collective-permute-start.11 = (f32[32,128]{1,0:T(8,128)S(1)}, f32[32,128]{1,0:T(8,128)S(1)}, u32[]{:S(2)}, u32[]{:S(2)}) collective-permute-start(f32[32,128]{1,0:T(8,128)S(1)} %shard_map.99), channel_id=1, source_target_pairs={{0,2},{1,3},{2,0},{3,1},{4,6},{5,7},{6,4},{7,5},{8,10},{9,11},{10,... | collective-permute-start | bytes 49160 | tf_op jit(solution)/shard_map/ppermute | solution.py:35
  33.0 3.0 %collective-permute-start.10 = (f32[32,128]{1,0:T(8,128)S(1)}, f32[32,128]{1,0:T(8,128)S(1)}, u32[]{:S(2)}, u32[]{:S(2)}) collective-permute-start(f32[32,128]{1,0:T(8,128)S(1)} %shard_map.99), channel_id=1, source_target_pairs={{0,1},{1,0},{2,3},{3,2},{4,5},{5,4},{6,7},{7,6},{8,9},{9,8},{10,11... | collective-permute-start | bytes 49160 | tf_op jit(solution)/shard_map/ppermute | solution.py:35
  38.8 2.3 %collective-permute-start.13 = (bf16[72,5120]{1,0:T(8,128)(2,1)S(1)}, bf16[72,5120]{1,0:T(8,128)(2,1)S(1)}, u32[]{:S(2)}, u32[]{:S(2)}) collective-permute-start(bf16[72,5120]{1,0:T(8,128)(2,1)S(1)} %get-tuple-element.16), channel_id=1, source_target_pairs={{0,1},{1,0},{2,3},{3,2},{4,5},{5,4},{6,7},{7,6},{8,9},{9,8},{10,11... | collective-permute-start | bytes 2211848 | tf_op jit(solution)/shard_map/ppermute | solution.py:35
  41.2 8.9 %collective-permute-start.15 = (bf16[24,5120]{1,0:T(8,128)(2,1)S(1)}, bf16[24,5120]{1,0:T(8,128)(2,1)S(1)}, u32[]{:S(2)}, u32[]{:S(2)}) collective-permute-start(bf16[24,5120]{1,0:T(8,128)(2,1)S(1)} %shard_map.101.order_ref), channel_id=1, source_target_pairs={{0,2},{1,3},{2,0},{3,1},{4,6},{5,7},{6,4},{7,5},{8,10},{9,11},{10,... | collective-permute-start | bytes 737288 | tf_op jit(solution)/shard_map/ppermute | solution.py:35
  41.9 18.0 %copy-start.2 = (bf16[8,5120]{1,0:T(8,128)(2,1)S(1)}, bf16[8,5120]{1,0:T(8,128)(2,1)}, u32[]{:S(2)}) copy-start(bf16[8,5120]{1,0:T(8,128)(2,1)} %rows_ref.1) | copy-start | bytes 245764
  42.0 8.1 %collective-permute-start.21 = (f32[1,5120]{1,0:T(1,128)S(1)}, f32[1,5120]{1,0:T(1,128)S(1)}, u32[]{:S(2)}, u32[]{:S(2)}) collective-permute-start(f32[1,5120]{1,0:T(1,128)S(1)} %get-tuple-element.20.own_ref), channel_id=1, source_target_pairs={{0,12},{1,13},{2,14},{3,15},{4,8},{5,9},{6,10},{7,11},{8,4},{9,5},... | collective-permute-start | bytes 61448 | tf_op jit(solution)/shard_map/ppermute | solution.py:35
  44.6 5.6 %collective-permute-start.20 = (f32[1,5120]{1,0:T(1,128)S(1)}, f32[1,5120]{1,0:T(1,128)S(1)}, u32[]{:S(2)}, u32[]{:S(2)}) collective-permute-start(f32[1,5120]{1,0:T(1,128)S(1)} %get-tuple-element.20.own_ref), channel_id=1, source_target_pairs={{0,8},{1,9},{2,10},{3,11},{4,12},{5,13},{6,14},{7,15},{8,0},{9,1},... | collective-permute-start | bytes 61448 | tf_op jit(solution)/shard_map/ppermute | solution.py:35
  44.6 5.6 %collective-permute-start.19 = (f32[1,5120]{1,0:T(1,128)S(1)}, f32[1,5120]{1,0:T(1,128)S(1)}, u32[]{:S(2)}, u32[]{:S(2)}) collective-permute-start(f32[1,5120]{1,0:T(1,128)S(1)} %get-tuple-element.20.own_ref), channel_id=1, source_target_pairs={{0,4},{1,5},{2,6},{3,7},{4,0},{5,1},{6,2},{7,3},{8,12},{9,13},{10,... | collective-permute-start | bytes 61448 | tf_op jit(solution)/shard_map/ppermute | solution.py:35
  46.5 9.8 %collective-permute-start.14 = (bf16[8,5120]{1,0:T(8,128)(2,1)S(1)}, bf16[8,5120]{1,0:T(8,128)(2,1)S(1)}, u32[]{:S(2)}, u32[]{:S(2)}) collective-permute-start(bf16[8,5120]{1,0:T(8,128)(2,1)S(1)} %get-tuple-element.19), channel_id=1, source_target_pairs={{0,2},{1,3},{2,0},{3,1},{4,6},{5,7},{6,4},{7,5},{8,10},{9,11},{10,... | collective-permute-start | bytes 245768 | tf_op jit(solution)/shard_map/ppermute | solution.py:35
  50.2 5.5 %collective-permute-start.22 = (f32[1,5120]{1,0:T(1,128)S(1)}, f32[1,5120]{1,0:T(1,128)S(1)}, u32[]{:S(2)}, u32[]{:S(2)}) collective-permute-start(f32[1,5120]{1,0:T(1,128)S(1)} %shard_map.104), channel_id=1, source_target_pairs={{0,2},{1,3},{2,0},{3,1},{4,6},{5,7},{6,4},{7,5},{8,10},{9,11},{10,... | collective-permute-start | bytes 61448 | tf_op jit(solution)/shard_map/ppermute | solution.py:35
  50.7 7.1 %collective-permute-start.18 = (bf16[8,5120]{1,0:T(8,128)(2,1)S(1)}, bf16[8,5120]{1,0:T(8,128)(2,1)S(1)}, u32[]{:S(2)}, u32[]{:S(2)}) collective-permute-start(bf16[8,5120]{1,0:T(8,128)(2,1)S(1)} %get-tuple-element.22), channel_id=1, source_target_pairs={{0,12},{1,13},{2,14},{3,15},{4,8},{5,9},{6,10},{7,11},{8,4},{9,5},... | collective-permute-start | bytes 245768 | tf_op jit(solution)/shard_map/ppermute | solution.py:35
  53.2 6.8 %collective-permute-start.17 = (bf16[8,5120]{1,0:T(8,128)(2,1)S(1)}, bf16[8,5120]{1,0:T(8,128)(2,1)S(1)}, u32[]{:S(2)}, u32[]{:S(2)}) collective-permute-start(bf16[8,5120]{1,0:T(8,128)(2,1)S(1)} %get-tuple-element.23), channel_id=1, source_target_pairs={{0,8},{1,9},{2,10},{3,11},{4,12},{5,13},{6,14},{7,15},{8,0},{9,1},... | collective-permute-start | bytes 245768 | tf_op jit(solution)/shard_map/ppermute | solution.py:35
  53.2 6.8 %collective-permute-start.16 = (bf16[8,5120]{1,0:T(8,128)(2,1)S(1)}, bf16[8,5120]{1,0:T(8,128)(2,1)S(1)}, u32[]{:S(2)}, u32[]{:S(2)}) collective-permute-start(bf16[8,5120]{1,0:T(8,128)(2,1)S(1)} %get-tuple-element.24), channel_id=1, source_target_pairs={{0,4},{1,5},{2,6},{3,7},{4,0},{5,1},{6,2},{7,3},{8,12},{9,13},{10,... | collective-permute-start | bytes 245768 | tf_op jit(solution)/shard_map/ppermute | solution.py:35
  (3 other events, 17.1 us)

commit v6 on v5

--- a/solution.py
+++ b/solution.py
@@ -223,6 +223,8 @@
 def slab_kernel(
     codes,
     place,
+    going_order,
+    rest_order,
     divisor_ref,
     tiles_ref,
     rows_ref,
@@ -233,7 +235,8 @@
     scalars_ref,
     parts_ref,
     kept_ref,
-    sent_ref,
+    going_ref,
+    rest_ref,
     turned,
     coefs,
 ):
@@ -285,32 +288,36 @@
         coefs[:, cut:], head2_ref[...], preferred_element_type=f32
     )
     kept_ref[...] = out[:half]
-    sent_ref[:half, :] = out[half:].astype(bf16)
+    sent = [out[k : k + own_count] for k in range(half, token_count, own_count)]
+    going_ref[...] = cat(*[sent[k] for k in going_order]).astype(bf16)
     gain_grad = (
         jnp.sum(out * rows_ref[:, :width].astype(f32), axis=0, keepdims=True) / gain_ref[...]
     )
 
     parts = two_parts(fold(gain_grad)).astype(bf16)
     parts_ref[...] = parts
-    sent_ref[half:, : parts.shape[1]] = parts
-    sent_ref[half:, parts.shape[1] :] = jnp.zeros((8, width - parts.shape[1]), bf16)
-
-
-def pair_kernel(order, own_count, kept_ref, twin_ref, *outs):
+    padded = jnp.concatenate(
+        [parts.astype(f32), jnp.zeros((8, width - parts.shape[1]), f32)], 1
+    )
+    rest_ref[...] = cat(*[sent[k] for k in rest_order], padded).astype(bf16)
+
+
+def pair_kernel(order, at, own_count, kept_ref, twin_ref, *outs):
+    twin = twin_ref[...].astype(f32)
     for o, out in zip(order, outs):
         blocks = []
         for k in o:
-            even = k // 2 * 2 * own_count
-            band = slice(even, even + 2 * own_count)
-            total = kept_ref[band, :] + twin_ref[band, :].astype(f32)
-            blocks.append(total[k % 2 * own_count : (k % 2 + 1) * own_count])
+            t = at.index(k) * own_count
+            blocks.append(
+                kept_ref[k * own_count : (k + 1) * own_count, :] + twin[t : t + own_count]
+            )
         out[...] = cat(*blocks).astype(out.dtype)
 
 
-def rest_kernel(order, own_count, order_ref, kept_ref, twin_ref, parts_ref, gain_out, *outs):
-    pair_kernel(order, own_count, kept_ref, twin_ref, *outs)
+def rest_kernel(order, at, own_count, order_ref, kept_ref, twin_ref, parts_ref, gain_out, *outs):
+    pair_kernel(order, at, own_count, kept_ref, twin_ref, *outs)
     parts = parts_ref[...].astype(f32)
-    twin_parts = twin_ref[twin_ref.shape[0] - 8 :, : parts.shape[1]].astype(f32)
+    twin_parts = twin_ref[...].astype(f32)[twin_ref.shape[0] - 8 :, : parts.shape[1]]
     gain_sum = one_value(parts) + one_value(twin_parts)
     c = gain_out.shape[1] // 8
     for k in range(8):
@@ -321,8 +328,8 @@
     out_ref[...] = (own_ref[...] + near_ref[...]) + (mid_ref[...] + far_ref[...])
 
 
-def hidden_kernel(rows_ref, gain_ref, kept_ref, *refs):
-    more, out_ref = refs[:-1], refs[-1]
+def hidden_kernel(rows_ref, gain_ref, kept_ref, sum_ref, came_ref, *refs):
+    more, (out_ref, gain_out) = refs[:-2], refs[-2:]
     rows = rows_ref[...].astype(f32)
     own_count, width = rows.shape
     inv_rms = lax.rsqrt(jnp.mean(rows * rows, axis=1, keepdims=True) + epsilon)
@@ -333,6 +340,7 @@
     grad = grad * gain_ref[...]
     inner_dot = jnp.sum(grad * units, axis=1, keepdims=True)
     out_ref[...] = (inv_rms * (grad - units * inner_dot / width)).astype(bf16)
+    gain_out[...] = sum_ref[...] + came_ref[...]
 
 
 def on_device(
@@ -389,14 +397,27 @@
         moved=head_bytes,
     )(softness_divisor, rows, output_vocab_matrix, left)
     tiles, right = links.gather_small(stats, lambda order: turn(order, 1))
+    b = own_count
+    if count == 16:
+        going_order = (6, 7, 4)
+        rest_order = ((0, 3, 2, 5), (1,))
+        sizes = [(4, f32), (1, bf16)]
+    else:
+        quarter = count // 4
+        going_order = tuple(range(quarter, 2 * quarter))
+        rest_order = (tuple(range(quarter)),)
+        sizes = [(quarter, f32)]
+    rest_at = tuple(sorted(sum(rest_order, ())))
+
     parts_shape = (8, width // 4)
-    scalars, parts, kept, sent = call(
-        functools.partial(slab_kernel, codes, links.small_place),
+    scalars, parts, kept, sent_going, sent_rest = call(
+        functools.partial(slab_kernel, codes, links.small_place, going_order, rest_at),
         (
             shaped((8, LANES), f32),
             shaped(parts_shape, bf16),
             shaped((half, width), f32),
-            shaped((half + 8, width), bf16),
+            shaped((len(going_order) * b, width), bf16),
+            shaped((len(rest_at) * b + 8, width), bf16),
         ),
         [SMEM] + [VMEM] * 6,
         [
@@ -407,29 +428,19 @@
         moved=head_bytes,
         limit=28,
     )(softness_divisor, tiles, rows, scaled, left, right, gain)
-    twin = swap(sent, 1)
-
-    b = own_count
-    if count == 16:
-        going_order = (6, 7, 4)
-        rest_order = ((0, 3, 2, 5), (1,))
-        sizes = [(4, f32), (1, bf16)]
-    else:
-        quarter = count // 4
-        going_order = tuple(range(quarter, 2 * quarter))
-        rest_order = (tuple(range(quarter)),)
-        sizes = [(quarter, f32)]
+    twin_going, twin_rest = swap(sent_going, 1), swap(sent_rest, 1)
+
     going = call(
-        functools.partial(pair_kernel, (going_order,), b),
+        functools.partial(pair_kernel, (going_order,), going_order, b),
         shaped((len(going_order) * b, width), bf16),
         [VMEM] * 2,
-    )(kept, twin)
+    )(kept, twin_going)
     gain_grad, kept, *rest = call(
-        functools.partial(rest_kernel, rest_order, b),
+        functools.partial(rest_kernel, rest_order, rest_at, b),
         (shaped((1, width), f32),) + tuple(shaped((k * b, width), t) for k, t in sizes),
         [spec(pl.ANY)] + [VMEM] * 3,
         flops=REST_FLOPS,
-    )(going, kept, twin, parts)
+    )(going, kept, twin_rest, parts)
     if count == 16:
         crossed = swap(going, 2)
         beside = swap(rest[0], 2)
@@ -437,23 +448,27 @@
         gain_grad = call(
             sum_kernel, shaped((1, width), f32), [spec(pl.ANY)] + [VMEM] * 4, limit=8
         )(crossed, gain_grad, gain_near, gain_mid, gain_far)
-        gain_grad = gain_grad + swap(gain_grad, 2)
+        gain_came = swap(gain_grad, 2)
         column = (kept[b:] + crossed.astype(f32)).astype(bf16)
         more = [beside] + [
             swap(column[k * b : (k + 1) * b], m) for k, m in ((0, 4), (1, 8), (2, 12))
         ]
     else:
-        for m in bits_of(count)[1:]:
+        for m in bits_of(count)[1:-1]:
             gain_grad = gain_grad + swap(gain_grad, m)
+        gain_came = swap(gain_grad, count // 2)
         for m in bits_of(count)[1:-1]:
             kept = kept + swap(going, m).astype(f32)
             cut = kept.shape[0] // 2
             kept, going = kept[:cut], kept[cut:].astype(bf16)
         more = [swap(going, count // 2)]
-    grad_hidden = call(
-        hidden_kernel, shaped((b, width), bf16), [VMEM] * (3 + len(more)), limit=8
-    )(backbone_feature_matrix, gain, kept, *more)
-    return (grad_hidden, gain_grad[0], scalars[0, 1:2], scalars[0, 0:1])
+    grad_hidden, grad_gain = call(
+        hidden_kernel,
+        (shaped((b, width), bf16), shaped((1, width), f32)),
+        [VMEM] * (5 + len(more)),
+        limit=8,
+    )(backbone_feature_matrix, gain, kept, gain_grad, gain_came, *more)
+    return (grad_hidden, grad_gain[0], scalars[0, 1:2], scalars[0, 0:1])
 
 
 def solution(mesh):

time: 61 us -> 60.3 us (0.989)
  waiting for transfers between devices: 15.8 us -> 14.9 us
  starting transfers between devices: 29.5 us -> 30.3 us
  other arithmetic: 0.77 us -> 0.14 us
    ppermute x23 -> x24, waiting for transfers between devices: 15.8 us -> 14.9 us  [swap(): return lax.ppermute(value, 'vocab', [(i, i ^ m) for i in range(self.count)])]
    ppermute x23 -> x24, starting transfers between devices: 29.5 us -> 30.3 us  [swap(): return lax.ppermute(value, 'vocab', [(i, i ^ m) for i in range(self.count)])]
    add x1 -> x0, other arithmetic: 0.63 us -> none  [on_device(): gain_grad = gain_grad + swap(gain_grad, 2)]
  transfers between devices with their start and end apart: 23 -> 24, of which waited for: 10 -> 10; matrix products, arithmetic and copies ran while one was open for 2% -> 1% of each run, Pallas kernels for 8% -> 8%
where the time goes in v6:
time: 60.3 us; the launch traced here: 60.1 us
  starting transfers between devices  30.3 us (50%)
  waiting for transfers between devices  14.9 us (25%)
  Pallas kernels  12.4 us (21%)
  between operations  1.44 us (2%)
  local copies, waits for them, and re-layouts  0.91 us (2%)
    ppermute x24, starting transfers between devices, swap(): return lax.ppermute(value, 'vocab', [(i, i ^ m) for i in range(self.count)])  30.3 us
    ppermute x24, waiting for transfers between devices, swap(): return lax.ppermute(value, 'vocab', [(i, i ^ m) for i in range(self.count)])  14.9 us
    pallas_call x2, Pallas kernels, turn(): call(functools.partial(turn_kernel, part), shaped((slab_width // 2, width...  4.68 us
    pallas_call x1, Pallas kernels, on_device(): call(functools.partial(slab_kernel, codes, links.small_place, going_order...  2.74 us
    pallas_call x1, Pallas kernels, on_device(): call(functools.partial(logits_kernel, codes), (shaped((token_count, slab_...  2.18 us
    pallas_call x1, Pallas kernels, on_device(): call(norm_kernel, shaped((own_count, width + LANES), bf16), [HBM] * 4, [p...  1.72 us
  transfers between devices with their start and end apart: 24, of which 10 were waited for; matrix products, arithmetic and copies ran while one was open for 1% of the time, Pallas kernels for 8%

profile of v6, /device:TPU:0, one launch (start us, length us, event | category | flops | bytes accessed | tf_op | source)
XLA Modules:
  0.0 60.1 jit_solution(15481015479576088957)
XLA Ops:
  0.6 1.7 %shard_map.93.refs_0_ = bf16[8,5248]{1,0:T(8,128)(2,1)} custom-call(s32[8]{0:T(128)} %ids_hbm.1, s32[8]{0:T(128)} %flags_hbm.1, bf16[8,5120]{1,0:T(8,128)(2,1)} %rows_ref.1, f32[1,5120]{1,0:T(1,128)} %bitcast.4), custom_call_target="tpu_custom_call" | custom-call | tf_op jit(solution)/shard_map/pallas_call | solution.py:366
  2.4 3.1 %collective-permute-start.2 = (bf16[8,5248]{1,0:T(8,128)(2,1)}, bf16[8,5248]{1,0:T(8,128)(2,1)S(1)}, u32[]{:S(2)}, u32[]{:S(2)}) collective-permute-start(bf16[8,5248]{1,0:T(8,128)(2,1)} %shard_map.93.refs_0_), channel_id=1, source_target_pairs={{0,4},{1,5},{2,6},{3,7},{4,0},{5,1},{6,2},{7,3},{8,12},{9,13},{10,... | collective-permute-start | bytes 251912 | tf_op jit(solution)/shard_map/ppermute | solution.py:35
  5.4 2.6 %collective-permute-start.1 = (bf16[8,5248]{1,0:T(8,128)(2,1)}, bf16[8,5248]{1,0:T(8,128)(2,1)S(1)}, u32[]{:S(2)}, u32[]{:S(2)}) collective-permute-start(bf16[8,5248]{1,0:T(8,128)(2,1)} %shard_map.93.refs_0_), channel_id=1, source_target_pairs={{0,8},{1,9},{2,10},{3,11},{4,12},{5,13},{6,14},{7,15},{8,0},{9,1},... | collective-permute-start | bytes 251912 | tf_op jit(solution)/shard_map/ppermute | solution.py:35
  8.0 1.5 %collective-permute-start = (bf16[8,5248]{1,0:T(8,128)(2,1)}, bf16[8,5248]{1,0:T(8,128)(2,1)S(1)}, u32[]{:S(2)}, u32[]{:S(2)}) collective-permute-start(bf16[8,5248]{1,0:T(8,128)(2,1)} %shard_map.93.refs_0_), channel_id=1, source_target_pairs={{0,2},{1,3},{2,0},{3,1},{4,6},{5,7},{6,4},{7,5},{8,10},{9,11},{10,... | collective-permute-start | bytes 251912 | tf_op jit(solution)/shard_map/ppermute | solution.py:35
  9.6 2.8 %collective-permute-done.1.refs_1_.refs_2_ = bf16[8,5248]{1,0:T(8,128)(2,1)S(1)} collective-permute-done((bf16[8,5248]{1,0:T(8,128)(2,1)}, bf16[8,5248]{1,0:T(8,128)(2,1)S(1)}, u32[]{:S(2)}, u32[]{:S(2)}) %collective-permute-start.1) | collective-permute-done | bytes 84000 | tf_op jit(solution)/shard_map/ppermute | solution.py:35
  12.4 1.6 %collective-permute-start.5 = (bf16[16,5248]{1,0:T(8,128)(2,1)S(1)}, bf16[16,5248]{1,0:T(8,128)(2,1)S(1)}, u32[]{:S(2)}, u32[]{:S(2)}) collective-permute-start(bf16[16,5248]{1,0:T(8,128)(2,1)S(1)} %shard_map.94.order_ref), channel_id=1, source_target_pairs={{0,2},{1,3},{2,0},{3,1},{4,6},{5,7},{6,4},{7,5},{8,10},{9,11},{10,... | collective-permute-start | bytes 503816 | tf_op jit(solution)/shard_map/ppermute | solution.py:35
  14.3 2.5 %collective-permute-start.3 = (bf16[8,5248]{1,0:T(8,128)(2,1)S(1)}, bf16[8,5248]{1,0:T(8,128)(2,1)S(1)}, u32[]{:S(2)}, u32[]{:S(2)}) collective-permute-start(bf16[8,5248]{1,0:T(8,128)(2,1)S(1)} %collective-permute-done.refs_1_), channel_id=1, source_target_pairs={{0,12},{1,13},{2,14},{3,15},{4,8},{5,9},{6,10},{7,11},{8,4},{9,5},... | collective-permute-start | bytes 251912 | tf_op jit(solution)/shard_map/ppermute | solution.py:35
  17.1 2.3 %shard_map.95.refs_7_.order_ref.head_ref = bf16[640,5120]{1,0:T(8,128)(2,1)S(1)} custom-call(bf16[5120,1280]{1,0:T(8,128)(2,1)S(1)} %copy-done, bf16[16,5248]{1,0:T(8,128)(2,1)S(1)} %shard_map.94.order_ref), custom_call_target="tpu_custom_call" | custom-call | flops 3000000000 | bytes 13107200 | tf_op jit(solution)/shard_map/pallas_call | solution.py:380
  19.4 1.2 %collective-permute-done.3.refs_4_ = bf16[8,5248]{1,0:T(8,128)(2,1)S(1)} collective-permute-done((bf16[8,5248]{1,0:T(8,128)(2,1)S(1)}, bf16[8,5248]{1,0:T(8,128)(2,1)S(1)}, u32[]{:S(2)}, u32[]{:S(2)}) %collective-permute-start.3) | collective-permute-done | bytes 84000 | tf_op jit(solution)/shard_map/ppermute | solution.py:35
  21.5 1.5 %collective-permute-done.6 = bf16[64,5248]{1,0:T(8,128)(2,1)S(1)} collective-permute-done((bf16[64,5248]{1,0:T(8,128)(2,1)S(1)}, bf16[64,5248]{1,0:T(8,128)(2,1)S(1)}, u32[]{:S(2)}, u32[]{:S(2)}) %collective-permute-start.6) | collective-permute-done | bytes 671776 | tf_op jit(solution)/shard_map/ppermute | solution.py:35
  23.0 2.2 %shard_map.97 = (f32[128,1280]{1,0:T(8,128)S(1)}, f32[8,128]{1,0:T(8,128)S(1)}) custom-call(f32[1]{0:T(128)S(6)} %copy.10.divisor_ref, bf16[128,5248]{1,0:T(8,128)(2,1)S(1)} %pad_maximum_fusion.rows_ref, bf16[5120,1280]{1,0:T(8,128)(2,1)S(1)} %copy-done, bf16[640,5120]{1,0:T(8,128)(2,1)S(1)} %shard_map.95.refs_7_.order_ref.head_ref), custom_call_target="tpu_custom_call" | custom-call | flops 1677721600 | bytes 13107200 | tf_op jit(solution)/shard_map/pallas_call | solution.py:391
  25.2 2.5 %collective-permute-start.9 = (f32[8,128]{1,0:T(8,128)S(1)}, f32[8,128]{1,0:T(8,128)S(1)}, u32[]{:S(2)}, u32[]{:S(2)}) collective-permute-start(f32[8,128]{1,0:T(8,128)S(1)} %get-tuple-element.16.order_ref.refs_0_), channel_id=1, source_target_pairs={{0,12},{1,13},{2,14},{3,15},{4,8},{5,9},{6,10},{7,11},{8,4},{9,5},... | collective-permute-start | bytes 12296 | tf_op jit(solution)/shard_map/ppermute | solution.py:35
  27.7 1.9 %collective-permute-start.7 = (f32[8,128]{1,0:T(8,128)S(1)}, f32[8,128]{1,0:T(8,128)S(1)}, u32[]{:S(2)}, u32[]{:S(2)}) collective-permute-start(f32[8,128]{1,0:T(8,128)S(1)} %get-tuple-element.16.order_ref.refs_0_), channel_id=1, source_target_pairs={{0,4},{1,5},{2,6},{3,7},{4,0},{5,1},{6,2},{7,3},{8,12},{9,13},{10,... | collective-permute-start | bytes 12296 | tf_op jit(solution)/shard_map/ppermute | solution.py:35
  29.6 2.3 %shard_map.98.refs_4_.head2_ref = bf16[640,5120]{1,0:T(8,128)(2,1)S(1)} custom-call(bf16[5120,1280]{1,0:T(8,128)(2,1)S(1)} %copy-done, f32[8,128]{1,0:T(8,128)S(1)} %get-tuple-element.16.order_ref.refs_0_), custom_call_target="tpu_custom_call" | custom-call | flops 3000000000 | bytes 13107200 | tf_op jit(solution)/shard_map/pallas_call | solution.py:380
  34.1 1.3 %collective-permute-done.12 = f32[32,128]{1,0:T(8,128)S(1)} collective-permute-done((f32[32,128]{1,0:T(8,128)S(1)}, f32[32,128]{1,0:T(8,128)S(1)}, u32[]{:S(2)}, u32[]{:S(2)}) %collective-permute-start.12) | collective-permute-done | bytes 16416 | tf_op jit(solution)/shard_map/ppermute | solution.py:35
  36.1 2.7 %shard_map.100 = (f32[8,128]{1,0:T(8,128)S(1)}, bf16[8,1280]{1,0:T(8,128)(2,1)S(1)}, f32[64,5120]{1,0:T(8,128)S(1)}, bf16[24,5120]{1,0:T(8,128)(2,1)S(1)}, bf16[48,5120]{1,0:T(8,128)(2,1)S(1)}) custom-call(f32[1]{0:T(128)S(6)} %copy.10.divisor_ref, f32[128,128]{1,0:T(8,128)S(1)} %pad_maximum_fusion.1.tiles_ref, ...), custom_call_target="tpu_custom_call" | custom-call | flops 1677721600 | bytes 13107200 | tf_op jit(solution)/shard_map/pallas_call | solution.py:413
  39.4 1.7 %collective-permute-done.13.twin_ref = bf16[24,5120]{1,0:T(8,128)(2,1)S(1)} collective-permute-done((bf16[24,5120]{1,0:T(8,128)(2,1)S(1)}, bf16[24,5120]{1,0:T(8,128)(2,1)S(1)}, u32[]{:S(2)}, u32[]{:S(2)}) %collective-permute-start.13) | collective-permute-done | bytes 245792 | tf_op jit(solution)/shard_map/ppermute | solution.py:35
  42.0 2.5 %collective-permute-start.18 = (f32[1,5120]{1,0:T(1,128)S(1)}, f32[1,5120]{1,0:T(1,128)S(1)}, u32[]{:S(2)}, u32[]{:S(2)}) collective-permute-start(f32[1,5120]{1,0:T(1,128)S(1)} %get-tuple-element.23.own_ref), channel_id=1, source_target_pairs={{0,12},{1,13},{2,14},{3,15},{4,8},{5,9},{6,10},{7,11},{8,4},{9,5},... | collective-permute-start | bytes 61448 | tf_op jit(solution)/shard_map/ppermute | solution.py:35
  44.6 1.9 %collective-permute-start.16 = (f32[1,5120]{1,0:T(1,128)S(1)}, f32[1,5120]{1,0:T(1,128)S(1)}, u32[]{:S(2)}, u32[]{:S(2)}) collective-permute-start(f32[1,5120]{1,0:T(1,128)S(1)} %get-tuple-element.23.own_ref), channel_id=1, source_target_pairs={{0,4},{1,5},{2,6},{3,7},{4,0},{5,1},{6,2},{7,3},{8,12},{9,13},{10,... | collective-permute-start | bytes 61448 | tf_op jit(solution)/shard_map/ppermute | solution.py:35
  46.5 2.7 %collective-permute-done.15.order_ref = bf16[24,5120]{1,0:T(8,128)(2,1)S(1)} collective-permute-done((bf16[24,5120]{1,0:T(8,128)(2,1)S(1)}, bf16[24,5120]{1,0:T(8,128)(2,1)S(1)}, u32[]{:S(2)}, u32[]{:S(2)}) %collective-permute-start.15) | collective-permute-done | bytes 245792 | tf_op jit(solution)/shard_map/ppermute | solution.py:35
  49.3 2.4 %collective-permute-start.23 = (bf16[8,5120]{1,0:T(8,128)(2,1)S(1)}, bf16[8,5120]{1,0:T(8,128)(2,1)S(1)}, u32[]{:S(2)}, u32[]{:S(2)}) collective-permute-start(bf16[8,5120]{1,0:T(8,128)(2,1)S(1)} %get-tuple-element.28), channel_id=1, source_target_pairs={{0,12},{1,13},{2,14},{3,15},{4,8},{5,9},{6,10},{7,11},{8,4},{9,5},... | collective-permute-start | bytes 245768 | tf_op jit(solution)/shard_map/ppermute | solution.py:35
  51.8 2.0 %collective-permute-start.21 = (bf16[8,5120]{1,0:T(8,128)(2,1)S(1)}, bf16[8,5120]{1,0:T(8,128)(2,1)S(1)}, u32[]{:S(2)}, u32[]{:S(2)}) collective-permute-start(bf16[8,5120]{1,0:T(8,128)(2,1)S(1)} %get-tuple-element.30), channel_id=1, source_target_pairs={{0,4},{1,5},{2,6},{3,7},{4,0},{5,1},{6,2},{7,3},{8,12},{9,13},{10,... | collective-permute-start | bytes 245768 | tf_op jit(solution)/shard_map/ppermute | solution.py:35
  54.5 1.3 %collective-permute-start.19 = (f32[1,5120]{1,0:T(1,128)S(1)}, f32[1,5120]{1,0:T(1,128)S(1)}, u32[]{:S(2)}, u32[]{:S(2)}) collective-permute-start(f32[1,5120]{1,0:T(1,128)S(1)} %shard_map.103.sum_ref), channel_id=1, source_target_pairs={{0,2},{1,3},{2,0},{3,1},{4,6},{5,7},{6,4},{7,5},{8,10},{9,11},{10,... | collective-permute-start | bytes 61448 | tf_op jit(solution)/shard_map/ppermute | solution.py:35
  56.4 2.0 %collective-permute-done.19.came_ref = f32[1,5120]{1,0:T(1,128)S(1)} collective-permute-done((f32[1,5120]{1,0:T(1,128)S(1)}, f32[1,5120]{1,0:T(1,128)S(1)}, u32[]{:S(2)}, u32[]{:S(2)}) %collective-permute-start.19) | collective-permute-done | bytes 20512 | tf_op jit(solution)/shard_map/ppermute | solution.py:35
  (49 shorter events, 8.3 us)
Async XLA Ops:
  2.4 7.2 %collective-permute-start.2 = (bf16[8,5248]{1,0:T(8,128)(2,1)}, bf16[8,5248]{1,0:T(8,128)(2,1)S(1)}, u32[]{:S(2)}, u32[]{:S(2)}) collective-permute-start(bf16[8,5248]{1,0:T(8,128)(2,1)} %shard_map.93.refs_0_), channel_id=1, source_target_pairs={{0,4},{1,5},{2,6},{3,7},{4,0},{5,1},{6,2},{7,3},{8,12},{9,13},{10,... | collective-permute-start | bytes 251912 | tf_op jit(solution)/shard_map/ppermute | solution.py:35
  5.4 6.9 %collective-permute-start.1 = (bf16[8,5248]{1,0:T(8,128)(2,1)}, bf16[8,5248]{1,0:T(8,128)(2,1)S(1)}, u32[]{:S(2)}, u32[]{:S(2)}) collective-permute-start(bf16[8,5248]{1,0:T(8,128)(2,1)} %shard_map.93.refs_0_), channel_id=1, source_target_pairs={{0,8},{1,9},{2,10},{3,11},{4,12},{5,13},{6,14},{7,15},{8,0},{9,1},... | collective-permute-start | bytes 251912 | tf_op jit(solution)/shard_map/ppermute | solution.py:35
  8.0 6.3 %collective-permute-start = (bf16[8,5248]{1,0:T(8,128)(2,1)}, bf16[8,5248]{1,0:T(8,128)(2,1)S(1)}, u32[]{:S(2)}, u32[]{:S(2)}) collective-permute-start(bf16[8,5248]{1,0:T(8,128)(2,1)} %shard_map.93.refs_0_), channel_id=1, source_target_pairs={{0,2},{1,3},{2,0},{3,1},{4,6},{5,7},{6,4},{7,5},{8,10},{9,11},{10,... | collective-permute-start | bytes 251912 | tf_op jit(solution)/shard_map/ppermute | solution.py:35
  12.4 8.3 %collective-permute-start.5 = (bf16[16,5248]{1,0:T(8,128)(2,1)S(1)}, bf16[16,5248]{1,0:T(8,128)(2,1)S(1)}, u32[]{:S(2)}, u32[]{:S(2)}) collective-permute-start(bf16[16,5248]{1,0:T(8,128)(2,1)S(1)} %shard_map.94.order_ref), channel_id=1, source_target_pairs={{0,2},{1,3},{2,0},{3,1},{4,6},{5,7},{6,4},{7,5},{8,10},{9,11},{10,... | collective-permute-start | bytes 503816 | tf_op jit(solution)/shard_map/ppermute | solution.py:35
  14.0 5.5 %collective-permute-start.4 = (bf16[8,5248]{1,0:T(8,128)(2,1)S(1)}, bf16[8,5248]{1,0:T(8,128)(2,1)S(1)}, u32[]{:S(2)}, u32[]{:S(2)}) collective-permute-start(bf16[8,5248]{1,0:T(8,128)(2,1)S(1)} %collective-permute-done.1.refs_1_.refs_2_), channel_id=1, source_target_pairs={{0,4},{1,5},{2,6},{3,7},{4,0},{5,1},{6,2},{7,3},{8,12},{9,13},{10,... | collective-permute-start | bytes 251912 | tf_op jit(solution)/shard_map/ppermute | solution.py:35
  14.3 6.4 %collective-permute-start.3 = (bf16[8,5248]{1,0:T(8,128)(2,1)S(1)}, bf16[8,5248]{1,0:T(8,128)(2,1)S(1)}, u32[]{:S(2)}, u32[]{:S(2)}) collective-permute-start(bf16[8,5248]{1,0:T(8,128)(2,1)S(1)} %collective-permute-done.refs_1_), channel_id=1, source_target_pairs={{0,12},{1,13},{2,14},{3,15},{4,8},{5,9},{6,10},{7,11},{8,4},{9,5},... | collective-permute-start | bytes 251912 | tf_op jit(solution)/shard_map/ppermute | solution.py:35
  20.7 2.2 %collective-permute-start.6 = (bf16[64,5248]{1,0:T(8,128)(2,1)S(1)}, bf16[64,5248]{1,0:T(8,128)(2,1)S(1)}, u32[]{:S(2)}, u32[]{:S(2)}) collective-permute-start(bf16[64,5248]{1,0:T(8,128)(2,1)S(1)} %shard_map.96), channel_id=1, source_target_pairs={{0,1},{1,0},{2,3},{3,2},{4,5},{5,4},{6,7},{7,6},{8,9},{9,8},{10,11... | collective-permute-start | bytes 2015240 | tf_op jit(solution)/shard_map/ppermute | solution.py:35
  25.2 6.8 %collective-permute-start.9 = (f32[8,128]{1,0:T(8,128)S(1)}, f32[8,128]{1,0:T(8,128)S(1)}, u32[]{:S(2)}, u32[]{:S(2)}) collective-permute-start(f32[8,128]{1,0:T(8,128)S(1)} %get-tuple-element.16.order_ref.refs_0_), channel_id=1, source_target_pairs={{0,12},{1,13},{2,14},{3,15},{4,8},{5,9},{6,10},{7,11},{8,4},{9,5},... | collective-permute-start | bytes 12296 | tf_op jit(solution)/shard_map/ppermute | solution.py:35
  27.7 4.5 %collective-permute-start.8 = (f32[8,128]{1,0:T(8,128)S(1)}, f32[8,128]{1,0:T(8,128)S(1)}, u32[]{:S(2)}, u32[]{:S(2)}) collective-permute-start(f32[8,128]{1,0:T(8,128)S(1)} %get-tuple-element.16.order_ref.refs_0_), channel_id=1, source_target_pairs={{0,8},{1,9},{2,10},{3,11},{4,12},{5,13},{6,14},{7,15},{8,0},{9,1},... | collective-permute-start | bytes 12296 | tf_op jit(solution)/shard_map/ppermute | solution.py:35
  27.7 4.5 %collective-permute-start.7 = (f32[8,128]{1,0:T(8,128)S(1)}, f32[8,128]{1,0:T(8,128)S(1)}, u32[]{:S(2)}, u32[]{:S(2)}) collective-permute-start(f32[8,128]{1,0:T(8,128)S(1)} %get-tuple-element.16.order_ref.refs_0_), channel_id=1, source_target_pairs={{0,4},{1,5},{2,6},{3,7},{4,0},{5,1},{6,2},{7,3},{8,12},{9,13},{10,... | collective-permute-start | bytes 12296 | tf_op jit(solution)/shard_map/ppermute | solution.py:35
  32.2 3.2 %collective-permute-start.12 = (f32[32,128]{1,0:T(8,128)S(1)}, f32[32,128]{1,0:T(8,128)S(1)}, u32[]{:S(2)}, u32[]{:S(2)}) collective-permute-start(f32[32,128]{1,0:T(8,128)S(1)} %shard_map.99), channel_id=1, source_target_pairs={{0,3},{1,2},{2,1},{3,0},{4,7},{5,6},{6,5},{7,4},{8,11},{9,10},{10,... | collective-permute-start | bytes 49160 | tf_op jit(solution)/shard_map/ppermute | solution.py:35
  32.3 3.8 %collective-permute-start.11 = (f32[32,128]{1,0:T(8,128)S(1)}, f32[32,128]{1,0:T(8,128)S(1)}, u32[]{:S(2)}, u32[]{:S(2)}) collective-permute-start(f32[32,128]{1,0:T(8,128)S(1)} %shard_map.99), channel_id=1, source_target_pairs={{0,2},{1,3},{2,0},{3,1},{4,6},{5,7},{6,4},{7,5},{8,10},{9,11},{10,... | collective-permute-start | bytes 49160 | tf_op jit(solution)/shard_map/ppermute | solution.py:35
  33.0 3.0 %collective-permute-start.10 = (f32[32,128]{1,0:T(8,128)S(1)}, f32[32,128]{1,0:T(8,128)S(1)}, u32[]{:S(2)}, u32[]{:S(2)}) collective-permute-start(f32[32,128]{1,0:T(8,128)S(1)} %shard_map.99), channel_id=1, source_target_pairs={{0,1},{1,0},{2,3},{3,2},{4,5},{5,4},{6,7},{7,6},{8,9},{9,8},{10,11... | collective-permute-start | bytes 49160 | tf_op jit(solution)/shard_map/ppermute | solution.py:35
  38.8 3.1 %collective-permute-start.14 = (bf16[48,5120]{1,0:T(8,128)(2,1)S(1)}, bf16[48,5120]{1,0:T(8,128)(2,1)S(1)}, u32[]{:S(2)}, u32[]{:S(2)}) collective-permute-start(bf16[48,5120]{1,0:T(8,128)(2,1)S(1)} %get-tuple-element.20), channel_id=1, source_target_pairs={{0,1},{1,0},{2,3},{3,2},{4,5},{5,4},{6,7},{7,6},{8,9},{9,8},{10,11... | collective-permute-start | bytes 1474568 | tf_op jit(solution)/shard_map/ppermute | solution.py:35
  38.9 2.2 %collective-permute-start.13 = (bf16[24,5120]{1,0:T(8,128)(2,1)S(1)}, bf16[24,5120]{1,0:T(8,128)(2,1)S(1)}, u32[]{:S(2)}, u32[]{:S(2)}) collective-permute-start(bf16[24,5120]{1,0:T(8,128)(2,1)S(1)} %get-tuple-element.19), channel_id=1, source_target_pairs={{0,1},{1,0},{2,3},{3,2},{4,5},{5,4},{6,7},{7,6},{8,9},{9,8},{10,11... | collective-permute-start | bytes 737288 | tf_op jit(solution)/shard_map/ppermute | solution.py:35
  41.2 8.1 %collective-permute-start.15 = (bf16[24,5120]{1,0:T(8,128)(2,1)S(1)}, bf16[24,5120]{1,0:T(8,128)(2,1)S(1)}, u32[]{:S(2)}, u32[]{:S(2)}) collective-permute-start(bf16[24,5120]{1,0:T(8,128)(2,1)S(1)} %shard_map.101.order_ref), channel_id=1, source_target_pairs={{0,2},{1,3},{2,0},{3,1},{4,6},{5,7},{6,4},{7,5},{8,10},{9,11},{10,... | collective-permute-start | bytes 737288 | tf_op jit(solution)/shard_map/ppermute | solution.py:35
  42.0 9.8 %collective-permute-start.18 = (f32[1,5120]{1,0:T(1,128)S(1)}, f32[1,5120]{1,0:T(1,128)S(1)}, u32[]{:S(2)}, u32[]{:S(2)}) collective-permute-start(f32[1,5120]{1,0:T(1,128)S(1)} %get-tuple-element.23.own_ref), channel_id=1, source_target_pairs={{0,12},{1,13},{2,14},{3,15},{4,8},{5,9},{6,10},{7,11},{8,4},{9,5},... | collective-permute-start | bytes 61448 | tf_op jit(solution)/shard_map/ppermute | solution.py:35
  44.6 9.2 %collective-permute-start.17 = (f32[1,5120]{1,0:T(1,128)S(1)}, f32[1,5120]{1,0:T(1,128)S(1)}, u32[]{:S(2)}, u32[]{:S(2)}) collective-permute-start(f32[1,5120]{1,0:T(1,128)S(1)} %get-tuple-element.23.own_ref), channel_id=1, source_target_pairs={{0,8},{1,9},{2,10},{3,11},{4,12},{5,13},{6,14},{7,15},{8,0},{9,1},... | collective-permute-start | bytes 61448 | tf_op jit(solution)/shard_map/ppermute | solution.py:35
  44.6 10.0 %collective-permute-start.16 = (f32[1,5120]{1,0:T(1,128)S(1)}, f32[1,5120]{1,0:T(1,128)S(1)}, u32[]{:S(2)}, u32[]{:S(2)}) collective-permute-start(f32[1,5120]{1,0:T(1,128)S(1)} %get-tuple-element.23.own_ref), channel_id=1, source_target_pairs={{0,4},{1,5},{2,6},{3,7},{4,0},{5,1},{6,2},{7,3},{8,12},{9,13},{10,... | collective-permute-start | bytes 61448 | tf_op jit(solution)/shard_map/ppermute | solution.py:35
  49.3 9.1 %collective-permute-start.23 = (bf16[8,5120]{1,0:T(8,128)(2,1)S(1)}, bf16[8,5120]{1,0:T(8,128)(2,1)S(1)}, u32[]{:S(2)}, u32[]{:S(2)}) collective-permute-start(bf16[8,5120]{1,0:T(8,128)(2,1)S(1)} %get-tuple-element.28), channel_id=1, source_target_pairs={{0,12},{1,13},{2,14},{3,15},{4,8},{5,9},{6,10},{7,11},{8,4},{9,5},... | collective-permute-start | bytes 245768 | tf_op jit(solution)/shard_map/ppermute | solution.py:35
  51.7 7.5 %collective-permute-start.22 = (bf16[8,5120]{1,0:T(8,128)(2,1)S(1)}, bf16[8,5120]{1,0:T(8,128)(2,1)S(1)}, u32[]{:S(2)}, u32[]{:S(2)}) collective-permute-start(bf16[8,5120]{1,0:T(8,128)(2,1)S(1)} %get-tuple-element.29), channel_id=1, source_target_pairs={{0,8},{1,9},{2,10},{3,11},{4,12},{5,13},{6,14},{7,15},{8,0},{9,1},... | collective-permute-start | bytes 245768 | tf_op jit(solution)/shard_map/ppermute | solution.py:35
  51.8 7.4 %collective-permute-start.21 = (bf16[8,5120]{1,0:T(8,128)(2,1)S(1)}, bf16[8,5120]{1,0:T(8,128)(2,1)S(1)}, u32[]{:S(2)}, u32[]{:S(2)}) collective-permute-start(bf16[8,5120]{1,0:T(8,128)(2,1)S(1)} %get-tuple-element.30), channel_id=1, source_target_pairs={{0,4},{1,5},{2,6},{3,7},{4,0},{5,1},{6,2},{7,3},{8,12},{9,13},{10,... | collective-permute-start | bytes 245768 | tf_op jit(solution)/shard_map/ppermute | solution.py:35
  53.7 5.5 %collective-permute-start.20 = (bf16[8,5120]{1,0:T(8,128)(2,1)S(1)}, bf16[8,5120]{1,0:T(8,128)(2,1)S(1)}, u32[]{:S(2)}, u32[]{:S(2)}) collective-permute-start(bf16[8,5120]{1,0:T(8,128)(2,1)S(1)} %get-tuple-element.24), channel_id=1, source_target_pairs={{0,2},{1,3},{2,0},{3,1},{4,6},{5,7},{6,4},{7,5},{8,10},{9,11},{10,... | collective-permute-start | bytes 245768 | tf_op jit(solution)/shard_map/ppermute | solution.py:35
  54.5 3.9 %collective-permute-start.19 = (f32[1,5120]{1,0:T(1,128)S(1)}, f32[1,5120]{1,0:T(1,128)S(1)}, u32[]{:S(2)}, u32[]{:S(2)}) collective-permute-start(f32[1,5120]{1,0:T(1,128)S(1)} %shard_map.103.sum_ref), channel_id=1, source_target_pairs={{0,2},{1,3},{2,0},{3,1},{4,6},{5,7},{6,4},{7,5},{8,10},{9,11},{10,... | collective-permute-start | bytes 61448 | tf_op jit(solution)/shard_map/ppermute | solution.py:35
  (4 other events, 34.4 us)
